TPU v7x, 32 devices: a whole 2x2x4 slice. The times are simulated.
32 devices in a mesh: bucket: 8 (over y, x, core), seq: 4 (over z).
Axes of the slice: x: 2, y: 2, z: 4, core: 2. Of those that a mesh axis runs over, the one named last changes fastest.
Arguments:
- tokens: bfloat16 [4096, 1536], P(('bucket', 'seq')), may hold values from -6 to 6
- captions: bfloat16 [2048, 4096], P(('bucket', 'seq')), may hold values from -6 to 6
- cotangent: bfloat16 [4096, 1536], P(('bucket', 'seq')), may hold values from -6 to 6
- counts: int32 [8], replicated, may hold values from 128 to 512, as said below
- cap_lens: int32 [8], replicated, may hold values from 8 to 256, as said below
- steps_t: int32 [8], replicated, may hold values from 0 to 999
- w_query: bfloat16 [1536, 1536], P(('bucket', 'seq')), may hold values from -0.15625 to 0.15625
- w_key: bfloat16 [1536, 1536], P(('bucket', 'seq')), may hold values from -0.15625 to 0.15625
- w_value: bfloat16 [1536, 1536], P(('bucket', 'seq')), may hold values from -0.15625 to 0.15625
- w_out: bfloat16 [1536, 1536], P(('bucket', 'seq')), may hold values from -0.15625 to 0.15625
- w_cap_key: bfloat16 [4096, 1536], P(('bucket', 'seq')), may hold values from -0.09375 to 0.09375
- w_cap_value: bfloat16 [4096, 1536], P(('bucket', 'seq')), may hold values from -0.09375 to 0.09375
- w_gate: bfloat16 [1536, 4096], P(('bucket', 'seq')), may hold values from -0.15625 to 0.15625
- w_up: bfloat16 [1536, 4096], P(('bucket', 'seq')), may hold values from -0.15625 to 0.15625
- w_down: bfloat16 [4096, 1536], P(('bucket', 'seq')), may hold values from -0.09375 to 0.09375
- w_mod: bfloat16 [1024, 6144], P(('bucket', 'seq')), may hold values from -0.1875 to 0.1875
- gains: bfloat16 [7, 1536], P(None, ('bucket', 'seq')), may hold values from 0.099609375 to 1.8984375
- cross_gate: bfloat16 [1536], P(('bucket', 'seq')), may hold values from -1.5 to 1.5
Outputs:
- block_out: bfloat16 [4096, 1536], P(('bucket', 'seq'))
- tokens_grad: float32 [4096, 1536], P(('bucket', 'seq'))
- w_query_grad: float32 [1536, 1536], P('bucket', 'seq')
- w_key_grad: float32 [1536, 1536], P('bucket', 'seq')
- w_value_grad: float32 [1536, 1536], P('bucket', 'seq')
- w_out_grad: float32 [1536, 1536], P('bucket', 'seq')
- w_cap_key_grad: float32 [4096, 1536], P('bucket', 'seq')
- w_cap_value_grad: float32 [4096, 1536], P('bucket', 'seq')
- w_gate_grad: float32 [1536, 4096], P('bucket', 'seq')
- w_up_grad: float32 [1536, 4096], P('bucket', 'seq')
- w_down_grad: float32 [4096, 1536], P('bucket', 'seq')
- w_mod_grad: float32 [1024, 6144], P('bucket', 'seq')
- gains_grad: float32 [7, 1536], P(None, ('bucket', 'seq'))
- cross_gate_grad: float32 [1536], P(('bucket', 'seq'))
Inputs may be any that keep to these rules, and one draw needn't show every extreme that they name: `counts`: each bucket has 128, 288 or 512 live rows, at its start; some bucket has 512. `cap_lens`: live caption tokens lie at the start of a bucket's slots; some bucket has 256.
All inputs are finite; a program needn't handle non-finite values.
Results may differ from a plain program's by a relative error of at most 0.029.
Values may be sent and summed in bfloat16 or wider, within the bound.
A program may use at most 256 MiB of HBM per device.

v0:
```python
import math

import jax
import jax.numpy as jnp
from jax import lax
from jax.sharding import PartitionSpec as P

HEAD_DIM = 64


def rms_rows(values):
    return values * lax.rsqrt(jnp.mean(values * values, axis=-1, keepdims=True) + 1e-05)


def head_rms(values):
    shaped = values.reshape(values.shape[:-1] + (values.shape[-1] // HEAD_DIM, HEAD_DIM))
    shaped = shaped * lax.rsqrt(jnp.mean(shaped * shaped, axis=-1, keepdims=True) + 1e-06)
    return shaped.reshape(values.shape)


def time_embed(step_value, width):
    half_width = width // 2
    freqs = jnp.exp(-math.log(10000.0) * jnp.arange(half_width, dtype=jnp.float32) / half_width)
    angles = step_value.astype(jnp.float32) * freqs
    return jnp.concatenate([jnp.cos(angles), jnp.sin(angles)])


def pick_entry(table, index):
    return jnp.sum(jnp.where(jnp.arange(table.shape[0]) == index, table, 0))


def bf_dot(left, right):
    return jnp.dot(left, right, preferred_element_type=jnp.float32)


def pre_attn(tokens_in, gain_pre, scale_attn):
    return rms_rows(tokens_in) * gain_pre * (1.0 + scale_attn)


def qk_norm(query_in, key_in, gain_query, gain_key):
    return (head_rms(query_in) * gain_query, head_rms(key_in) * gain_key)


def cap_norm(key_in, gain_cap):
    return head_rms(key_in) * gain_cap


def middle(tokens_in, attn_out, gain_post, gate_attn, gain_ffn, scale_ffn):
    resid_one = tokens_in + jnp.tanh(gate_attn) * rms_rows(attn_out) * gain_post
    return (resid_one, rms_rows(resid_one) * gain_ffn * (1.0 + scale_ffn))


def activate(gate_proj, up_proj):
    return jax.nn.silu(gate_proj) * up_proj


def finish(resid_one, ffn_out, gain_last, gate_ffn):
    return resid_one + jnp.tanh(gate_ffn) * rms_rows(ffn_out) * gain_last


def left_dot(rows_left, rows_right):
    return lax.dot_general(
        rows_left, rows_right, (((0,), (0,)), ((), ())), preferred_element_type=jnp.float32
    )


def on_device(
    tokens,
    captions,
    cotangent,
    counts,
    cap_lens,
    steps_t,
    w_query,
    w_key,
    w_value,
    w_out,
    w_cap_key,
    w_cap_value,
    w_gate,
    w_up,
    w_down,
    w_mod,
    gains,
    cross_gate,
):
    gathered = (
        lax.all_gather(w_query, ("bucket", "seq"), axis=0, tiled=True),
        lax.all_gather(w_key, ("bucket", "seq"), axis=0, tiled=True),
        lax.all_gather(w_value, ("bucket", "seq"), axis=0, tiled=True),
        lax.all_gather(w_out, ("bucket", "seq"), axis=0, tiled=True),
        lax.all_gather(w_cap_key, ("bucket", "seq"), axis=0, tiled=True),
        lax.all_gather(w_cap_value, ("bucket", "seq"), axis=0, tiled=True),
        lax.all_gather(w_gate, ("bucket", "seq"), axis=0, tiled=True),
        lax.all_gather(w_up, ("bucket", "seq"), axis=0, tiled=True),
        lax.all_gather(w_down, ("bucket", "seq"), axis=0, tiled=True),
        lax.all_gather(w_mod, ("bucket", "seq"), axis=0, tiled=True),
        lax.all_gather(gains, ("bucket", "seq"), axis=1, tiled=True),
        lax.all_gather(cross_gate, ("bucket", "seq"), axis=0, tiled=True),
    )
    (
        full_query,
        full_key,
        full_value,
        full_out,
        full_cap_key,
        full_cap_value,
        full_gate,
        full_up,
        full_down,
        full_mod,
        full_gains,
        full_cross,
    ) = gathered
    width = full_query.shape[0]
    heads = width // HEAD_DIM
    row_count = tokens.shape[0]
    seq_count = lax.axis_size("seq")
    bucket_count = lax.axis_size("bucket")
    span = row_count * seq_count
    head_share = heads // seq_count
    group_id = lax.axis_index("bucket")
    seq_place = lax.axis_index("seq")
    live_rows = pick_entry(counts, group_id)
    cap_len = pick_entry(cap_lens, group_id)
    step_value = pick_entry(steps_t, group_id)
    token_total = jnp.sum(counts).astype(jnp.float32)
    row_ids = seq_place * row_count + jnp.arange(row_count)
    gain_f = full_gains.astype(jnp.float32)
    gate_cross = jnp.tanh(full_cross.astype(jnp.float32))
    scale = HEAD_DIM ** (-0.5)
    cond = jax.nn.silu(time_embed(step_value, full_mod.shape[0])).astype(jnp.bfloat16)
    modulation = bf_dot(cond[None, :], full_mod)[0]
    scale_attn = modulation[0:width]
    gate_attn = modulation[width : 2 * width]
    scale_ffn = modulation[2 * width : 3 * width]
    gate_ffn = modulation[3 * width : 4 * width]
    tokens_f = tokens.astype(jnp.float32)
    hidden_pre, pre_back = jax.vjp(pre_attn, tokens_f, gain_f[0], scale_attn)
    hidden_in = hidden_pre.astype(jnp.bfloat16)
    query_proj = bf_dot(hidden_in, full_query)
    key_proj = bf_dot(hidden_in, full_key)
    value_proj = bf_dot(hidden_in, full_value)
    (query_f, key_f), norm_back = jax.vjp(qk_norm, query_proj, key_proj, gain_f[4], gain_f[5])
    query_norm = query_f.astype(jnp.bfloat16)
    key_norm = key_f.astype(jnp.bfloat16)
    value_low = value_proj.astype(jnp.bfloat16)
    query_three = query_norm.reshape(row_count, heads, HEAD_DIM)
    key_three = key_norm.reshape(row_count, heads, HEAD_DIM)
    value_three = value_low.reshape(row_count, heads, HEAD_DIM)
    cap_key_proj = bf_dot(captions, full_cap_key)
    cap_value_proj = bf_dot(captions, full_cap_value)
    cap_key_f, cap_back = jax.vjp(cap_norm, cap_key_proj, gain_f[6])
    cap_keys, cap_values = (
        lax.all_gather(cap_key_f.astype(jnp.bfloat16), "seq", axis=0, tiled=True),
        lax.all_gather(cap_value_proj.astype(jnp.bfloat16), "seq", axis=0, tiled=True),
    )
    cap_keys3 = cap_keys.reshape(cap_keys.shape[0], heads, HEAD_DIM)
    cap_values3 = cap_values.reshape(cap_values.shape[0], heads, HEAD_DIM)
    cap_live = jnp.arange(cap_keys.shape[0]) < cap_len
    cap_scores = (
        jnp.einsum("qhd,khd->hqk", query_three, cap_keys3, preferred_element_type=jnp.float32)
        * scale
    )
    cap_scores = jnp.where(cap_live[None, None, :], cap_scores, -1e30)
    cap_probs = jax.nn.softmax(cap_scores, axis=-1)
    cross_out = jnp.einsum(
        "hqk,khd->qhd",
        cap_probs.astype(jnp.bfloat16),
        cap_values3,
        preferred_element_type=jnp.float32,
    ).reshape(row_count, width)
    query_block = min(512, span)
    query_four = query_three.reshape(row_count, seq_count, head_share, HEAD_DIM)
    key_four = key_three.reshape(row_count, seq_count, head_share, HEAD_DIM)
    value_four = value_three.reshape(row_count, seq_count, head_share, HEAD_DIM)
    query_all = lax.all_to_all(query_four, "seq", split_axis=1, concat_axis=0, tiled=True)
    key_all = lax.all_to_all(key_four, "seq", split_axis=1, concat_axis=0, tiled=True)
    value_all = lax.all_to_all(value_four, "seq", split_axis=1, concat_axis=0, tiled=True)
    head_part = query_all.shape[2]
    query_flat = query_all[:, 0]
    key_flat = key_all[:, 0]
    value_flat = value_all[:, 0]
    head_key_ok = jnp.arange(span) < live_rows

    def one_query(query_part):
        scores = (
            jnp.einsum("qhd,khd->hqk", query_part, key_flat, preferred_element_type=jnp.float32)
            * scale
        )
        scores = jnp.where(head_key_ok[None, None, :], scores, -1e30)
        top = jnp.max(scores, axis=-1)
        weights_exp = jnp.exp(scores - top[..., None])
        weight_sum = jnp.sum(weights_exp, axis=-1)
        probs = weights_exp / weight_sum[..., None]
        result = jnp.einsum(
            "hqk,khd->qhd",
            probs.astype(jnp.bfloat16),
            value_flat,
            preferred_element_type=jnp.float32,
        )
        return (result, jnp.transpose(top + jnp.log(weight_sum)))

    outs_blocks, lse_blocks = lax.map(
        one_query, query_flat.reshape(span // query_block, query_block, head_part, HEAD_DIM)
    )
    heads_out = outs_blocks.reshape(span, 1, head_part, HEAD_DIM)
    heads_lse = lse_blocks.reshape(span, 1, head_part)
    self_back = lax.all_to_all(
        heads_out.astype(jnp.bfloat16), "seq", split_axis=0, concat_axis=1, tiled=True
    ).astype(heads_out.dtype)
    self_out3 = self_back.reshape(row_count, heads, HEAD_DIM)
    self_out = self_out3.reshape(row_count, width)
    mixed = self_out + gate_cross * cross_out
    mixed_low = mixed.astype(jnp.bfloat16)
    attn_out = bf_dot(mixed_low, full_out)
    (resid_one, ffn_pre), middle_back = jax.vjp(
        middle, tokens_f, attn_out, gain_f[1], gate_attn, gain_f[2], scale_ffn
    )
    hidden_ffn = ffn_pre.astype(jnp.bfloat16)
    gate_proj = bf_dot(hidden_ffn, full_gate)
    up_proj = bf_dot(hidden_ffn, full_up)
    act_pre, act_back = jax.vjp(activate, gate_proj, up_proj)
    act_low = act_pre.astype(jnp.bfloat16)
    ffn_out = bf_dot(act_low, full_down)
    out_f, finish_back = jax.vjp(finish, resid_one, ffn_out, gain_f[3], gate_ffn)
    block_out = out_f.astype(jnp.bfloat16)
    row_live = (row_ids < live_rows).astype(jnp.float32)
    weighted = (
        cotangent.astype(jnp.float32) * row_live[:, None] * (bucket_count * span / token_total)
    )
    d_resid, d_ffn_out, d_gain_last, d_gate_ffn = finish_back(weighted)
    d_ffn_low = d_ffn_out.astype(jnp.bfloat16)
    d_act = bf_dot(d_ffn_low, full_down.T)
    d_gate_proj, d_up_proj = act_back(d_act)
    d_gate_low = d_gate_proj.astype(jnp.bfloat16)
    d_up_low = d_up_proj.astype(jnp.bfloat16)
    d_hidden_ffn = bf_dot(d_gate_low, full_gate.T) + bf_dot(d_up_low, full_up.T)
    d_tokens_one, d_attn_out, d_gain_post, d_gate_attn, d_gain_ffn, d_scale_ffn = middle_back(
        (d_resid, d_hidden_ffn)
    )
    d_attn_low = d_attn_out.astype(jnp.bfloat16)
    d_mixed_low = bf_dot(d_attn_low, full_out.T).astype(jnp.bfloat16)
    d_mixed = d_mixed_low.astype(jnp.float32)
    d_cross_low = (gate_cross * d_mixed).astype(jnp.bfloat16)
    grad_cross = jnp.sum(d_mixed * cross_out, axis=0) * (1.0 - gate_cross * gate_cross)
    d_cross3 = d_cross_low.reshape(row_count, heads, HEAD_DIM)
    d_cap_probs = jnp.einsum(
        "qhd,khd->hqk", d_cross3, cap_values3, preferred_element_type=jnp.float32
    )
    d_cap_scores = cap_probs * (
        d_cap_probs - jnp.sum(cap_probs * d_cap_probs, axis=-1, keepdims=True)
    )
    d_cap_low = d_cap_scores.astype(jnp.bfloat16)
    d_query_cross = (
        jnp.einsum("hqk,khd->qhd", d_cap_low, cap_keys3, preferred_element_type=jnp.float32) * scale
    )
    d_cap_keys = (
        jnp.einsum("hqk,qhd->khd", d_cap_low, query_three, preferred_element_type=jnp.float32)
        * scale
    )
    d_cap_values = jnp.einsum(
        "hqk,qhd->khd", cap_probs.astype(jnp.bfloat16), d_cross3, preferred_element_type=jnp.float32
    )
    own_cap_keys, own_cap_values = (
        lax.psum_scatter(
            d_cap_keys.reshape(cap_keys.shape[0], width).astype(jnp.bfloat16),
            "seq",
            scatter_dimension=0,
            tiled=True,
        ).astype(jnp.float32),
        lax.psum_scatter(
            d_cap_values.reshape(cap_keys.shape[0], width).astype(jnp.bfloat16),
            "seq",
            scatter_dimension=0,
            tiled=True,
        ).astype(jnp.float32),
    )
    d_cap_key_proj, d_gain_cap = cap_back(own_cap_keys)
    d_cap_key_low = d_cap_key_proj.astype(jnp.bfloat16)
    d_cap_value_low = own_cap_values.astype(jnp.bfloat16)
    d_out3 = d_mixed_low.reshape(row_count, heads, HEAD_DIM)
    d_out_four = d_out3.reshape(row_count, seq_count, head_share, HEAD_DIM)
    query_ex, key_ex, value_ex, d_out_ex = (
        lax.all_to_all(query_four, "seq", split_axis=1, concat_axis=0, tiled=True),
        lax.all_to_all(key_four, "seq", split_axis=1, concat_axis=0, tiled=True),
        lax.all_to_all(value_four, "seq", split_axis=1, concat_axis=0, tiled=True),
        lax.all_to_all(d_out_four, "seq", split_axis=1, concat_axis=0, tiled=True),
    )
    query_heads = query_ex[:, 0]
    key_heads = key_ex[:, 0]
    value_heads = value_ex[:, 0]
    d_out_heads = d_out_ex[:, 0]
    head_part = query_heads.shape[1]
    heads_flat = heads_out[:, 0]
    lse_flat = heads_lse[:, 0]
    head_delta = jnp.sum(d_out_heads.astype(jnp.float32) * heads_flat, axis=-1)
    key_ok = jnp.arange(span) < live_rows

    def back_query(state, block_idx):
        d_key_acc, d_value_acc = state
        query_part = lax.dynamic_slice_in_dim(query_heads, block_idx * query_block, query_block, 0)
        d_out_part = lax.dynamic_slice_in_dim(d_out_heads, block_idx * query_block, query_block, 0)
        lse_part = jnp.transpose(
            lax.dynamic_slice_in_dim(lse_flat, block_idx * query_block, query_block, 0)
        )
        delta_part = jnp.transpose(
            lax.dynamic_slice_in_dim(head_delta, block_idx * query_block, query_block, 0)
        )
        scores = (
            jnp.einsum("qhd,khd->hqk", query_part, key_heads, preferred_element_type=jnp.float32)
            * scale
        )
        scores = jnp.where(key_ok[None, None, :], scores, -1e30)
        probs = jnp.exp(scores - lse_part[..., None])
        d_probs = jnp.einsum(
            "qhd,khd->hqk", d_out_part, value_heads, preferred_element_type=jnp.float32
        )
        d_scores = (probs * (d_probs - delta_part[..., None])).astype(jnp.bfloat16)
        d_query_part = (
            jnp.einsum("hqk,khd->qhd", d_scores, key_heads, preferred_element_type=jnp.float32)
            * scale
        )
        d_key_acc = (
            d_key_acc
            + jnp.einsum("hqk,qhd->khd", d_scores, query_part, preferred_element_type=jnp.float32)
            * scale
        )
        d_value_acc = d_value_acc + jnp.einsum(
            "hqk,qhd->khd",
            probs.astype(jnp.bfloat16),
            d_out_part,
            preferred_element_type=jnp.float32,
        )
        return ((d_key_acc, d_value_acc), d_query_part)

    zero_heads = jnp.zeros((span, head_part, HEAD_DIM), jnp.float32)
    (d_key_heads, d_value_heads), d_query_blocks = lax.scan(
        back_query, (zero_heads, zero_heads), jnp.arange(span // query_block)
    )
    d_query_back, d_key_back, d_value_back = (
        lax.all_to_all(
            d_query_blocks.reshape(span, 1, head_part, HEAD_DIM).astype(jnp.bfloat16),
            "seq",
            split_axis=0,
            concat_axis=1,
            tiled=True,
        ).astype(jnp.float32),
        lax.all_to_all(
            d_key_heads.reshape(span, 1, head_part, HEAD_DIM).astype(jnp.bfloat16),
            "seq",
            split_axis=0,
            concat_axis=1,
            tiled=True,
        ).astype(jnp.float32),
        lax.all_to_all(
            d_value_heads.reshape(span, 1, head_part, HEAD_DIM).astype(jnp.bfloat16),
            "seq",
            split_axis=0,
            concat_axis=1,
            tiled=True,
        ).astype(jnp.float32),
    )
    d_query_self = d_query_back.reshape(row_count, width)
    d_key_sum = d_key_back.reshape(row_count, width)
    d_value_sum = d_value_back.reshape(row_count, width)
    d_query_norm = d_query_self + d_query_cross.reshape(row_count, width)
    d_query_proj, d_key_proj, d_gain_query, d_gain_key = norm_back((d_query_norm, d_key_sum))
    d_query_low = d_query_proj.astype(jnp.bfloat16)
    d_key_low = d_key_proj.astype(jnp.bfloat16)
    d_value_low = d_value_sum.astype(jnp.bfloat16)
    d_hidden = (
        bf_dot(d_query_low, full_query.T)
        + bf_dot(d_key_low, full_key.T)
        + bf_dot(d_value_low, full_value.T)
    )
    d_tokens_two, d_gain_pre, d_scale_attn = pre_back(d_hidden)
    tokens_grad = d_tokens_one + d_tokens_two

    def split_cols(matrix):
        return matrix.reshape(matrix.shape[0], seq_count, matrix.shape[1] // seq_count)

    hidden_all, mixed_all, ffn_all, act_all, caption_all = (
        lax.all_gather(hidden_in, "seq", axis=0, tiled=True),
        lax.all_gather(mixed_low, "seq", axis=0, tiled=True),
        lax.all_gather(hidden_ffn, "seq", axis=0, tiled=True),
        lax.all_gather(act_low, "seq", axis=0, tiled=True),
        lax.all_gather(captions, "seq", axis=0, tiled=True),
    )
    column_parts = (
        lax.all_to_all(split_cols(d_query_low), "seq", split_axis=1, concat_axis=0, tiled=True),
        lax.all_to_all(split_cols(d_key_low), "seq", split_axis=1, concat_axis=0, tiled=True),
        lax.all_to_all(split_cols(d_value_low), "seq", split_axis=1, concat_axis=0, tiled=True),
        lax.all_to_all(split_cols(d_attn_low), "seq", split_axis=1, concat_axis=0, tiled=True),
        lax.all_to_all(split_cols(d_gate_low), "seq", split_axis=1, concat_axis=0, tiled=True),
        lax.all_to_all(split_cols(d_up_low), "seq", split_axis=1, concat_axis=0, tiled=True),
        lax.all_to_all(split_cols(d_ffn_low), "seq", split_axis=1, concat_axis=0, tiled=True),
        lax.all_to_all(split_cols(d_cap_key_low), "seq", split_axis=1, concat_axis=0, tiled=True),
        lax.all_to_all(split_cols(d_cap_value_low), "seq", split_axis=1, concat_axis=0, tiled=True),
    )
    (
        col_query,
        col_key,
        col_value,
        col_out,
        col_gate,
        col_up,
        col_down,
        col_cap_key,
        col_cap_value,
    ) = tuple((piece[:, 0] for piece in column_parts))
    grad_query = left_dot(hidden_all, col_query)
    grad_key = left_dot(hidden_all, col_key)
    grad_value = left_dot(hidden_all, col_value)
    grad_out = left_dot(mixed_all, col_out)
    grad_gate = left_dot(ffn_all, col_gate)
    grad_up = left_dot(ffn_all, col_up)
    grad_down = left_dot(act_all, col_down)
    grad_cap_key = left_dot(caption_all, col_cap_key)
    grad_cap_value = left_dot(caption_all, col_cap_value)
    d_modulation = jnp.concatenate([d_scale_attn, d_gate_attn, d_scale_ffn, d_gate_ffn])
    grad_gains = jnp.stack(
        [d_gain_pre, d_gain_post, d_gain_ffn, d_gain_last, d_gain_query, d_gain_key, d_gain_cap]
    )
    slice_width = width // (bucket_count * seq_count)
    shaped_gains = grad_gains.reshape(grad_gains.shape[0], bucket_count, seq_count, slice_width)
    shaped_cross = grad_cross.reshape(bucket_count, seq_count, slice_width)
    mod_part, gains_part, cross_part = (
        lax.psum_scatter(
            d_modulation.astype(jnp.bfloat16), "seq", scatter_dimension=0, tiled=True
        ).astype(jnp.float32),
        lax.psum_scatter(
            shaped_gains.astype(jnp.bfloat16), "seq", scatter_dimension=2, tiled=True
        ).astype(jnp.float32),
        lax.psum_scatter(
            shaped_cross.astype(jnp.bfloat16), "seq", scatter_dimension=1, tiled=True
        ).astype(jnp.float32),
    )
    grad_mod = cond.astype(jnp.float32)[:, None] * mod_part[None, :]
    (
        sum_query,
        sum_key,
        sum_value,
        sum_out,
        sum_cap_key,
        sum_cap_value,
        sum_gate,
        sum_up,
        sum_down,
        sum_mod,
        sum_gains,
        sum_cross,
    ) = (
        lax.psum_scatter(
            grad_query.astype(jnp.bfloat16), "bucket", scatter_dimension=0, tiled=True
        ).astype(jnp.float32),
        lax.psum_scatter(
            grad_key.astype(jnp.bfloat16), "bucket", scatter_dimension=0, tiled=True
        ).astype(jnp.float32),
        lax.psum_scatter(
            grad_value.astype(jnp.bfloat16), "bucket", scatter_dimension=0, tiled=True
        ).astype(jnp.float32),
        lax.psum_scatter(
            grad_out.astype(jnp.bfloat16), "bucket", scatter_dimension=0, tiled=True
        ).astype(jnp.float32),
        lax.psum_scatter(
            grad_cap_key.astype(jnp.bfloat16), "bucket", scatter_dimension=0, tiled=True
        ).astype(jnp.float32),
        lax.psum_scatter(
            grad_cap_value.astype(jnp.bfloat16), "bucket", scatter_dimension=0, tiled=True
        ).astype(jnp.float32),
        lax.psum_scatter(
            grad_gate.astype(jnp.bfloat16), "bucket", scatter_dimension=0, tiled=True
        ).astype(jnp.float32),
        lax.psum_scatter(
            grad_up.astype(jnp.bfloat16), "bucket", scatter_dimension=0, tiled=True
        ).astype(jnp.float32),
        lax.psum_scatter(
            grad_down.astype(jnp.bfloat16), "bucket", scatter_dimension=0, tiled=True
        ).astype(jnp.float32),
        lax.psum_scatter(
            grad_mod.astype(jnp.bfloat16), "bucket", scatter_dimension=0, tiled=True
        ).astype(jnp.float32),
        lax.psum_scatter(
            gains_part.astype(jnp.bfloat16), "bucket", scatter_dimension=1, tiled=True
        ).astype(jnp.float32),
        lax.psum_scatter(
            cross_part.astype(jnp.bfloat16), "bucket", scatter_dimension=0, tiled=True
        ).astype(jnp.float32),
    )
    sum_gains = sum_gains.reshape(grad_gains.shape[0], slice_width)
    sum_cross = sum_cross.reshape(slice_width)
    return (
        block_out,
        tokens_grad,
        sum_query,
        sum_key,
        sum_value,
        sum_out,
        sum_cap_key,
        sum_cap_value,
        sum_gate,
        sum_up,
        sum_down,
        sum_mod,
        sum_gains,
        sum_cross,
    )


def solution(mesh):
    in_specs = (
        P(("bucket", "seq"), None),
        P(("bucket", "seq"), None),
        P(("bucket", "seq"), None),
        P(),
        P(),
        P(),
        P(("bucket", "seq"), None),
        P(("bucket", "seq"), None),
        P(("bucket", "seq"), None),
        P(("bucket", "seq"), None),
        P(("bucket", "seq"), None),
        P(("bucket", "seq"), None),
        P(("bucket", "seq"), None),
        P(("bucket", "seq"), None),
        P(("bucket", "seq"), None),
        P(("bucket", "seq"), None),
        P(None, ("bucket", "seq")),
        P(("bucket", "seq")),
    )
    out_specs = (
        P(("bucket", "seq"), None),
        P(("bucket", "seq"), None),
        P("bucket", "seq"),
        P("bucket", "seq"),
        P("bucket", "seq"),
        P("bucket", "seq"),
        P("bucket", "seq"),
        P("bucket", "seq"),
        P("bucket", "seq"),
        P("bucket", "seq"),
        P("bucket", "seq"),
        P("bucket", "seq"),
        P(None, ("bucket", "seq")),
        P(("bucket", "seq")),
    )
    return jax.shard_map(
        on_device, mesh=mesh, in_specs=in_specs, out_specs=out_specs, check_vma=False
    )
```

profile of v0, /device:TPU:8, one launch (start us, length us, event | category | flops | bytes accessed | tf_op | source)
XLA Modules:
  0.0 1802.1 jit_solution(4235463223193753558)
XLA Ops:
  14.0 65.8 %all-gather = bf16[32,48,7]{1,2,0:T(8,128)(2,1)S(1)} all-gather(bf16[1,48,7]{1,2,0:T(8,128)(2,1)} %bitcast.337), channel_id=1, replica_groups=mesh['bucket'=8,'seq'=4] {'bucket','seq'}, dimensions={0}, use_global_device_ids=true | all-gather | bytes 22176 | tf_op jit(solution)/shard_map/all_gather | solution.py:98
  83.6 42.5 %all-reduce = bf16[1536]{0:T(1024)(128)(2,1)S(1)} all-reduce(bf16[1536]{0:T(1024)(128)(2,1)S(1)} %dynamic-update-slice), channel_id=1, replica_groups=mesh['bucket'=8,'seq'=4] {'bucket','seq'}, use_global_device_ids=true, to_apply=%add | all-reduce | flops 1536 | bytes 6144
  131.7 6.3 fusion.80
  139.3 35.6 %all-gather.19.cloned.1.call-done = bf16[1536,1536]{1,0:T(8,128)(2,1)} async-done(((bf16[48,1536]{1,0:T(8,128)(2,1)}), bf16[1536,1536]{1,0:T(8,128)(2,1)}) %all-gather.19.cloned.1.call-update) | async-done | bytes 4718608 | tf_op jit(solution)/shard_map/all_gather | solution.py:90
  179.0 4.2 all-to-all-start
  183.2 60.8 %all-gather.23.cloned.1.call-done = bf16[1536,1536]{1,0:T(8,128)(2,1)} async-done(((bf16[48,1536]{1,0:T(8,128)(2,1)}), bf16[1536,1536]{1,0:T(8,128)(2,1)}) %all-gather.23.cloned.1.call-update) | async-done | bytes 4718608 | tf_op jit(solution)/shard_map/all_gather | solution.py:89
  248.7 60.3 %all-gather.21.cloned.1.call-done = bf16[1536,1536]{1,0:T(8,128)(2,1)} async-done(((bf16[48,1536]{1,0:T(8,128)(2,1)}), bf16[1536,1536]{1,0:T(8,128)(2,1)}) %all-gather.21.cloned.1.call-update) | async-done | bytes 4718608 | tf_op jit(solution)/shard_map/all_gather | solution.py:88
  309.0 4.0 fusion.81
  315.8 89.8 %all-gather.27.cloned.1.call-done = bf16[4096,1536]{1,0:T(8,128)(2,1)} async-done(((bf16[128,1536]{1,0:T(8,128)(2,1)}), bf16[4096,1536]{1,0:T(8,128)(2,1)}) %all-gather.27.cloned.1.call-update) | async-done | bytes 12582928 | tf_op jit(solution)/shard_map/all_gather | solution.py:92
  405.6 7.7 fusion.78
  425.1 4.5 all-to-all-start.1
  429.6 40.5 %all_gather.66 = bf16[256,1536]{1,0:T(8,128)(2,1)} all-gather(bf16[64,1536]{1,0:T(8,128)(2,1)S(1)} %get-tuple-element.182), channel_id=1, replica_groups=mesh['bucket'=8,'seq'=4] {'seq'}, dimensions={0}, use_global_device_ids=true | all-gather | bytes 983040 | tf_op jit(solution)/shard_map/all_gather | solution.py:155
  471.6 4.7 fusion.79
  476.3 4.1 all-to-all-start.2
  480.3 38.9 %all-gather.25.cloned.1.call-done = bf16[4096,1536]{1,0:T(8,128)(2,1)} async-done(((bf16[128,1536]{1,0:T(8,128)(2,1)}), bf16[4096,1536]{1,0:T(8,128)(2,1)}) %all-gather.25.cloned.1.call-update) | async-done | bytes 12582928 | tf_op jit(solution)/shard_map/all_gather | solution.py:93
  519.2 7.5 convolution_convert_fusion.11
  538.0 7.1 all-to-all-start.3
  545.2 31.9 %all_gather.64 = bf16[256,1536]{1,0:T(8,128)(2,1)S(1)} all-gather(bf16[64,1536]{1,0:T(8,128)(2,1)} %convolution_convert_fusion.11), channel_id=1, replica_groups=mesh['bucket'=8,'seq'=4] {'seq'}, dimensions={0}, use_global_device_ids=true | all-gather | bytes 983040 | tf_op jit(solution)/shard_map/all_gather | solution.py:156
  585.5 6.8 all-gather.29.cloned.1.call-done
  596.6 92.4 %all-gather.31.cloned.1.call-done = bf16[1536,4096]{1,0:T(8,128)(2,1)} async-done(((bf16[48,4096]{1,0:T(8,128)(2,1)}), bf16[1536,4096]{1,0:T(8,128)(2,1)}) %all-gather.31.cloned.1.call-update) | async-done | bytes 12582928 | tf_op jit(solution)/shard_map/all_gather | solution.py:94
  689.0 7.7 fusion.83
  696.7 89.5 %all-gather.33.cloned.1.call-done = bf16[1536,4096]{1,0:T(8,128)(2,1)} async-done(((bf16[48,4096]{1,0:T(8,128)(2,1)}), bf16[1536,4096]{1,0:T(8,128)(2,1)}) %all-gather.33.cloned.1.call-update) | async-done | bytes 12582928 | tf_op jit(solution)/shard_map/all_gather | solution.py:95
  786.2 9.0 multiply_convert_fusion.4
  795.2 88.1 %all-gather.35.cloned.1.call-done = bf16[4096,1536]{1,0:T(8,128)(2,1)} async-done(((bf16[128,1536]{1,0:T(8,128)(2,1)}), bf16[4096,1536]{1,0:T(8,128)(2,1)}) %all-gather.35.cloned.1.call-update) | async-done | bytes 12582928 | tf_op jit(solution)/shard_map/all_gather | solution.py:96
  883.3 6.8 multiply_reduce_fusion.14
  892.4 10.0 multiply_convert_fusion.3
  902.5 9.6 fusion.84
  912.2 9.9 multiply_reduce_fusion.4
  944.7 5.2 all-to-all-start.4
  951.3 9.7 all-to-all-done.4
  966.0 5.5 multiply_convert_fusion.1
  980.2 6.2 all-to-all-start.5
  995.8 7.0 all-to-all-done.5
  1002.8 7.8 all-to-all-start.6
  1010.6 5.1 fusion.26
  1021.4 6.6 all-to-all-done.6
  1028.0 7.4 all-to-all-start.7
  1073.7 5.2 all-to-all-start.8
  1081.9 4.1 fusion.85
  1086.1 4.0 convolution_add_fusion.1
  1102.5 15.4 all_to_all.258
  1121.8 22.1 %all_to_all.259 = bf16[128,4,384]{2,0,1:T(8,128)(2,1)S(1)} all-to-all(bf16[128,4,384]{2,0,1:T(8,128)(2,1)S(1)} %copy.312), channel_id=1, replica_groups=mesh['bucket'=8,'seq'=4] {'seq'}, dimensions={1} | all-to-all | bytes 786432 | tf_op jit(solution)/shard_map/all_to_all | solution.py:393
  1147.5 20.4 %all_to_all.260 = bf16[128,4,384]{2,0,1:T(8,128)(2,1)S(1)} all-to-all(bf16[128,4,384]{2,0,1:T(8,128)(2,1)S(1)} %bitcast.314), channel_id=1, replica_groups=mesh['bucket'=8,'seq'=4] {'seq'}, dimensions={1} | all-to-all | bytes 786432 | tf_op jit(solution)/shard_map/all_to_all | solution.py:394
  1173.1 17.9 all-reduce.7
  1195.2 7.5 all-to-all-start.12
  1202.8 10.1 all-to-all-done.12
  1212.9 4.3 fusion.3
  1218.3 18.0 all_to_all.261
  1239.3 50.5 %all_to_all.262 = bf16[128,4,1024]{2,0,1:T(8,128)(2,1)S(1)} all-to-all(bf16[128,4,1024]{2,0,1:T(8,128)(2,1)S(1)} %bitcast.290), channel_id=1, replica_groups=mesh['bucket'=8,'seq'=4] {'seq'}, dimensions={1} | all-to-all | bytes 2097152 | tf_op jit(solution)/shard_map/all_to_all | solution.py:395
  1289.7 5.0 convolution_convert_fusion.4
  1296.1 24.2 %all_to_all.263 = bf16[128,4,1024]{2,0,1:T(8,128)(2,1)S(1)} all-to-all(bf16[128,4,1024]{2,0,1:T(8,128)(2,1)S(1)} %bitcast.291), channel_id=1, replica_groups=mesh['bucket'=8,'seq'=4] {'seq'}, dimensions={1} | all-to-all | bytes 2097152 | tf_op jit(solution)/shard_map/all_to_all | solution.py:396
  1320.3 4.9 convolution_convert_fusion.3
  1326.2 12.0 all_to_all.264
  1338.2 6.2 convolution_convert_fusion.2
  1348.9 22.5 %all-reduce.6 = (bf16[7,8,1,48]{3,0,2,1:T(8,128)(2,1)S(1)}, bf16[8,1,48]{2,1,0:T(2,128)(2,1)S(1)}) all-reduce(bf16[7,8,1,48]{3,0,2,1:T(8,128)(2,1)S(1)} %copy.326, bf16[8,1,48]{2,1,0:T(2,128)(2,1)S(1)} %copy.329), channel_id=16, replica_groups=mesh['bucket'=8,'seq'=4] {'bucket'}, use_global_device_ids=true, to_apply=%region_49.50.clone | all-reduce | flops 3072 | bytes 12288
  1375.7 38.2 %reduce-scatter.18.cloned.1.call-done = bf16[192,384]{1,0:T(8,128)(2,1)} async-done(((bf16[1536,384]{1,0:T(8,128)(2,1)}), bf16[192,384]{1,0:T(8,128)(2,1)}) %reduce-scatter.18.cloned.1.call-update) | async-done | bytes 147472 | tf_op jit(solution)/shard_map/reduce_scatter | solution.py:457
  1415.6 38.7 %reduce-scatter.20.cloned.1.call-done = bf16[192,384]{1,0:T(8,128)(2,1)} async-done(((bf16[1536,384]{1,0:T(8,128)(2,1)}), bf16[192,384]{1,0:T(8,128)(2,1)}) %reduce-scatter.20.cloned.1.call-update) | async-done | bytes 147472 | tf_op jit(solution)/shard_map/reduce_scatter | solution.py:460
  1456.0 38.4 %reduce-scatter.22.cloned.1.call-done = bf16[192,384]{1,0:T(8,128)(2,1)} async-done(((bf16[1536,384]{1,0:T(8,128)(2,1)}), bf16[192,384]{1,0:T(8,128)(2,1)}) %reduce-scatter.22.cloned.1.call-update) | async-done | bytes 147472 | tf_op jit(solution)/shard_map/reduce_scatter | solution.py:463
  1496.0 48.4 %reduce-scatter.38.cloned.1.call-done = bf16[128,1536]{1,0:T(8,128)(2,1)} async-done(((bf16[1024,1536]{1,0:T(8,128)(2,1)}), bf16[128,1536]{1,0:T(8,128)(2,1)}) %reduce-scatter.38.cloned.1.call-update) | async-done | bytes 393232 | tf_op jit(solution)/shard_map/reduce_scatter | solution.py:481
  1546.4 47.5 %reduce-scatter.26.cloned.1.call-done = bf16[512,384]{0,1:T(8,128)(2,1)} async-done(((bf16[4096,384]{0,1:T(8,128)(2,1)}), bf16[512,384]{0,1:T(8,128)(2,1)}) %reduce-scatter.26.cloned.1.call-update) | async-done | bytes 393232 | tf_op jit(solution)/shard_map/reduce_scatter | solution.py:466
  1596.0 48.0 %reduce-scatter.30.cloned.1.call-done = bf16[512,384]{0,1:T(8,128)(2,1)} async-done(((bf16[4096,384]{0,1:T(8,128)(2,1)}), bf16[512,384]{0,1:T(8,128)(2,1)}) %reduce-scatter.30.cloned.1.call-update) | async-done | bytes 393232 | tf_op jit(solution)/shard_map/reduce_scatter | solution.py:469
  1646.0 47.5 %reduce-scatter.32.cloned.1.call-done = bf16[192,1024]{1,0:T(8,128)(2,1)} async-done(((bf16[1536,1024]{1,0:T(8,128)(2,1)}), bf16[192,1024]{1,0:T(8,128)(2,1)}) %reduce-scatter.32.cloned.1.call-update) | async-done | bytes 393232 | tf_op jit(solution)/shard_map/reduce_scatter | solution.py:472
  1695.4 47.9 %reduce-scatter.34.cloned.1.call-done = bf16[192,1024]{1,0:T(8,128)(2,1)} async-done(((bf16[1536,1024]{1,0:T(8,128)(2,1)}), bf16[192,1024]{1,0:T(8,128)(2,1)}) %reduce-scatter.34.cloned.1.call-update) | async-done | bytes 393232 | tf_op jit(solution)/shard_map/reduce_scatter | solution.py:475
  1745.2 47.7 %reduce-scatter.36.cloned.1.call-done = bf16[512,384]{1,0:T(8,128)(2,1)} async-done(((bf16[4096,384]{1,0:T(8,128)(2,1)}), bf16[512,384]{1,0:T(8,128)(2,1)}) %reduce-scatter.36.cloned.1.call-update) | async-done | bytes 393232 | tf_op jit(solution)/shard_map/reduce_scatter | solution.py:478
  (519 shorter events, 220.3 us)
Async XLA Ops:
  7.2 72.8 %copy-start.119 = (s32[8]{0:T(128)S(1)}, s32[8]{0:T(128)}, u32[]{:S(2)}) copy-start(s32[8]{0:T(128)} %param.23) | copy-start | bytes 100
  7.2 74.8 %copy-start.118 = (s32[8]{0:T(128)S(1)}, s32[8]{0:T(128)}, u32[]{:S(2)}) copy-start(s32[8]{0:T(128)} %param.21) | copy-start | bytes 100
  7.2 76.1 %copy-start.120 = (bf16[48]{0:T(256)(128)(2,1)S(1)}, bf16[48]{0:T(256)(128)(2,1)}, u32[]{:S(2)}) copy-start(bf16[48]{0:T(256)(128)(2,1)} %param.35) | copy-start | bytes 292
  7.2 120.0 %copy-start.121 = (s32[8]{0:T(128)S(1)}, s32[8]{0:T(128)}, u32[]{:S(2)}) copy-start(s32[8]{0:T(128)} %param.22) | copy-start | bytes 100
  7.2 123.7 %copy-start.4 = (bf16[128,1536]{1,0:T(8,128)(2,1)S(1)}, bf16[128,1536]{1,0:T(8,128)(2,1)}, u32[]{:S(2)}) copy-start(bf16[128,1536]{1,0:T(8,128)(2,1)} %param.18) | copy-start | bytes 1179652
  7.2 124.5 %all-gather.17.cloned.1.call-start = ((), (), s32[]{:S(2)}) async-start(), calls=%async_computation.30 | async-start | bytes 12976128 | tf_op jit(solution)/shard_map/all_gather | solution.py:97
  8.0 167.0 %all-gather.19.cloned.1.call-start = ((), (), s32[]{:S(2)}) async-start(), calls=%async_computation.31 | async-start | bytes 4866048 | tf_op jit(solution)/shard_map/all_gather | solution.py:90
  8.7 235.2 %all-gather.23.cloned.1.call-start = ((), (), s32[]{:S(2)}) async-start(), calls=%async_computation.33 | async-start | bytes 4866048 | tf_op jit(solution)/shard_map/all_gather | solution.py:89
  9.4 299.6 %all-gather.21.cloned.1.call-start = ((), (), s32[]{:S(2)}) async-start(), calls=%async_computation.32 | async-start | bytes 4866048 | tf_op jit(solution)/shard_map/all_gather | solution.py:88
  10.0 395.6 %all-gather.27.cloned.1.call-start = ((), (), s32[]{:S(2)}) async-start(), calls=%async_computation.35 | async-start | bytes 12976128 | tf_op jit(solution)/shard_map/all_gather | solution.py:92
  10.6 508.6 %all-gather.25.cloned.1.call-start = ((), (), s32[]{:S(2)}) async-start(), calls=%async_computation.34 | async-start | bytes 12976128 | tf_op jit(solution)/shard_map/all_gather | solution.py:93
  11.2 581.1 %all-gather.29.cloned.1.call-start = ((), (), s32[]{:S(2)}) async-start(), calls=%async_computation.36 | async-start | bytes 4866048 | tf_op jit(solution)/shard_map/all_gather | solution.py:91
  11.9 677.1 %all-gather.31.cloned.1.call-start = ((), (), s32[]{:S(2)}) async-start(), calls=%async_computation.37 | async-start | bytes 12976128 | tf_op jit(solution)/shard_map/all_gather | solution.py:94
  12.7 773.5 %all-gather.33.cloned.1.call-start = ((), (), s32[]{:S(2)}) async-start(), calls=%async_computation.38 | async-start | bytes 12976128 | tf_op jit(solution)/shard_map/all_gather | solution.py:95
  13.4 869.9 %all-gather.35.cloned.1.call-start = ((), (), s32[]{:S(2)}) async-start(), calls=%async_computation.39 | async-start | bytes 12976128 | tf_op jit(solution)/shard_map/all_gather | solution.py:96
  130.9 285.9 %copy-start.70 = (f32[1536]{0:T(1024)}, f32[1536]{0:T(1024)S(1)}, u32[]{:S(2)}) copy-start(f32[1536]{0:T(1024)S(1)} %get-tuple-element.168) | copy-start | bytes 18436
  131.0 293.3 %copy-start.57 = (f32[1536]{0:T(1024)}, f32[1536]{0:T(1024)S(1)}, u32[]{:S(2)}) copy-start(f32[1536]{0:T(1024)S(1)} %get-tuple-element.167) | copy-start | bytes 18436
  138.9 170.1 %copy-start.5 = (bf16[128,1536]{1,0:T(8,128)(2,1)}, bf16[128,1536]{1,0:T(8,128)(2,1)S(1)}, u32[]{:S(2)}) copy-start(bf16[128,1536]{1,0:T(8,128)(2,1)S(1)} %fusion.33) | copy-start | bytes 1179652
  179.0 246.1 %all-to-all-start = ((bf16[128,4,6,64]{0,3,2,1:T(8,128)(2,1)}), bf16[128,4,6,64]{0,3,2,1:T(8,128)(2,1)}, u32[]{:S(2)}, u32[]{:S(2)}) async-start(bf16[128,4,6,64]{0,3,2,1:T(8,128)(2,1)} %bitcast.4), calls=%async_computation | async-start | bytes 786432 | tf_op jit(solution)/shard_map/all_to_all | solution.py:179
  247.1 169.8 %copy-start.2 = (f32[128,1536]{1,0:T(8,128)}, f32[128,1536]{1,0:T(8,128)S(1)}, u32[]{:S(2)}) copy-start(f32[128,1536]{1,0:T(8,128)S(1)} %fusion.82) | copy-start | bytes 2359300
  247.4 65.7 %copy-start.8 = (f32[128,1536]{0,1:T(8,128)}, f32[128,1536]{0,1:T(8,128)S(1)}, u32[]{:S(2)}) copy-start(f32[128,1536]{0,1:T(8,128)S(1)} %copy.277) | copy-start | bytes 2359300
  247.5 61.6 %copy-start.77 = (f32[128,24]{0,1:T(8,128)}, f32[128,24]{0,1:T(8,128)S(1)}, u32[]{:S(2)}) copy-start(f32[128,24]{0,1:T(8,128)S(1)} %multiply_reduce_fusion.17) | copy-start | bytes 36868
  313.0 92.6 %copy-start.6 = (bf16[64,4096]{1,0:T(8,128)(2,1)S(1)}, bf16[64,4096]{1,0:T(8,128)(2,1)}, u32[]{:S(2)}) copy-start(bf16[64,4096]{1,0:T(8,128)(2,1)} %param.19) | copy-start | bytes 1572868
  314.6 98.8 %copy-start.75 = (f32[128,24]{0,1:T(8,128)}, f32[128,24]{0,1:T(8,128)S(1)}, u32[]{:S(2)}) copy-start(f32[128,24]{0,1:T(8,128)S(1)} %multiply_reduce_fusion.18) | copy-start | bytes 36868
  314.6 98.7 %copy-start.73 = (f32[128,24]{0,1:T(8,128)}, f32[128,24]{0,1:T(8,128)S(1)}, u32[]{:S(2)}) copy-start(f32[128,24]{0,1:T(8,128)S(1)} %fusion.60) | copy-start | bytes 36868
  315.8 101.1 %copy-start.15 = (f32[128,1536]{1,0:T(8,128)S(1)}, f32[128,1536]{1,0:T(8,128)}, u32[]{:S(2)}) copy-start(f32[128,1536]{1,0:T(8,128)} %copy.278) | copy-start | bytes 2359300
  315.8 101.1 %copy-start.81 = (f32[1536]{0:T(1024)S(1)}, f32[1536]{0:T(1024)}, u32[]{:S(2)}) copy-start(f32[1536]{0:T(1024)} %get-tuple-element.169) | copy-start | bytes 18436
  424.0 47.6 %copy-start.124 = (pred[256]{0:T(512)(128)(4,1)S(1)}, pred[256]{0:T(512)(128)(4,1)}, u32[]{:S(2)}) copy-start(pred[256]{0:T(512)(128)(4,1)} %iota_compare_fusion.1) | copy-start | bytes 772
  424.2 52.1 %copy-start.34 = (f32[64,1536]{1,0:T(8,128)}, f32[64,1536]{1,0:T(8,128)S(1)}, u32[]{:S(2)}) copy-start(f32[64,1536]{1,0:T(8,128)S(1)} %mul.692) | copy-start | bytes 1179652
  425.1 51.2 %all-to-all-start.1 = ((bf16[128,4,6,64]{0,3,2,1:T(8,128)(2,1)}), bf16[128,4,6,64]{0,3,2,1:T(8,128)(2,1)S(1)}, u32[]{:S(2)}, u32[]{:S(2)}) async-start(bf16[128,4,6,64]{0,3,2,1:T(8,128)(2,1)} %bitcast.9), calls=%async_computation.1 | async-start | bytes 786432 | tf_op jit(solution)/shard_map/all_to_all | solution.py:177
  476.3 52.4 %all-to-all-start.2 = ((bf16[128,4,6,64]{0,3,2,1:T(8,128)(2,1)}), bf16[128,4,6,64]{0,3,2,1:T(8,128)(2,1)S(1)}, u32[]{:S(2)}, u32[]{:S(2)}) async-start(bf16[128,4,6,64]{0,3,2,1:T(8,128)(2,1)} %bitcast.14), calls=%async_computation.2 | async-start | bytes 786432 | tf_op jit(solution)/shard_map/all_to_all | solution.py:178
  535.7 42.5 %copy-start.39 = (f32[512,6,64]{0,2,1:T(8,128)}, f32[512,6,64]{0,2,1:T(8,128)S(1)}, u32[]{:S(2)}) copy-start(f32[512,6,64]{0,2,1:T(8,128)S(1)} %fusion.18) | copy-start | bytes 2359300
  535.8 42.4 %copy-start.100 = (f32[24,128]{1,0:T(8,128)S(1)}, f32[24,128]{1,0:T(8,128)}, u32[]{:S(2)}) copy-start(f32[24,128]{1,0:T(8,128)} %get-tuple-element.208) | copy-start | bytes 36868
  538.0 43.4 %all-to-all-start.3 = ((bf16[4,2,24576]{2,1,0:T(2,128)(2,1)}), bf16[4,2,24576]{2,1,0:T(2,128)(2,1)S(1)}, u32[]{:S(2)}, u32[]{:S(2)}) async-start(bf16[4,2,24576]{2,1,0:T(2,128)(2,1)} %reshape.475), calls=%async_computation.3 | async-start | bytes 786432 | tf_op jit(solution)/shard_map/all_to_all | solution.py:209
  545.2 551.6 %reduce-scatter.24.cloned.1.call-start = ((), (), s32[]{:S(2)}) async-start(), calls=%async_computation.46 | async-start | bytes 983040 | tf_op jit(solution)/shard_map/reduce_scatter | solution.py:266
  595.9 100.8 %copy-start.105 = (f32[128]{0:T(128)}, f32[128]{0:T(128)S(1)}, u32[]{:S(2)}) copy-start(f32[128]{0:T(128)S(1)} %fusion.68) | copy-start | bytes 1540
  596.6 189.6 %copy-start.18 = (bf16[128,1536]{1,0:T(8,128)(2,1)}, bf16[128,1536]{1,0:T(8,128)(2,1)S(1)}, u32[]{:S(2)}) copy-start(bf16[128,1536]{1,0:T(8,128)(2,1)S(1)} %multiply_convert_fusion.6) | copy-start | bytes 1179652
  933.9 164.9 %all-gather.37.cloned.1.call-start = ((), (), s32[]{:S(2)}) async-start(), calls=%async_computation.40 | async-start | bytes 1966080 | tf_op jit(solution)/shard_map/all_gather | solution.py:384
  934.5 233.5 %all-gather.39.cloned.1.call-start = ((), (), s32[]{:S(2)}) async-start(), calls=%async_computation.44 | async-start | bytes 1966080 | tf_op jit(solution)/shard_map/all_gather | solution.py:385
  935.2 267.5 %all-gather.41.cloned.1.call-start = ((), (), s32[]{:S(2)}) async-start(), calls=%async_computation.47 | async-start | bytes 2621440 | tf_op jit(solution)/shard_map/all_gather | solution.py:388
  935.8 281.5 %reduce-scatter.28.cloned.1.call-start = ((), (), s32[]{:S(2)}) async-start(), calls=%async_computation.49 | async-start | bytes 983040 | tf_op jit(solution)/shard_map/reduce_scatter | solution.py:272
  939.8 25.1 %copy-start.40 = (f32[512,6,64]{0,2,1:T(8,128)S(1)}, f32[512,6,64]{0,2,1:T(8,128)}, u32[]{:S(2)}) copy-start(f32[512,6,64]{0,2,1:T(8,128)} %copy-done.39) | copy-start | bytes 2359300
  942.2 347.5 %all-gather.43.cloned.1.call-start = ((), (), s32[]{:S(2)}) async-start(), calls=%async_computation.51 | async-start | bytes 1966080 | tf_op jit(solution)/shard_map/all_gather | solution.py:386
  944.7 16.3 all-to-all-start.4
  949.9 388.2 %all-gather.45.cloned.1.call-start = ((), (), s32[]{:S(2)}) async-start(), calls=%async_computation.54 | async-start | bytes 5242880 | tf_op jit(solution)/shard_map/all_gather | solution.py:387
  980.2 22.6 %all-to-all-start.5 = ((bf16[4,2,24576]{2,1,0:T(2,128)(2,1)}), bf16[4,2,24576]{2,1,0:T(2,128)(2,1)S(1)}, u32[]{:S(2)}, u32[]{:S(2)}) async-start(bf16[4,2,24576]{2,1,0:T(2,128)(2,1)} %reshape.477), calls=%async_computation.5 | async-start | bytes 786432 | tf_op jit(solution)/shard_map/all_to_all | solution.py:342
  1002.8 25.2 %all-to-all-start.6 = ((bf16[4,2,24576]{2,1,0:T(2,128)(2,1)}), bf16[4,2,24576]{2,1,0:T(2,128)(2,1)}, u32[]{:S(2)}, u32[]{:S(2)}) async-start(bf16[4,2,24576]{2,1,0:T(2,128)(2,1)} %reshape.479), calls=%async_computation.6 | async-start | bytes 786432 | tf_op jit(solution)/shard_map/all_to_all | solution.py:349
  1015.7 21.7 %copy-start.94 = (bf16[1536]{0:T(1024)(128)(2,1)S(1)}, bf16[1536]{0:T(1024)(128)(2,1)}, u32[]{:S(2)}) copy-start(bf16[1536]{0:T(1024)(128)(2,1)} %get-tuple-element.152) | copy-start | bytes 9220
  1015.7 22.3 %copy-start.93 = (bf16[1536]{0:T(1024)(128)(2,1)S(1)}, bf16[1536]{0:T(1024)(128)(2,1)}, u32[]{:S(2)}) copy-start(bf16[1536]{0:T(1024)(128)(2,1)} %get-tuple-element.158) | copy-start | bytes 9220
  1028.0 34.0 %all-to-all-start.7 = ((bf16[4,2,24576]{2,1,0:T(2,128)(2,1)}), bf16[4,2,24576]{2,1,0:T(2,128)(2,1)}, u32[]{:S(2)}, u32[]{:S(2)}) async-start(bf16[4,2,24576]{2,1,0:T(2,128)(2,1)} %reshape.481), calls=%async_computation.7 | async-start | bytes 786432 | tf_op jit(solution)/shard_map/all_to_all | solution.py:356
  1073.7 25.2 %all-to-all-start.8 = ((bf16[128,4,384]{2,0,1:T(8,128)(2,1)}), bf16[128,4,384]{2,0,1:T(8,128)(2,1)}, u32[]{:S(2)}, u32[]{:S(2)}) async-start(bf16[128,4,384]{2,0,1:T(8,128)(2,1)} %copy.310), calls=%async_computation.8 | async-start | bytes 786432 | tf_op jit(solution)/shard_map/all_to_all | solution.py:391
  1078.9 269.3 %reduce-scatter.40.cloned.1.call-start = ((), (), s32[]{:S(2)}) async-start(), calls=%async_computation.57 | async-start | bytes 71680
  1098.8 275.3 %reduce-scatter.16.cloned.1.call-start = ((), (), s32[]{:S(2)}) async-start(), calls=%async_computation.41 | async-start | bytes 1327104 | tf_op jit(solution)/shard_map/reduce_scatter | solution.py:454
  1102.4 311.6 %reduce-scatter.18.cloned.1.call-start = ((), (), s32[]{:S(2)}) async-start(), calls=%async_computation.42 | async-start | bytes 1327104 | tf_op jit(solution)/shard_map/reduce_scatter | solution.py:457
  1121.4 332.9 %reduce-scatter.20.cloned.1.call-start = ((), (), s32[]{:S(2)}) async-start(), calls=%async_computation.43 | async-start | bytes 1327104 | tf_op jit(solution)/shard_map/reduce_scatter | solution.py:460
  1147.4 347.0 %reduce-scatter.22.cloned.1.call-start = ((), (), s32[]{:S(2)}) async-start(), calls=%async_computation.45 | async-start | bytes 1327104 | tf_op jit(solution)/shard_map/reduce_scatter | solution.py:463
  1168.0 23.1 %copy-start.97 = (f32[1024]{0:T(1024)S(1)}, f32[1024]{0:T(1024)}, u32[]{:S(2)}) copy-start(f32[1024]{0:T(1024)} %get-tuple-element.177) | copy-start | bytes 12292
  1171.6 372.9 %reduce-scatter.38.cloned.1.call-start = ((), (), s32[]{:S(2)}) async-start(), calls=%async_computation.56 | async-start | bytes 3538944 | tf_op jit(solution)/shard_map/reduce_scatter | solution.py:481
  1195.2 17.6 all-to-all-start.12
  1202.8 391.2 %reduce-scatter.26.cloned.1.call-start = ((), (), s32[]{:S(2)}) async-start(), calls=%async_computation.48 | async-start | bytes 3538944 | tf_op jit(solution)/shard_map/reduce_scatter | solution.py:466
  1217.2 426.7 %reduce-scatter.30.cloned.1.call-start = ((), (), s32[]{:S(2)}) async-start(), calls=%async_computation.50 | async-start | bytes 3538944 | tf_op jit(solution)/shard_map/reduce_scatter | solution.py:469
  1239.1 454.3 %reduce-scatter.32.cloned.1.call-start = ((), (), s32[]{:S(2)}) async-start(), calls=%async_computation.52 | async-start | bytes 3538944 | tf_op jit(solution)/shard_map/reduce_scatter | solution.py:472
  1294.8 448.5 %reduce-scatter.34.cloned.1.call-start = ((), (), s32[]{:S(2)}) async-start(), calls=%async_computation.53 | async-start | bytes 3538944 | tf_op jit(solution)/shard_map/reduce_scatter | solution.py:475
  1325.2 467.7 %reduce-scatter.36.cloned.1.call-start = ((), (), s32[]{:S(2)}) async-start(), calls=%async_computation.55 | async-start | bytes 3538944 | tf_op jit(solution)/shard_map/reduce_scatter | solution.py:478
  (103 other events, 612.8 us)
Sparse Core Ops, SparseCore 0:
  10.9 98.0 all-gather.16
  111.9 62.9 all-gather.18
  177.7 66.1 all-gather.22
  246.6 62.3 all-gather.20
  311.7 93.8 all-gather.26
  408.4 110.7 all-gather.24
  522.0 70.2 all-gather.28
  595.1 93.8 all-gather.30
  691.9 94.2 all-gather.32
  789.0 94.2 all-gather.34
  934.0 22.6 reduce-scatter.23
  958.2 45.0 all-gather.36
  1004.8 48.4 all-gather.38
  1054.7 60.2 all-gather.40
  1117.1 31.7 reduce-scatter.27
  1150.4 36.4 all-gather.42
  1188.3 122.3 all-gather.44
  1313.4 19.0 reduce-scatter.39
  1336.0 38.0 reduce-scatter.15
  1377.2 36.7 reduce-scatter.17
  1417.6 36.7 reduce-scatter.19
  1457.6 36.7 reduce-scatter.21
  1498.2 46.1 reduce-scatter.37
  1547.6 46.2 reduce-scatter.25
  1597.7 46.2 reduce-scatter.29
  1647.1 46.2 reduce-scatter.31
  1697.0 46.1 reduce-scatter.33
  1746.6 46.2 reduce-scatter.35
where the time goes:
time: 1820 us; the launch traced here: 1800 us
  waiting for transfers between devices  1010 us (55%)
  blocking collectives  384 us (21%)
  matrix products  177 us (10%)
  local copies, waits for them, and re-layouts  103 us (6%)
  starting transfers between devices  60.8 us (3%)
  other arithmetic  52.4 us (3%)
  between operations  18.8 us (1%)
    dot_general x17, matrix products, bf_dot(): return jnp.dot(left, right, preferred_element_type=jnp.float32)  102 us
    all_gather x1, waiting for transfers between devices, on_device(): lax.all_gather(w_gate, ('bucket', 'seq'), axis=0, tiled=True)  92.4 us
    all_gather x1, waiting for transfers between devices, on_device(): lax.all_gather(w_cap_key, ('bucket', 'seq'), axis=0, tiled=True)  89.8 us
    all_gather x1, waiting for transfers between devices, on_device(): lax.all_gather(w_up, ('bucket', 'seq'), axis=0, tiled=True)  89.5 us
    all_gather x1, waiting for transfers between devices, on_device(): lax.all_gather(w_down, ('bucket', 'seq'), axis=0, tiled=True)  88.1 us
    unnamed x3, blocking collectives  82.9 us
    all_gather x1, blocking collectives, on_device(): lax.all_gather(gains, ('bucket', 'seq'), axis=1, tiled=True)  65.8 us
    all_gather x1, waiting for transfers between devices, on_device(): lax.all_gather(w_key, ('bucket', 'seq'), axis=0, tiled=True)  60.8 us
  transfers between devices with their start and end apart: 38, of which 23 were waited for; matrix products, arithmetic and copies ran while one was open for 15% of the time, Pallas kernels for 0%

commit v1 on v0

v1 whole, which is shorter than its diff:
```python
import functools
import math

import jax
import jax.numpy as jnp
from jax import lax
from jax.experimental import pallas as pl
from jax.experimental.pallas import tpu as pltpu
from jax.sharding import PartitionSpec as P

HEAD_DIM = 64
MESH = pl.DeviceIdType.MESH
F32, BF16 = jnp.float32, jnp.bfloat16


def rms_rows(values):
    return values * lax.rsqrt(jnp.mean(values * values, axis=-1, keepdims=True) + 1e-05)


def head_rms(values):
    shaped = values.reshape(values.shape[:-1] + (values.shape[-1] // HEAD_DIM, HEAD_DIM))
    shaped = shaped * lax.rsqrt(jnp.mean(shaped * shaped, axis=-1, keepdims=True) + 1e-06)
    return shaped.reshape(values.shape)


def time_embed(steps, width):
    half_width = width // 2
    freqs = jnp.exp(-math.log(10000.0) * jnp.arange(half_width, dtype=F32) / half_width)
    angles = steps.astype(F32)[:, None] * freqs
    return jnp.concatenate([jnp.cos(angles), jnp.sin(angles)], axis=1)


def pick_entry(table, index):
    return jnp.sum(jnp.where(jnp.arange(table.shape[0]) == index, table, 0))


def bf_dot(left, right):
    return jnp.dot(left, right, preferred_element_type=F32)


def left_dot(rows_left, rows_right):
    return lax.dot_general(
        rows_left, rows_right, (((0,), (0,)), ((), ())), preferred_element_type=F32
    )


def right_dot(left, right):
    return lax.dot_general(left, right, (((1,), (1,)), ((), ())), preferred_element_type=F32)


def pre_attn(tokens_in, gain_pre, scale_attn):
    return rms_rows(tokens_in) * gain_pre * (1.0 + scale_attn)


def qk_norm(query_in, key_in, gain_query, gain_key):
    return (head_rms(query_in) * gain_query, head_rms(key_in) * gain_key)


def cap_norm(key_in, gain_cap):
    return head_rms(key_in) * gain_cap


def middle(tokens_in, attn_out, gain_post, gate_attn, gain_ffn, scale_ffn):
    resid_one = tokens_in + jnp.tanh(gate_attn) * rms_rows(attn_out) * gain_post
    return (resid_one, rms_rows(resid_one) * gain_ffn * (1.0 + scale_ffn))


def activate(gate_proj, up_proj):
    return jax.nn.silu(gate_proj) * up_proj


def finish(resid_one, ffn_out, gain_last, gate_ffn):
    return resid_one + jnp.tanh(gate_ffn) * rms_rows(ffn_out) * gain_last


def flip(index, bit):
    return index + bit - 2 * bit * lax.rem(lax.div(index, bit), 2)


class Copies:
    def __init__(self, send, recv):
        self.send, self.recv, self.used = send, recv, 0

    def take(self, count=1):
        first = self.used
        self.used += count
        assert self.used <= self.send.shape[0], self.used
        return first

    def remote(self, src, dst, b, s, at=None):
        at = self.take() if at is None else at
        return pltpu.make_async_remote_copy(
            src_ref=src,
            dst_ref=dst,
            send_sem=self.send.at[at],
            recv_sem=self.recv.at[at],
            device_id={"bucket": b, "seq": s},
            device_id_type=MESH,
        )

    def local(self, src, dst):
        return pltpu.make_async_copy(src, dst, self.send.at[self.take()])


def greet(b, s):
    pl.semaphore_signal(
        pltpu.get_barrier_semaphore(),
        inc=1,
        device_id={"bucket": b, "seq": s},
        device_id_type=MESH,
    )


class Relay:
    def __init__(self, copies, own, out, b, s, seq):
        self.copies, self.own, self.out, self.b, self.s, self.seq = copies, own, out, b, s, seq
        self.base = {1: copies.take(seq - 1), -1: copies.take(seq - 1)}
        self.up = jnp.where(s < seq - 1, s + 1, s - 1)
        self.down = jnp.where(s > 0, s - 1, s + 1)
        self.kept = copies.local(own, out.at[s])

    def packet(self, way, j):
        block = self.out.at[self.s - way * j]
        return self.copies.remote(
            self.own if j == 0 else block,
            block,
            self.b,
            self.up if way > 0 else self.down,
            self.base[way] + j,
        )

    def sends(self, way):
        return self.s < self.seq - 1 if way > 0 else self.s > 0

    def has(self, way, j):
        return self.s >= j if way > 0 else self.s + j <= self.seq - 1

    def start(self, j):
        if j == 0:
            self.kept.start()
        for way in (1, -1):
            if j > 0:

                @pl.when(self.has(way, j))
                def _():
                    self.packet(way, j - 1).wait_recv()

            if j <= self.seq - 2:

                @pl.when(jnp.logical_and(self.sends(way), self.has(way, j)))
                def _():
                    self.packet(way, j).start()

    def sent(self, j):
        for way in (1, -1):

            @pl.when(jnp.logical_and(self.sends(way), self.has(way, j)))
            def _():
                self.packet(way, j).wait_send()

        if j == 0:
            self.kept.wait()


def greet_line(b, s, seq):
    @pl.when(s > 0)
    def _():
        greet(b, s - 1)

    @pl.when(s < seq - 1)
    def _():
        greet(b, s + 1)

    peers = jnp.where(s > 0, 1, 0) + jnp.where(s < seq - 1, 1, 0)
    pl.semaphore_wait(pltpu.get_barrier_semaphore(), peers)


def halves_of(shape):
    if len(shape) == 3:
        return shape[0] // 2
    return (shape[0] // 32) * 16 if shape[0] >= 32 else shape[0] // 2


def gather_kernel(buckets, seq, kinds, *refs):
    count = len(kinds)
    tokens, captions, small, cond, w_mod = refs[:5]
    shards = refs[5 : 5 + count]
    tok_all, cap_all, small_all, mod_out = refs[5 + count : 9 + count]
    fulls = refs[9 + count : 9 + 2 * count]
    part, got_bucket, got_seq, mod_sum, send, recv = refs[9 + 2 * count :]
    b, s = lax.axis_index("bucket"), lax.axis_index("seq")
    copies = Copies(send, recv)
    chips = buckets // 2
    place = b * seq + s
    to_b, to_s = lax.rem(place, buckets), lax.div(place, buckets)
    back = s * buckets + b
    from_b, from_s = lax.div(back, seq), lax.rem(back, seq)
    stays = jnp.logical_and(to_b == b, to_s == s)

    lanes = part.shape[2]
    for j in range(part.shape[1]):
        part[:, j, :] = bf_dot(cond[...], w_mod[:, j * lanes : (j + 1) * lanes])

    for k in range(1, buckets):
        greet(lax.rem(b + k, buckets), s)
    for k in range(1, seq):
        greet(b, lax.rem(s + k, seq))

    @pl.when(jnp.logical_not(stays))
    def _():
        greet(from_b, from_s)

    peers = buckets - 1 + seq - 1 + jnp.where(stays, 0, 1)
    pl.semaphore_wait(pltpu.get_barrier_semaphore(), peers)

    sent = []

    def go(copy):
        copy.start()
        sent.append(copy)
        return copy

    mod_moves = []
    for k in range(1, buckets):
        peer = lax.rem(b + k, buckets)
        mod_moves.append(go(copies.remote(part.at[peer], got_bucket.at[k], peer, s)))
    small_moves = []
    for k in range(1, seq):
        peer = lax.rem(s + k, seq)
        small_moves.append(go(copies.remote(small, small_all.at[b, s], b, peer)))
    small_own = copies.local(small, small_all.at[b, s])
    small_own.start()

    tok = Relay(copies, tokens, tok_all, b, s, seq)
    cap = Relay(copies, captions, cap_all, b, s, seq)
    queue = [(tok, j) for j in range(seq)] + [(cap, j) for j in range(seq)]
    ahead = [(None, at) for at in range(count)]
    items = []
    while queue or ahead:
        items += queue[:1] + ahead[:1]
        queue, ahead = queue[1:], ahead[1:]

    first = [None] * count

    def depart(at):
        kind, shard, full = kinds[at], shards[at], fulls[at]
        if kind == "row":
            move = copies.remote(shard, full.at[to_b], to_b, to_s)
            keep = copies.local(shard, full.at[b])

            @pl.when(jnp.logical_not(stays))
            def _():
                move.start()

            @pl.when(stays)
            def _():
                keep.start()

            first[at] = (move, keep)
            return
        wide = full.shape[-1]

        def columns(peer):
            if kind == "cut":
                return shard.at[peer]
            return shard.at[:, pl.ds(pl.multiple_of(peer * wide, 128), wide)]

        moves = []
        for k in range(1, seq):
            peer = lax.rem(s + k, seq)
            move = copies.remote(columns(peer), full.at[b, s], b, peer)
            move.start()
            moves.append(move)
        keep = copies.local(columns(s), full.at[b, s])
        keep.start()
        first[at] = (moves, keep)

    def arrived(at):
        moves, keep = first[at]
        if kinds[at] == "row":

            @pl.when(jnp.logical_not(stays))
            def _():
                moves.wait()

            @pl.when(stays)
            def _():
                keep.wait()

            return
        for move in moves:
            move.wait()
        keep.wait()

    twin = flip(b, 1)
    second = [None] * count
    if chips == 4:
        near_x, near_y = flip(b, 2), flip(b, 4)
        far = flip(near_x, 4)

        def stage_a(at):
            full = fulls[at]
            second[at] = {
                "x": go(copies.remote(full.at[b], full.at[b], near_x, s)),
                "y": go(copies.remote(full.at[b], full.at[b], near_y, s)),
                "twin": [go(copies.remote(full.at[b], full.at[b], twin, s))],
            }

        def stage_b(at):
            full, now = fulls[at], second[at]
            cut = halves_of(full.shape[1:])
            now["x"].wait_recv()
            block = full.at[near_x, pl.ds(0, cut)]
            now["dy"] = go(copies.remote(block, block, near_y, s))
            block = full.at[near_x]
            now["twin"].append(go(copies.remote(block, block, twin, s)))
            now["y"].wait_recv()
            block = full.at[near_y, pl.ds(cut, full.shape[1] - cut)]
            now["dx"] = go(copies.remote(block, block, near_x, s))
            block = full.at[near_y]
            now["twin"].append(go(copies.remote(block, block, twin, s)))

        def stage_c(at):
            full, now = fulls[at], second[at]
            now["dy"].wait_recv()
            now["dx"].wait_recv()
            block = full.at[far]
            now["twin"].append(go(copies.remote(block, block, twin, s)))

    else:

        def stage_a(at):
            full = fulls[at]
            second[at] = {"far": [], "twin": []}
            for k in range(1, chips):
                peer = lax.rem(b + 2 * k, buckets)
                second[at]["far"].append(go(copies.remote(full.at[b], full.at[b], peer, s)))
            second[at]["twin"].append(go(copies.remote(full.at[b], full.at[b], twin, s)))

        def stage_b(at):
            full = fulls[at]
            for k, copy in enumerate(second[at]["far"], 1):
                copy.wait_recv()
                block = full.at[lax.rem(b + buckets - 2 * k, buckets)]
                second[at]["twin"].append(go(copies.remote(block, block, twin, s)))

        def stage_c(at):
            pass

    def begin(i):
        relay, j = items[i]
        if relay is None:
            depart(j)
        else:
            relay.start(j)

    begin(0)
    begin(1)
    for move in small_moves:
        move.wait_recv()
    small_own.wait()
    small_next = []
    for k in range(1, buckets):
        peer = lax.rem(b + k, buckets)
        small_next.append(go(copies.remote(small_all.at[b], small_all.at[b], peer, s)))
    total = part[b]
    for k, move in enumerate(mod_moves, 1):
        move.wait_recv()
        total = total + got_bucket[k]
    mod_sum[...] = total
    mod_next = []
    for k in range(1, seq):
        peer = lax.rem(s + k, seq)
        mod_next.append(go(copies.remote(mod_sum, got_seq.at[k], b, peer)))

    for i, (relay, j) in enumerate(items):
        if relay is None:
            arrived(j)
        elif j <= seq - 2:
            relay.sent(j)
        if i + 2 < len(items):
            begin(i + 2)
        if relay is None:
            stage_a(j)
            if j >= 1:
                stage_b(j - 1)
            if j >= 2:
                stage_c(j - 2)
    stage_b(count - 1)
    if count >= 2:
        stage_c(count - 2)
    stage_c(count - 1)

    total = mod_sum[...]
    for k, move in enumerate(mod_next, 1):
        move.wait_recv()
        total = total + got_seq[k]
    mod_out[...] = total
    for move in small_next:
        move.wait_recv()
    for now in second:
        for move in now["twin"]:
            move.wait_recv()
    for move in sent:
        move.wait_send()


def gather_all(buckets, seq, tokens, captions, small, cond, w_mod, shards, kinds):
    any_spec = pl.BlockSpec(memory_space=pl.ANY)
    vmem = pl.BlockSpec(memory_space=pltpu.VMEM)
    fulls, inputs, names = [], [], []
    for shard, kind in zip(shards, kinds, strict=True):
        rows, wide = shard.shape
        if kind == "row":
            fulls.append(jax.ShapeDtypeStruct((buckets, rows, wide), BF16))
        else:
            part = wide // seq
            fulls.append(jax.ShapeDtypeStruct((buckets, seq, rows, part), BF16))
            if part % 128:
                kind = "cut"
                shard = shard.reshape(rows, seq, part).transpose(1, 0, 2)
        inputs.append(shard)
        names.append(kind)
    mod_lanes = w_mod.shape[1] // 8
    n_sems = 64 + 16 * buckets + len(shards) * (seq + 2 * buckets)
    outs = pl.pallas_call(
        functools.partial(gather_kernel, buckets, seq, tuple(names)),
        out_shape=[
            jax.ShapeDtypeStruct((seq,) + tokens.shape, BF16),
            jax.ShapeDtypeStruct((seq,) + captions.shape, BF16),
            jax.ShapeDtypeStruct((buckets, seq) + small.shape, F32),
            jax.ShapeDtypeStruct((8, mod_lanes), F32),
            *fulls,
        ],
        in_specs=[any_spec, any_spec, any_spec, vmem, vmem] + [any_spec] * len(shards),
        out_specs=[any_spec, any_spec, any_spec, vmem] + [any_spec] * len(shards),
        scratch_shapes=[
            pltpu.VMEM((buckets, 8, mod_lanes), F32),
            pltpu.VMEM((buckets, 8, mod_lanes), F32),
            pltpu.VMEM((seq, 8, mod_lanes), F32),
            pltpu.VMEM((8, mod_lanes), F32),
            pltpu.SemaphoreType.DMA((n_sems,)),
            pltpu.SemaphoreType.DMA((n_sems,)),
        ],
        compiler_params=pltpu.CompilerParams(
            collective_id=0, has_side_effects=True, vmem_limit_bytes=24 * 2**20
        ),
    )(tokens, captions, small, cond, w_mod, *inputs)
    weights = []
    for full, kind in zip(outs[4:], names, strict=True):
        weights.append(full.reshape(-1, full.shape[-1]))
    return outs[0], outs[1], outs[2], outs[3], weights


def line_gather_kernel(seq, own, out, send, recv):
    b, s = lax.axis_index("bucket"), lax.axis_index("seq")
    greet_line(b, s, seq)
    relay = Relay(Copies(send, recv), own, out, b, s, seq)
    for j in range(seq):
        relay.start(j)
    for j in range(seq - 1):
        relay.sent(j)


def line_gather(seq, own, collective_id):
    return pl.pallas_call(
        functools.partial(line_gather_kernel, seq),
        out_shape=jax.ShapeDtypeStruct((seq,) + own.shape, own.dtype),
        in_specs=[pl.BlockSpec(memory_space=pl.ANY)],
        out_specs=pl.BlockSpec(memory_space=pl.ANY),
        scratch_shapes=[pltpu.SemaphoreType.DMA((2 * seq + 2,))] * 2,
        compiler_params=pltpu.CompilerParams(collective_id=collective_id, has_side_effects=True),
    )(own).reshape(-1, own.shape[-1])


def add_rows(out, terms):
    rows = out.shape[0]
    step = 16 if rows % 16 == 0 else rows

    def body(i, carry):
        at = pl.ds(pl.multiple_of(i * step, step), step)
        total = terms[0][at, :].astype(F32)
        for term in terms[1:]:
            total = total + term[at, :].astype(F32)
        out[at, :] = total.astype(out.dtype)
        return carry

    lax.fori_loop(0, rows // step, body, 0)


def line_scatter_kernel(seq, parts, out, from_left, from_right, send, recv):
    b, s = lax.axis_index("bucket"), lax.axis_index("seq")
    greet_line(b, s, seq)
    copies = Copies(send, recv)
    rows = parts.shape[1]
    cuts = 2 if rows % 32 == 0 else 1
    thin = rows // cuts
    steps = (seq - 1) * cuts
    base_r, base_l = copies.take(steps), copies.take(steps)
    up, down = jnp.where(s < seq - 1, s + 1, s - 1), jnp.where(s > 0, s - 1, s + 1)

    def to_right(q):
        j, at = q // cuts, pl.ds(q % cuts * thin, thin)
        return copies.remote(parts.at[seq - 1 - j, at], from_left.at[j, at], b, up, base_r + q)

    def to_left(q):
        j, at = q // cuts, pl.ds(q % cuts * thin, thin)
        return copies.remote(parts.at[j, at], from_right.at[j, at], b, down, base_l + q)

    def right_on(q):
        return s < seq - 1 - q // cuts

    def left_on(q):
        return s > q // cuts

    def right_step(q):
        j, at = q // cuts, pl.ds(q % cuts * thin, thin)
        block = parts.at[seq - 1 - j, at]

        @pl.when(jnp.logical_and(s > 0, right_on(q)))
        def _():
            to_right(q).wait_recv()
            add_rows(block, [block, from_left.at[j, at]])

        @pl.when(right_on(q))
        def _():
            if q >= 2:
                to_right(q - 2).wait_send()
            to_right(q).start()

    def left_step(q):
        j, at = q // cuts, pl.ds(q % cuts * thin, thin)
        block = parts.at[j, at]

        @pl.when(jnp.logical_and(s < seq - 1, left_on(q)))
        def _():
            to_left(q).wait_recv()
            add_rows(block, [block, from_right.at[j, at]])

        @pl.when(left_on(q))
        def _():
            if q >= 2:
                to_left(q - 2).wait_send()
            to_left(q).start()

    @pl.when(s < seq // 2)
    def _():
        for q in range(steps):
            right_step(q)
            left_step(q)

    @pl.when(s >= seq // 2)
    def _():
        for q in range(steps):
            left_step(q)
            right_step(q)

    for t in range(seq):

        @pl.when(s == t)
        def _():
            terms = [parts.at[t]]
            if t > 0:
                for c in range(cuts):
                    to_right((seq - 1 - t) * cuts + c).wait_recv()
                terms.append(from_left.at[seq - 1 - t])
            if t < seq - 1:
                for c in range(cuts):
                    to_left(t * cuts + c).wait_recv()
                terms.append(from_right.at[t])
            add_rows(out, terms)

    for q in range(steps):
        more = q + 2 < steps

        @pl.when(jnp.logical_and(right_on(q), jnp.logical_not(right_on(q + 2)) if more else True))
        def _():
            to_right(q).wait_send()

        @pl.when(jnp.logical_and(left_on(q), jnp.logical_not(left_on(q + 2)) if more else True))
        def _():
            to_left(q).wait_send()


def line_scatter(seq, parts, collective_id):
    rows, wide = parts.shape[0] // seq, parts.shape[1]
    vmem = pl.BlockSpec(memory_space=pltpu.VMEM)
    return pl.pallas_call(
        functools.partial(line_scatter_kernel, seq),
        out_shape=jax.ShapeDtypeStruct((rows, wide), F32),
        in_specs=[vmem],
        out_specs=vmem,
        input_output_aliases={},
        scratch_shapes=[
            pltpu.VMEM((seq - 1, rows, wide), BF16),
            pltpu.VMEM((seq - 1, rows, wide), BF16),
            pltpu.SemaphoreType.DMA((4 * seq,)),
            pltpu.SemaphoreType.DMA((4 * seq,)),
        ],
        compiler_params=pltpu.CompilerParams(
            collective_id=collective_id, has_side_effects=True, vmem_limit_bytes=24 * 2**20
        ),
    )(parts.astype(BF16).reshape(seq, rows, wide))


def scatter_kernel(buckets, seq, kinds, *refs):
    count = len(kinds)
    vec, grads = refs[0], refs[1 : 1 + count]
    vec_all, outs = refs[1 + count], refs[2 + count : 2 + 2 * count]
    at = 2 + 2 * count
    vec_seq, vec_sum, send, recv = refs[at : at + 4]
    scratch = refs[at + 4 :]
    b, s = lax.axis_index("bucket"), lax.axis_index("seq")
    copies = Copies(send, recv)
    chips = buckets // 2
    chip, core = lax.div(b, 2), lax.rem(b, 2)
    place = s * buckets + b
    to_b = lax.div(place, seq)
    twin = flip(b, 1)
    sent = []

    def go(copy):
        copy.start()
        sent.append(copy)
        return copy

    for k in range(1, buckets):
        greet(lax.rem(b + k, buckets), s)
    for k in range(1, seq):
        greet(b, lax.rem(s + k, seq))
    for j in range(seq):
        d = b * seq + j
        src_b, src_s = lax.rem(d, buckets), lax.div(d, buckets)

        @pl.when(jnp.logical_not(jnp.logical_and(src_b == b, src_s == s)))
        def _():
            greet(src_b, src_s)

    peers = buckets - 1 + seq - 1 + seq - jnp.where(to_b == b, 1, 0)
    pl.semaphore_wait(pltpu.get_barrier_semaphore(), peers)

    vec_moves = []
    for k in range(1, seq):
        vec_moves.append(go(copies.remote(vec, vec_seq.at[k], b, lax.rem(s + k, seq))))

    begun = []

    def begin(w):
        own, other = scratch[6 * w], scratch[6 * w + 1]
        swap = copies.remote(grads[w].at[:, 1 - core], other, twin, s)
        keep = copies.local(grads[w].at[:, core], own)
        swap.start()
        keep.start()
        begun.append((swap, keep))

    begin(0)
    if count > 1:
        begin(1)

    for move in vec_moves:
        move.wait_recv()
    add_rows(vec_sum, [vec] + [vec_seq.at[k] for k in range(1, seq)])
    vec_next = []
    for k in range(1, buckets):
        peer = lax.rem(b + k, buckets)
        vec_next.append(go(copies.remote(vec_sum, vec_all.at[b], peer, s)))
    vec_own = copies.local(vec_sum, vec_all.at[b])
    vec_own.start()

    state = [None] * count
    if chips == 4:
        mx, my = flip(chip, 1), flip(chip, 2)
        far = flip(mx, 2)
        near_x, near_y = flip(b, 2), flip(b, 4)

        def stage_a(w):
            own, other, half_x, half_y, _, _ = scratch[6 * w : 6 * w + 6]
            swap, keep = begun[w]
            swap.wait()
            keep.wait()
            if w + 2 < count:
                begin(w + 2)
            add_rows(own.at[far], [own.at[far], other.at[far]])
            rows = own.shape[1]
            cut = halves_of(own.shape[1:])
            state[w] = [
                go(copies.remote(own.at[far, pl.ds(0, cut)], half_x, near_x, s)),
                go(copies.remote(own.at[far, pl.ds(cut, rows - cut)], half_y, near_y, s)),
            ]

        def stage_b(w):
            own, other, half_x, half_y, got_x, got_y = scratch[6 * w : 6 * w + 6]
            rows = own.shape[1]
            cut = halves_of(own.shape[1:])
            top, low = pl.ds(0, cut), pl.ds(cut, rows - cut)
            move_x, move_y = state[w]
            move_x.wait_recv()
            add_rows(own.at[my, top], [own.at[my, top], other.at[my, top], half_x])
            add_rows(own.at[my, low], [own.at[my, low], other.at[my, low]])
            next_y = go(copies.remote(own.at[my], got_y, near_y, s))
            move_y.wait_recv()
            add_rows(own.at[mx, low], [own.at[mx, low], other.at[mx, low], half_y])
            add_rows(own.at[mx, top], [own.at[mx, top], other.at[mx, top]])
            next_x = go(copies.remote(own.at[mx], got_x, near_x, s))
            state[w] = [next_x, next_y]

        def terms_of(w):
            own, other, _, _, got_x, got_y = scratch[6 * w : 6 * w + 6]
            return [own.at[chip], other.at[chip], got_x, got_y]

    else:

        def stage_a(w):
            own, other, got = scratch[6 * w], scratch[6 * w + 1], scratch[6 * w + 4]
            swap, keep = begun[w]
            swap.wait()
            keep.wait()
            if w + 2 < count:
                begin(w + 2)
            state[w] = []
            for k in range(1, chips):
                to = lax.rem(chip + k, chips)
                add_rows(own.at[to], [own.at[to], other.at[to]])
                state[w].append(go(copies.remote(own.at[to], got.at[k], 2 * to + core, s)))

        def stage_b(w):
            pass

        def terms_of(w):
            own, other, got = scratch[6 * w], scratch[6 * w + 1], scratch[6 * w + 4]
            return [own.at[chip], other.at[chip]] + [got.at[k] for k in range(1, chips)]

    last = [None] * count

    def stage_c(w):
        for move in state[w]:
            move.wait_recv()
        add_rows(outs[w], terms_of(w))

    row_base = {w: copies.take(2 * seq) for w in range(count) if kinds[w] == "row"}

    def stage_c_row(w):
        for move in state[w]:
            move.wait_recv()
        out, terms = outs[w], terms_of(w)
        done, landed = scratch[6 * count + 2 * w], scratch[6 * count + 2 * w + 1]
        wide = out.shape[-1]
        me = lax.rem(place, seq)
        base = row_base[w]
        rows = terms[0].shape[0]
        step = 16 if rows % 16 == 0 else rows

        def body(i, carry):
            at = pl.ds(pl.multiple_of(i * step, step), step)
            total = terms[0][at, :].astype(F32)
            for term in terms[1:]:
                total = total + term[at, :].astype(F32)
            for t in range(seq):
                done[t, at, :] = total[:, t * wide : (t + 1) * wide].astype(BF16)
            return carry

        lax.fori_loop(0, rows // step, body, 0)
        moves = []
        for t in range(seq):
            move = pltpu.make_async_remote_copy(
                src_ref=done.at[t],
                dst_ref=landed.at[me],
                send_sem=send.at[base + t],
                recv_sem=recv.at[base + me],
                device_id={"bucket": to_b, "seq": t},
                device_id_type=MESH,
            )
            keep = pltpu.make_async_copy(done.at[t], landed.at[me], send.at[base + seq + t])
            here = jnp.logical_and(to_b == b, s == t)

            @pl.when(jnp.logical_not(here))
            def _():
                move.start()

            @pl.when(here)
            def _():
                keep.start()

            moves.append((move, keep, here))
        last[w] = moves

    def stage_d(w):
        if kinds[w] != "row":
            return
        out = outs[w]
        done, landed = scratch[6 * count + 2 * w], scratch[6 * count + 2 * w + 1]
        base = row_base[w]
        for j in range(seq):
            d = b * seq + j
            here = jnp.logical_and(lax.rem(d, buckets) == b, lax.div(d, buckets) == s)

            @pl.when(jnp.logical_not(here))
            def _():
                pltpu.make_async_remote_copy(
                    src_ref=done.at[j],
                    dst_ref=landed.at[j],
                    send_sem=send.at[base + j],
                    recv_sem=recv.at[base + j],
                    device_id={"bucket": twin, "seq": s},
                    device_id_type=MESH,
                ).wait_recv()

        for move, keep, here in last[w]:

            @pl.when(jnp.logical_not(here))
            def _():
                move.wait_send()

            @pl.when(here)
            def _():
                keep.wait()

        for j in range(seq):
            add_rows(out.at[j], [landed.at[j]])

    for w in range(count + 2):
        if w < count:
            stage_a(w)
        if 1 <= w <= count:
            stage_b(w - 1)
        if w >= 2:
            if kinds[w - 2] == "row":
                stage_c_row(w - 2)
            else:
                stage_c(w - 2)
    for w in range(count):
        stage_d(w)
    for move in vec_next:
        move.wait_recv()
    vec_own.wait()
    for move in sent:
        move.wait_send()


def scatter_all(buckets, seq, vec, grads, kinds):
    chips = buckets // 2
    any_spec = pl.BlockSpec(memory_space=pl.ANY)
    vmem = pl.BlockSpec(memory_space=pltpu.VMEM)
    inputs, outs, scratch, tail = [], [], [], []
    for grad, kind in zip(grads, kinds, strict=True):
        rows, wide = grad.shape[0] // buckets, grad.shape[1]
        inputs.append(grad.astype(BF16).reshape(chips, 2, rows, wide))
        cut = halves_of((rows, wide))
        scratch += [
            pltpu.VMEM((chips, rows, wide), BF16),
            pltpu.VMEM((chips, rows, wide), BF16),
            pltpu.VMEM((cut, wide), BF16),
            pltpu.VMEM((rows - cut, wide), BF16),
            pltpu.VMEM((rows, wide) if chips == 4 else (chips, rows, wide), BF16),
            pltpu.VMEM((rows, wide) if chips == 4 else (16, 128), BF16),
        ]
        if kind == "row":
            shape = (seq, rows, wide // seq)
            outs.append(jax.ShapeDtypeStruct(shape, F32))
            tail += [pltpu.VMEM(shape, BF16)] * 2
        else:
            outs.append(jax.ShapeDtypeStruct((rows, wide), F32))
            tail += [pltpu.VMEM((16, 128), BF16)] * 2
    n_sems = 32 + 2 * buckets + len(grads) * (8 + 3 * seq + buckets)
    results = pl.pallas_call(
        functools.partial(scatter_kernel, buckets, seq, tuple(kinds)),
        out_shape=[jax.ShapeDtypeStruct((buckets,) + vec.shape, F32), *outs],
        in_specs=[vmem] + [any_spec] * len(grads),
        out_specs=[any_spec] + [vmem] * len(grads),
        scratch_shapes=[
            pltpu.VMEM((seq,) + vec.shape, F32),
            pltpu.VMEM(vec.shape, F32),
            pltpu.SemaphoreType.DMA((n_sems,)),
            pltpu.SemaphoreType.DMA((n_sems,)),
            *scratch,
            *tail,
        ],
        compiler_params=pltpu.CompilerParams(
            collective_id=1, has_side_effects=True, vmem_limit_bytes=60 * 2**20
        ),
    )(vec, *inputs)
    return results[0], [out.reshape(-1, out.shape[-1]) for out in results[1:]]


def attention(queries, keys, values, live, scale):
    scores = jnp.einsum("qhd,khd->hqk", queries, keys, preferred_element_type=F32) * scale
    scores = jnp.where(live[None, None, :], scores, -1e30)
    probs = jax.nn.softmax(scores, axis=-1)
    mixed = jnp.einsum("hqk,khd->qhd", probs.astype(BF16), values, preferred_element_type=F32)
    return probs, mixed


def attention_back(probs, queries, keys, values, d_out, scale):
    d_probs = jnp.einsum("qhd,khd->hqk", d_out, values, preferred_element_type=F32)
    d_scores = probs * (d_probs - jnp.sum(probs * d_probs, axis=-1, keepdims=True))
    d_low = d_scores.astype(BF16)
    d_query = jnp.einsum("hqk,khd->qhd", d_low, keys, preferred_element_type=F32) * scale
    d_key = jnp.einsum("hqk,qhd->khd", d_low, queries, preferred_element_type=F32) * scale
    d_value = jnp.einsum("hqk,qhd->khd", probs.astype(BF16), d_out, preferred_element_type=F32)
    return d_query, d_key, d_value


def on_device(
    tokens,
    captions,
    cotangent,
    counts,
    cap_lens,
    steps_t,
    w_query,
    w_key,
    w_value,
    w_out,
    w_cap_key,
    w_cap_value,
    w_gate,
    w_up,
    w_down,
    w_mod,
    gains,
    cross_gate,
):
    buckets, seq = lax.axis_size("bucket"), lax.axis_size("seq")
    b, s = lax.axis_index("bucket"), lax.axis_index("seq")
    place = b * seq + s
    rows, width = tokens.shape
    span = rows * seq
    share = width // seq
    heads = share // HEAD_DIM
    scale = HEAD_DIM ** (-0.5)
    live_rows, cap_len = pick_entry(counts, b), pick_entry(cap_lens, b)
    token_total = jnp.sum(counts).astype(F32)

    cond_size = w_mod.shape[0] * buckets * seq
    cond = jax.nn.silu(time_embed(steps_t, cond_size)).astype(BF16)
    cond_part = lax.dynamic_slice_in_dim(cond, place * w_mod.shape[0], w_mod.shape[0], 1)
    slim = gains.shape[1]
    small = jnp.concatenate([gains, cross_gate[None]], axis=0).astype(F32)
    small = jnp.pad(small, ((0, 0), (0, 128 - slim)))
    tok_all, cap_all, small_all, mod, weights = gather_all(
        buckets,
        seq,
        tokens,
        captions,
        small,
        cond_part,
        w_mod,
        [w_query, w_key, w_value, w_cap_key, w_cap_value, w_out, w_gate, w_up, w_down],
        ["col", "col", "col", "col", "col", "row", "col", "col", "row"],
    )
    wq, wk, wv, wck, wcv, wo, wg, wu, wd = weights
    caps = cap_all.reshape(-1, captions.shape[1])
    small_rows = small_all[..., :slim].transpose(2, 0, 1, 3).reshape(8, width)
    gain_f = small_rows[:7]
    own_cols = lax.dynamic_slice_in_dim(small_rows, s * share, share, 1)
    gate_cross = jnp.tanh(own_cols[7])
    scale_attn, gate_attn, scale_ffn, gate_ffn = mod.reshape(4, width)

    hidden = pre_attn(tok_all.astype(F32), gain_f[0], scale_attn).astype(BF16).reshape(span, width)
    query_proj, key_proj = bf_dot(hidden, wq), bf_dot(hidden, wk)
    value_low = bf_dot(hidden, wv).astype(BF16)
    (query_f, key_f), norm_back = jax.vjp(qk_norm, query_proj, key_proj, own_cols[4], own_cols[5])
    cap_key_f, cap_back = jax.vjp(cap_norm, bf_dot(caps, wck), own_cols[6])

    def by_head(values):
        return values.astype(BF16).reshape(values.shape[0], heads, HEAD_DIM)

    query, key, value = by_head(query_f), by_head(key_f), by_head(value_low)
    cap_key, cap_value = by_head(cap_key_f), by_head(bf_dot(caps, wcv))
    probs, self_out = attention(query, key, value, jnp.arange(span) < live_rows, scale)
    cap_live = jnp.arange(caps.shape[0]) < cap_len
    cap_probs, cross_out = attention(query, cap_key, cap_value, cap_live, scale)
    self_out, cross_out = self_out.reshape(span, share), cross_out.reshape(span, share)
    mixed_low = (self_out + gate_cross * cross_out).astype(BF16)
    attn_out = line_scatter(seq, bf_dot(mixed_low, wo), 2)

    tokens_f = tokens.astype(F32)
    (resid_one, ffn_pre), middle_back = jax.vjp(
        middle, tokens_f, attn_out, gain_f[1], gate_attn, gain_f[2], scale_ffn
    )
    ffn_all = line_gather(seq, ffn_pre.astype(BF16), 3)
    act_pre, act_back = jax.vjp(activate, bf_dot(ffn_all, wg), bf_dot(ffn_all, wu))
    act_low = act_pre.astype(BF16)
    ffn_out = line_scatter(seq, bf_dot(act_low, wd), 4)
    out_f, finish_back = jax.vjp(finish, resid_one, ffn_out, gain_f[3], gate_ffn)
    block_out = out_f.astype(BF16)

    row_live = (s * rows + jnp.arange(rows) < live_rows).astype(F32)
    weighted = cotangent.astype(F32) * row_live[:, None] * (buckets * span / token_total)
    d_resid, d_ffn_out, d_gain_last, d_gate_ffn = finish_back(weighted)
    d_ffn_all = line_gather(seq, d_ffn_out.astype(BF16), 5)
    d_gate, d_up = act_back(right_dot(d_ffn_all, wd))
    d_gate, d_up = d_gate.astype(BF16), d_up.astype(BF16)
    d_hidden_ffn = line_scatter(seq, right_dot(d_gate, wg) + right_dot(d_up, wu), 6)
    d_tokens_one, d_attn_out, d_gain_post, d_gate_attn, d_gain_ffn, d_scale_ffn = middle_back(
        (d_resid, d_hidden_ffn)
    )
    d_attn_all = line_gather(seq, d_attn_out.astype(BF16), 7)
    d_mixed_low = right_dot(d_attn_all, wo).astype(BF16)
    d_mixed = d_mixed_low.astype(F32)
    d_cross_low = (gate_cross * d_mixed).astype(BF16)
    grad_cross = jnp.sum(d_mixed * cross_out, axis=0) * (1.0 - gate_cross * gate_cross)

    d_query_cross, d_cap_key, d_cap_value = attention_back(
        cap_probs, query, cap_key, cap_value, by_head(d_cross_low), scale
    )
    d_query, d_key, d_value = attention_back(probs, query, key, value, by_head(d_mixed_low), scale)
    d_cap_key, d_gain_cap = cap_back(d_cap_key.reshape(-1, share))
    d_query, d_key, d_gain_query, d_gain_key = norm_back(
        ((d_query + d_query_cross).reshape(span, share), d_key.reshape(span, share))
    )
    d_query, d_key, d_cap_key = d_query.astype(BF16), d_key.astype(BF16), d_cap_key.astype(BF16)
    d_value = d_value.reshape(span, share).astype(BF16)
    d_cap_value = d_cap_value.reshape(-1, share).astype(BF16)
    d_hidden = line_scatter(
        seq, right_dot(d_query, wq) + right_dot(d_key, wk) + right_dot(d_value, wv), 8
    )
    _, pre_back = jax.vjp(pre_attn, tokens_f, gain_f[0], scale_attn)
    d_tokens_two, d_gain_pre, d_scale_attn = pre_back(d_hidden)
    tokens_grad = d_tokens_one + d_tokens_two

    own_sums = jnp.stack([d_gain_query, d_gain_key, d_gain_cap, grad_cross])
    own_wide = lax.dynamic_update_slice(jnp.zeros((4, width), F32), own_sums, (0, s * share))
    vec = jnp.concatenate(
        [
            jnp.stack([d_scale_attn, d_gate_attn, d_scale_ffn, d_gate_ffn]),
            jnp.stack([d_gain_pre, d_gain_post, d_gain_ffn, d_gain_last]),
            own_wide,
            jnp.zeros((4, width), F32),
        ]
    )
    grads = [
        left_dot(ffn_all, d_gate),
        left_dot(ffn_all, d_up),
        left_dot(act_low, d_ffn_all),
        left_dot(mixed_low, d_attn_all),
        left_dot(caps, d_cap_key),
        left_dot(caps, d_cap_value),
        left_dot(hidden, d_query),
        left_dot(hidden, d_key),
        left_dot(hidden, d_value),
    ]
    kinds = ["col", "col", "row", "row", "col", "col", "col", "col", "col"]
    vec_all, sums = scatter_all(buckets, seq, vec, grads, kinds)
    s_gate, s_up, s_down, s_out, s_cap_key, s_cap_value, s_query, s_key, s_value = sums

    quarter = 4 * width // seq
    mod_rows = vec_all[:, :4].reshape(buckets, -1, quarter)
    mod_rows = lax.dynamic_slice_in_dim(mod_rows, s, 1, 1)[:, 0]
    cond_size = cond.shape[1] // buckets
    cond_cols = lax.dynamic_slice_in_dim(cond, b * cond_size, cond_size, 1).astype(F32)
    s_mod = jnp.sum(cond_cols[:, :, None] * mod_rows[:, None, :], axis=0)
    tail = lax.dynamic_slice(vec_all, (0, 4, place * slim), (buckets, 8, slim))
    tail = jnp.sum(tail, axis=0)
    return (
        block_out,
        tokens_grad,
        s_query,
        s_key,
        s_value,
        s_out,
        s_cap_key,
        s_cap_value,
        s_gate,
        s_up,
        s_down,
        s_mod,
        tail[:7],
        tail[7],
    )


def solution(mesh):
    spread = P(("bucket", "seq"), None)
    in_specs = (
        *([spread] * 3),
        *([P()] * 3),
        *([spread] * 10),
        P(None, ("bucket", "seq")),
        P(("bucket", "seq")),
    )
    out_specs = (
        spread,
        spread,
        *([P("bucket", "seq")] * 10),
        P(None, ("bucket", "seq")),
        P(("bucket", "seq")),
    )
    return jax.shard_map(
        on_device, mesh=mesh, in_specs=in_specs, out_specs=out_specs, check_vma=False
    )
```

time: 1820 us -> 689 us (0.38)
  waiting for transfers between devices: 1010 us -> 0 us
  Pallas kernels: 0 us -> 488 us
  blocking collectives: 384 us -> 0 us
  matrix products: 177 us -> 91.9 us
  starting transfers between devices: 60.8 us -> 0 us
  local copies, waits for them, and re-layouts: 103 us -> 65.1 us
    all_gather x15 -> x0, waiting for transfers between devices: 562 us -> none  [the longest x1 92.4 us: on_device(): lax.all_gather(w_gate, ('bucket', 'seq'), axis=0, tiled=True)]
    pallas_call x0 -> x9, Pallas kernels: none -> 488 us  [the longest x1 167 us: gather_all(): pl.pallas_call(functools.partial(gather_kernel, buckets, seq, tuple(names...]
    reduce_scatter x12 -> x0, waiting for transfers between devices: 403 us -> none  [the longest x1 48.4 us: on_device(): lax.psum_scatter(grad_mod.astype(jnp.bfloat16), 'bucket', scatter_dimensi...]
    all_to_all x7 -> x0, blocking collectives: 163 us -> none  [the longest x1 50.5 us: on_device(): lax.all_to_all(split_cols(d_gate_low), 'seq', split_axis=1, concat_axis=0...]
    all_gather x3 -> x0, blocking collectives: 138 us -> none  [the longest x1 65.8 us: on_device(): lax.all_gather(gains, ('bucket', 'seq'), axis=1, tiled=True)]
    unnamed x3 -> x0, blocking collectives: 82.9 us -> none
    dot_general x28 -> x26, matrix products: 135 us -> 55.8 us  [the longest x9 22.9 us: bf_dot(): return jnp.dot(left, right, preferred_element_type=F32)]
    all_to_all x10 -> x0, starting transfers between devices: 59.3 us -> none  [the longest x1 7.81 us: on_device(): lax.all_to_all(d_key_heads.reshape(span, 1, head_part, HEAD_DIM).astype(j...]
  transfers between devices with their start and end apart: 38 -> 0, of which waited for: 23 -> 0; matrix products, arithmetic and copies ran while one was open for 15% -> 0% of each run, Pallas kernels for 0% -> 0%
where the time goes in v1:
time: 689 us; the launch traced here: 682 us
  Pallas kernels  488 us (71%)
  matrix products  91.9 us (13%)
  local copies, waits for them, and re-layouts  65.1 us (9%)
  other arithmetic  34.3 us (5%)
    pallas_call x1, Pallas kernels, gather_all(): pl.pallas_call(functools.partial(gather_kernel, buckets, seq, tuple(names...  167 us
    pallas_call x4, Pallas kernels, line_scatter(): pl.pallas_call(functools.partial(line_scatter_kernel, seq), out_shape=jax...  125 us
    pallas_call x1, Pallas kernels, scatter_all(): pl.pallas_call(functools.partial(scatter_kernel, buckets, seq, tuple(kind...  118 us
    pallas_call x3, Pallas kernels, line_gather(): pl.pallas_call(functools.partial(line_gather_kernel, seq), out_shape=jax....  78.8 us
    unnamed x272, local copies, waits for them, and re-layouts  44.9 us
    dot_general x9, matrix products, left_dot(): lax.dot_general(rows_left, rows_right, (((0,), (0,)), ((), ())), preferre...  26.5 us
    dot_general x9, matrix products, bf_dot(): return jnp.dot(left, right, preferred_element_type=F32)  22.9 us
    dot_general x7, matrix products, right_dot(): lax.dot_general(left, right, (((1,), (1,)), ((), ())), preferred_element_...  16.5 us

profile of v1, /device:TPU:8, one launch (start us, length us, event | category | flops | bytes accessed | tf_op | source)
XLA Modules:
  0.0 682.0 jit_solution(597057508499937334)
XLA Ops:
  14.5 166.5 %shard_map.281 = (bf16[4,128,1536]{2,1,0:T(8,128)(2,1)S(1)}, bf16[4,64,4096]{2,1,0:T(8,128)(2,1)S(1)}, f32[8,4,8,128]{3,2,1,0:T(8,128)S(1)}, f32[8,768]{1,0:T(8,...) custom-call(bf16[128,1536]{1,0:T(8,128)(2,1)S(1)} %copy-done.3, ...), custom_call_target="tpu_custom_call" | custom-call | tf_op jit(solution)/shard_map/pallas_call | solution.py:426
  181.1 1.1 copy-done.1
  183.3 1.6 copy-done.10
  187.0 1.7 copy-done.27
  188.6 1.6 copy-done.30
  190.3 1.6 copy-done.32
  191.9 1.7 copy-done.34
  195.3 1.9 fusion.3
  197.8 1.6 convolution_convert_fusion.12
  200.4 2.0 convolution_convert_fusion.14
  202.4 1.7 copy.63
  204.8 1.2 iota_compare_fusion.2
  205.9 1.7 copy.61
  207.7 3.5 multiply_reduce_fusion.15
  213.7 1.6 copy.59
  215.2 2.6 multiply_reduce_fusion.16
  218.8 5.0 copy.64
  223.8 2.9 multiply_reduce_fusion.17
  227.3 4.6 fusion.85
  231.9 3.2 fusion.57
  235.8 5.0 fusion.86
  240.8 3.9 fusion.30
  245.8 41.3 %shard_map.282 = f32[128,1536]{1,0:T(8,128)S(1)} custom-call(bf16[4,128,1536]{2,1,0:T(8,128)(2,1)S(1)} %bitcast.194), custom_call_target="tpu_custom_call" | custom-call | tf_op jit(solution)/shard_map/pallas_call | solution.py:588
  287.9 2.4 multiply_reduce_fusion.13
  292.2 2.0 multiply_convert_fusion.4.own
  294.3 28.6 %shard_map.283 = bf16[4,128,1536]{2,1,0:T(8,128)(2,1)} custom-call(bf16[128,1536]{1,0:T(8,128)(2,1)} %multiply_convert_fusion.4.own), custom_call_target="tpu_custom_call" | custom-call | tf_op jit(solution)/shard_map/pallas_call | solution.py:466
  322.9 4.3 fusion.87
  327.2 3.2 multiply_convert_fusion.3
  330.4 1.8 convolution_convert_fusion.5
  332.2 28.6 %shard_map.284 = f32[128,1536]{1,0:T(8,128)S(1)} custom-call(bf16[4,128,1536]{2,1,0:T(8,128)(2,1)S(1)} %bitcast.202), custom_call_target="tpu_custom_call" | custom-call | tf_op jit(solution)/shard_map/pallas_call | solution.py:588
  362.4 1.1 compare_convert_fusion
  363.6 1.3 multiply_reduce_fusion.12
  365.8 1.3 tanh.43
  367.1 1.4 mul.791
  368.5 2.3 multiply_reduce_fusion.3
  371.5 2.9 fusion.43
  374.4 24.5 %shard_map.285 = bf16[4,128,1536]{2,1,0:T(8,128)(2,1)} custom-call(bf16[128,1536]{1,0:T(8,128)(2,1)} %get-tuple-element.93.own), custom_call_target="tpu_custom_call" | custom-call | tf_op jit(solution)/shard_map/pallas_call | solution.py:466
  399.0 6.2 multiply_convert_fusion.2
  405.2 1.8 fusion.88
  407.8 1.8 fusion.10
  409.7 27.7 %shard_map.286 = f32[128,1536]{1,0:T(8,128)S(1)} custom-call(bf16[4,128,1536]{2,1,0:T(8,128)(2,1)S(1)} %bitcast.201), custom_call_target="tpu_custom_call" | custom-call | tf_op jit(solution)/shard_map/pallas_call | solution.py:588
  438.5 1.4 multiply_reduce_fusion.5
  441.8 25.7 %shard_map.287 = bf16[4,128,1536]{2,1,0:T(8,128)(2,1)} custom-call(bf16[128,1536]{1,0:T(8,128)(2,1)} %fusion.44.own), custom_call_target="tpu_custom_call" | custom-call | tf_op jit(solution)/shard_map/pallas_call | solution.py:466
  467.5 3.6 fusion.42
  471.1 4.0 multiply_reduce_fusion.1
  475.9 1.8 multiply_convert_fusion
  478.4 1.2 copy-done.48
  484.1 1.2 fusion.50
  490.4 27.0 %shard_map.288 = f32[128,1536]{1,0:T(8,128)S(1)} custom-call(bf16[4,128,1536]{2,1,0:T(8,128)(2,1)S(1)} %bitcast.195), custom_call_target="tpu_custom_call" | custom-call | tf_op jit(solution)/shard_map/pallas_call | solution.py:588
  518.0 1.1 fusion.47
  521.1 1.3 concatenate.11.refs_0_
  522.5 5.3 convolution_convert_fusion.4
  527.8 3.5 convolution_convert_fusion.3
  531.3 3.5 convolution_convert_fusion.2
  534.9 1.8 convolution_convert_fusion.10
  536.9 2.9 convolution_convert_fusion.1
  540.4 3.0 convolution_convert_fusion
  543.5 2.0 convolution_convert_fusion.9
  545.5 2.1 convolution_convert_fusion.8
  547.6 2.3 convolution_convert_fusion.7
  549.8 117.6 %shard_map.289 = (f32[8,16,1536]{2,1,0:T(8,128)}, f32[192,1024]{1,0:T(8,128)}, f32[192,1024]{1,0:T(8,128)}, f32[4,128,384]{2,1,0:T(8,128)}, f32[4,48,384]{2,1,0:...) custom-call(f32[16,1536]{1,0:T(8,128)} %concatenate.11.refs_0_, ...), custom_call_target="tpu_custom_call" | custom-call | tf_op jit(solution)/shard_map/pallas_call | solution.py:865
  669.3 1.4 multiply_reduce_fusion
  672.2 1.7 copy.95
  673.9 1.8 copy.96
  (347 shorter events, 58.8 us)
Async XLA Ops:
  193.6 12.4 %copy-start.5 = (bf16[8,4,48,384]{3,2,1,0:T(8,128)(2,1)}, bf16[8,4,48,384]{3,2,1,0:T(8,128)(2,1)S(1)}, u32[]{:S(2)}) copy-start(bf16[8,4,48,384]{3,2,1,0:T(8,128)(2,1)S(1)} %get-tuple-element.42) | copy-start | bytes 3538948
  195.3 2.5 copy-start.14
  197.8 2.6 copy-start.35
  200.4 3.7 copy-start.108
  200.4 3.7 copy-start.109
  207.7 6.0 copy-start.8
  211.2 6.7 copy-start.75
  213.1 22.0 %copy-start.101 = (f32[384]{0:T(512)}, f32[384]{0:T(512)S(1)}, u32[]{:S(2)}) copy-start(f32[384]{0:T(512)S(1)} %get-tuple-element.83) | copy-start | bytes 4612
  213.6 4.3 copy-start.81
  213.7 4.3 copy-start.83
  215.2 2.7 copy-start.39
  217.9 5.9 copy-start.77
  218.8 17.1 %copy-start.44 = (bf16[512,6,64]{0,2,1:T(8,128)(2,1)}, bf16[512,6,64]{0,2,1:T(8,128)(2,1)S(1)}, u32[]{:S(2)}) copy-start(bf16[512,6,64]{0,2,1:T(8,128)(2,1)S(1)} %get-tuple-element.128) | copy-start | bytes 1179652
  218.8 17.1 %copy-start.50 = (bf16[512,6,64]{0,2,1:T(8,128)(2,1)}, bf16[512,6,64]{0,2,1:T(8,128)(2,1)S(1)}, u32[]{:S(2)}) copy-start(bf16[512,6,64]{0,2,1:T(8,128)(2,1)S(1)} %get-tuple-element.127) | copy-start | bytes 1179652
  226.7 5.2 copy-start.46
  226.8 5.1 copy-start.79
  227.3 4.6 copy-start.72
  227.3 4.6 copy-start.71
  240.8 3.9 copy-start.99
  240.8 3.9 copy-start.12
  245.8 42.1 %copy-start.94 = (f32[2,768]{1,0:T(2,128)S(1)}, f32[2,768]{1,0:T(2,128)}, u32[]{:S(2)}) copy-start(f32[2,768]{1,0:T(2,128)} %get-tuple-element.103) | copy-start | bytes 18436
  245.8 42.1 %copy-start.4 = (bf16[128,1536]{1,0:T(8,128)(2,1)S(1)}, bf16[128,1536]{1,0:T(8,128)(2,1)}, u32[]{:S(2)}) copy-start(bf16[128,1536]{1,0:T(8,128)(2,1)} %refs_0_.1) | copy-start | bytes 1179652
  322.8 4.3 copy-start.28
  322.9 4.3 copy-start.54
  327.2 3.2 copy-start.120
  327.2 3.2 copy-start.33
  399.0 6.2 copy-start.31
  405.2 2.6 copy-start.29
  409.6 27.8 %copy-start.36 = (f32[128,1536]{1,0:T(8,128)S(1)}, f32[128,1536]{1,0:T(8,128)}, u32[]{:S(2)}) copy-start(f32[128,1536]{1,0:T(8,128)} %get-tuple-element.90) | copy-start | bytes 2359300
  409.6 27.8 %copy-start.104 = (f32[128]{0:T(128)S(1)}, f32[128]{0:T(128)}, u32[]{:S(2)}) copy-start(f32[128]{0:T(128)} %copy-done.103) | copy-start | bytes 1540
  409.6 28.8 %copy-start.114 = (f32[128]{0:T(128)S(1)}, f32[128]{0:T(128)}, u32[]{:S(2)}) copy-start(f32[128]{0:T(128)} %get-tuple-element.89) | copy-start | bytes 1540
  409.7 28.9 %copy-start.43 = (bf16[128,1536]{1,0:T(8,128)(2,1)S(1)}, bf16[128,1536]{1,0:T(8,128)(2,1)}, u32[]{:S(2)}) copy-start(bf16[128,1536]{1,0:T(8,128)(2,1)} %param.20) | copy-start | bytes 1179652
  409.7 28.8 %copy-start.105 = (f32[128]{0:T(128)S(1)}, f32[128]{0:T(128)}, u32[]{:S(2)}) copy-start(f32[128]{0:T(128)} %compare_convert_fusion) | copy-start | bytes 1540
  409.7 28.8 %copy-start.106 = (f32[128]{0:T(128)S(1)}, f32[128]{0:T(128)}, u32[]{:S(2)}) copy-start(f32[128]{0:T(128)} %fusion.75) | copy-start | bytes 1540
  437.4 2.5 copy-start.84
  437.4 2.5 copy-start.111
  440.0 27.5 %copy-start.102 = (f32[384]{0:T(512)S(1)}, f32[384]{0:T(512)}, u32[]{:S(2)}) copy-start(f32[384]{0:T(512)} %copy-done.101) | copy-start | bytes 4612
  467.5 3.6 copy-start.100
  467.5 3.6 copy-start.115
  471.1 4.0 copy-start.118
  471.1 4.1 slice-start
  471.1 4.8 slice-start.1
  482.9 2.4 copy-start.76
  484.1 3.2 slice-start.2
  490.4 27.1 %copy-start.113 = (f32[128]{0:T(128)S(1)}, f32[128]{0:T(128)}, u32[]{:S(2)}) copy-start(f32[128]{0:T(128)} %get-tuple-element.97) | copy-start | bytes 1540
  490.4 27.6 %copy-start.38 = (f32[128,1536]{1,0:T(8,128)S(1)}, f32[128,1536]{1,0:T(8,128)}, u32[]{:S(2)}) copy-start(f32[128,1536]{1,0:T(8,128)} %copy-done.37) | copy-start | bytes 2359300
  522.5 5.3 copy-start.55
  522.5 5.3 copy-start.125
  527.8 3.5 copy-start.56
  527.8 3.5 copy-start.123
  531.3 3.5 copy-start.57
  531.3 3.5 copy-start.66
  536.8 3.0 copy-start.49
  536.8 3.0 copy-start.98
  536.8 3.0 copy-start.117
  540.4 3.0 copy-start.53
  667.4 8.3 %copy-start.70 = (f32[192,384]{1,0:T(8,128)S(1)}, f32[192,384]{1,0:T(8,128)}, u32[]{:S(2)}) copy-start(f32[192,384]{1,0:T(8,128)} %get-tuple-element.147) | copy-start | bytes 884740
  667.4 9.0 %copy-start.69 = (f32[4,48,384]{2,1,0:T(8,128)S(1)}, f32[4,48,384]{2,1,0:T(8,128)}, u32[]{:S(2)}) copy-start(f32[4,48,384]{2,1,0:T(8,128)} %get-tuple-element.53) | copy-start | bytes 884740
  667.4 9.7 %copy-start.64 = (f32[512,384]{1,0:T(8,128)S(1)}, f32[512,384]{1,0:T(8,128)}, u32[]{:S(2)}) copy-start(f32[512,384]{1,0:T(8,128)} %get-tuple-element.149) | copy-start | bytes 2359300
  669.3 8.7 %copy-start.63 = (f32[512,384]{1,0:T(8,128)S(1)}, f32[512,384]{1,0:T(8,128)}, u32[]{:S(2)}) copy-start(f32[512,384]{1,0:T(8,128)} %get-tuple-element.150) | copy-start | bytes 2359300
  671.7 7.2 %copy-start.107 = (f32[8,48]{1,0:T(8,128)}, f32[8,48]{1,0:T(8,128)S(1)}, u32[]{:S(2)}) copy-start(f32[8,48]{1,0:T(8,128)S(1)} %dynamic-slice_reduce_fusion) | copy-start | bytes 4612
  673.9 5.0 copy-start.62
  677.1 2.7 copy-start.61
  678.0 2.7 copy-start.60
  (66 other events, 87.4 us)

commit v2 on v1

--- a/solution.py
+++ b/solution.py
@@ -488,98 +488,91 @@
     lax.fori_loop(0, rows // step, body, 0)
 
 
+class Pour:
+    def __init__(self, copies, parts, from_left, from_right, b, s, seq):
+        self.copies, self.parts, self.b, self.s, self.seq = copies, parts, b, s, seq
+        self.got = {1: from_left, -1: from_right}
+        rows = parts.shape[1]
+        self.cuts = 2 if rows % 32 == 0 else 1
+        self.thin = rows // self.cuts
+        self.count = (seq - 1) * self.cuts
+        self.base = {1: copies.take(self.count), -1: copies.take(self.count)}
+        self.next = {
+            1: jnp.where(s < seq - 1, s + 1, s - 1),
+            -1: jnp.where(s > 0, s - 1, s + 1),
+        }
+
+    def block(self, way, q):
+        j, at = q // self.cuts, pl.ds(q % self.cuts * self.thin, self.thin)
+        return self.parts.at[self.seq - 1 - j if way > 0 else j, at], self.got[way].at[j, at]
+
+    def packet(self, way, q):
+        src, dst = self.block(way, q)
+        return self.copies.remote(src, dst, self.b, self.next[way], self.base[way] + q)
+
+    def on(self, way, q):
+        j = q // self.cuts
+        return self.s < self.seq - 1 - j if way > 0 else self.s > j
+
+    def behind(self, way):
+        return self.s > 0 if way > 0 else self.s < self.seq - 1
+
+    def one(self, way, q):
+        src, dst = self.block(way, q)
+
+        @pl.when(jnp.logical_and(self.behind(way), self.on(way, q)))
+        def _():
+            self.packet(way, q).wait_recv()
+            add_rows(src, [src, dst])
+
+        @pl.when(self.on(way, q))
+        def _():
+            if q >= 2:
+                self.packet(way, q - 2).wait_send()
+            self.packet(way, q).start()
+
+    def step(self, q):
+        @pl.when(self.s < self.seq // 2)
+        def _():
+            self.one(1, q)
+            self.one(-1, q)
+
+        @pl.when(self.s >= self.seq // 2)
+        def _():
+            self.one(-1, q)
+            self.one(1, q)
+
+    def end(self, out):
+        seq, cuts = self.seq, self.cuts
+        for t in range(seq):
+
+            @pl.when(self.s == t)
+            def _():
+                terms = [self.parts.at[t]]
+                for way, j in ((1, seq - 1 - t), (-1, t)):
+                    if j < seq - 1:
+                        for c in range(cuts):
+                            self.packet(way, j * cuts + c).wait_recv()
+                        terms.append(self.got[way].at[j])
+                add_rows(out, terms)
+
+        for q in range(self.count):
+            more = q + 2 < self.count
+            for way in (1, -1):
+                last = jnp.logical_not(self.on(way, q + 2)) if more else True
+
+                @pl.when(jnp.logical_and(self.on(way, q), last))
+                def _():
+                    self.packet(way, q).wait_send()
+
+
 def line_scatter_kernel(seq, parts, out, from_left, from_right, send, recv):
     b, s = lax.axis_index("bucket"), lax.axis_index("seq")
     greet_line(b, s, seq)
-    copies = Copies(send, recv)
-    rows = parts.shape[1]
-    cuts = 2 if rows % 32 == 0 else 1
-    thin = rows // cuts
-    steps = (seq - 1) * cuts
-    base_r, base_l = copies.take(steps), copies.take(steps)
-    up, down = jnp.where(s < seq - 1, s + 1, s - 1), jnp.where(s > 0, s - 1, s + 1)
-
-    def to_right(q):
-        j, at = q // cuts, pl.ds(q % cuts * thin, thin)
-        return copies.remote(parts.at[seq - 1 - j, at], from_left.at[j, at], b, up, base_r + q)
-
-    def to_left(q):
-        j, at = q // cuts, pl.ds(q % cuts * thin, thin)
-        return copies.remote(parts.at[j, at], from_right.at[j, at], b, down, base_l + q)
-
-    def right_on(q):
-        return s < seq - 1 - q // cuts
-
-    def left_on(q):
-        return s > q // cuts
-
-    def right_step(q):
-        j, at = q // cuts, pl.ds(q % cuts * thin, thin)
-        block = parts.at[seq - 1 - j, at]
-
-        @pl.when(jnp.logical_and(s > 0, right_on(q)))
-        def _():
-            to_right(q).wait_recv()
-            add_rows(block, [block, from_left.at[j, at]])
-
-        @pl.when(right_on(q))
-        def _():
-            if q >= 2:
-                to_right(q - 2).wait_send()
-            to_right(q).start()
-
-    def left_step(q):
-        j, at = q // cuts, pl.ds(q % cuts * thin, thin)
-        block = parts.at[j, at]
-
-        @pl.when(jnp.logical_and(s < seq - 1, left_on(q)))
-        def _():
-            to_left(q).wait_recv()
-            add_rows(block, [block, from_right.at[j, at]])
-
-        @pl.when(left_on(q))
-        def _():
-            if q >= 2:
-                to_left(q - 2).wait_send()
-            to_left(q).start()
-
-    @pl.when(s < seq // 2)
-    def _():
-        for q in range(steps):
-            right_step(q)
-            left_step(q)
-
-    @pl.when(s >= seq // 2)
-    def _():
-        for q in range(steps):
-            left_step(q)
-            right_step(q)
-
-    for t in range(seq):
-
-        @pl.when(s == t)
-        def _():
-            terms = [parts.at[t]]
-            if t > 0:
-                for c in range(cuts):
-                    to_right((seq - 1 - t) * cuts + c).wait_recv()
-                terms.append(from_left.at[seq - 1 - t])
-            if t < seq - 1:
-                for c in range(cuts):
-                    to_left(t * cuts + c).wait_recv()
-                terms.append(from_right.at[t])
-            add_rows(out, terms)
-
-    for q in range(steps):
-        more = q + 2 < steps
-
-        @pl.when(jnp.logical_and(right_on(q), jnp.logical_not(right_on(q + 2)) if more else True))
-        def _():
-            to_right(q).wait_send()
-
-        @pl.when(jnp.logical_and(left_on(q), jnp.logical_not(left_on(q + 2)) if more else True))
-        def _():
-            to_left(q).wait_send()
+    pour = Pour(Copies(send, recv), parts, from_left, from_right, b, s, seq)
+    for q in range(pour.count):
+        pour.step(q)
+    pour.end(out)
 
 
 def line_scatter(seq, parts, collective_id):
@@ -603,150 +596,94 @@
     )(parts.astype(BF16).reshape(seq, rows, wide))
 
 
-def scatter_kernel(buckets, seq, kinds, *refs):
-    count = len(kinds)
-    vec, grads = refs[0], refs[1 : 1 + count]
-    vec_all, outs = refs[1 + count], refs[2 + count : 2 + 2 * count]
-    at = 2 + 2 * count
-    vec_seq, vec_sum, send, recv = refs[at : at + 4]
-    scratch = refs[at + 4 :]
-    b, s = lax.axis_index("bucket"), lax.axis_index("seq")
-    copies = Copies(send, recv)
-    chips = buckets // 2
-    chip, core = lax.div(b, 2), lax.rem(b, 2)
-    place = s * buckets + b
-    to_b = lax.div(place, seq)
-    twin = flip(b, 1)
-    sent = []
-
-    def go(copy):
+class GradSums:
+    def __init__(self, copies, b, s, buckets, seq, kinds, grads, outs, scratch):
+        self.copies, self.b, self.s, self.buckets, self.seq = copies, b, s, buckets, seq
+        self.kinds, self.grads, self.outs = kinds, grads, outs
+        self.scratch = [scratch[8 * w : 8 * w + 8] for w in range(len(kinds))]
+        self.chips = buckets // 2
+        self.chip, self.core = lax.div(b, 2), lax.rem(b, 2)
+        self.place = s * buckets + b
+        self.to_b = lax.div(self.place, seq)
+        self.twin = flip(b, 1)
+        self.begun, self.state, self.last = {}, {}, {}
+        self.sent = []
+
+    def go(self, copy):
         copy.start()
-        sent.append(copy)
+        self.sent.append(copy)
         return copy
 
-    for k in range(1, buckets):
-        greet(lax.rem(b + k, buckets), s)
-    for k in range(1, seq):
-        greet(b, lax.rem(s + k, seq))
-    for j in range(seq):
-        d = b * seq + j
-        src_b, src_s = lax.rem(d, buckets), lax.div(d, buckets)
-
-        @pl.when(jnp.logical_not(jnp.logical_and(src_b == b, src_s == s)))
-        def _():
-            greet(src_b, src_s)
-
-    peers = buckets - 1 + seq - 1 + seq - jnp.where(to_b == b, 1, 0)
-    pl.semaphore_wait(pltpu.get_barrier_semaphore(), peers)
-
-    vec_moves = []
-    for k in range(1, seq):
-        vec_moves.append(go(copies.remote(vec, vec_seq.at[k], b, lax.rem(s + k, seq))))
-
-    begun = []
-
-    def begin(w):
-        own, other = scratch[6 * w], scratch[6 * w + 1]
-        swap = copies.remote(grads[w].at[:, 1 - core], other, twin, s)
-        keep = copies.local(grads[w].at[:, core], own)
+    def begin(self, w):
+        own, other = self.scratch[w][:2]
+        grad = self.grads[w]
+        swap = self.copies.remote(grad.at[:, 1 - self.core], other, self.twin, self.s)
+        keep = self.copies.local(grad.at[:, self.core], own)
         swap.start()
         keep.start()
-        begun.append((swap, keep))
-
-    begin(0)
-    if count > 1:
-        begin(1)
-
-    for move in vec_moves:
-        move.wait_recv()
-    add_rows(vec_sum, [vec] + [vec_seq.at[k] for k in range(1, seq)])
-    vec_next = []
-    for k in range(1, buckets):
-        peer = lax.rem(b + k, buckets)
-        vec_next.append(go(copies.remote(vec_sum, vec_all.at[b], peer, s)))
-    vec_own = copies.local(vec_sum, vec_all.at[b])
-    vec_own.start()
-
-    state = [None] * count
-    if chips == 4:
-        mx, my = flip(chip, 1), flip(chip, 2)
-        far = flip(mx, 2)
-        near_x, near_y = flip(b, 2), flip(b, 4)
-
-        def stage_a(w):
-            own, other, half_x, half_y, _, _ = scratch[6 * w : 6 * w + 6]
-            swap, keep = begun[w]
-            swap.wait()
-            keep.wait()
-            if w + 2 < count:
-                begin(w + 2)
-            add_rows(own.at[far], [own.at[far], other.at[far]])
-            rows = own.shape[1]
-            cut = halves_of(own.shape[1:])
-            state[w] = [
-                go(copies.remote(own.at[far, pl.ds(0, cut)], half_x, near_x, s)),
-                go(copies.remote(own.at[far, pl.ds(cut, rows - cut)], half_y, near_y, s)),
-            ]
-
-        def stage_b(w):
-            own, other, half_x, half_y, got_x, got_y = scratch[6 * w : 6 * w + 6]
-            rows = own.shape[1]
-            cut = halves_of(own.shape[1:])
-            top, low = pl.ds(0, cut), pl.ds(cut, rows - cut)
-            move_x, move_y = state[w]
-            move_x.wait_recv()
-            add_rows(own.at[my, top], [own.at[my, top], other.at[my, top], half_x])
-            add_rows(own.at[my, low], [own.at[my, low], other.at[my, low]])
-            next_y = go(copies.remote(own.at[my], got_y, near_y, s))
-            move_y.wait_recv()
-            add_rows(own.at[mx, low], [own.at[mx, low], other.at[mx, low], half_y])
-            add_rows(own.at[mx, top], [own.at[mx, top], other.at[mx, top]])
-            next_x = go(copies.remote(own.at[mx], got_x, near_x, s))
-            state[w] = [next_x, next_y]
-
-        def terms_of(w):
-            own, other, _, _, got_x, got_y = scratch[6 * w : 6 * w + 6]
-            return [own.at[chip], other.at[chip], got_x, got_y]
-
-    else:
-
-        def stage_a(w):
-            own, other, got = scratch[6 * w], scratch[6 * w + 1], scratch[6 * w + 4]
-            swap, keep = begun[w]
-            swap.wait()
-            keep.wait()
-            if w + 2 < count:
-                begin(w + 2)
-            state[w] = []
-            for k in range(1, chips):
-                to = lax.rem(chip + k, chips)
+        self.begun[w] = (swap, keep)
+
+    def stage_a(self, w):
+        own, other, half_x, half_y, got, _ = self.scratch[w][:6]
+        for copy in self.begun[w]:
+            copy.wait()
+        if w + 2 in range(len(self.kinds)) and w + 2 not in self.begun:
+            self.begin(w + 2)
+        rows = own.shape[1]
+        if self.chips != 4:
+            moves = []
+            for k in range(1, self.chips):
+                to = lax.rem(self.chip + k, self.chips)
                 add_rows(own.at[to], [own.at[to], other.at[to]])
-                state[w].append(go(copies.remote(own.at[to], got.at[k], 2 * to + core, s)))
-
-        def stage_b(w):
-            pass
-
-        def terms_of(w):
-            own, other, got = scratch[6 * w], scratch[6 * w + 1], scratch[6 * w + 4]
-            return [own.at[chip], other.at[chip]] + [got.at[k] for k in range(1, chips)]
-
-    last = [None] * count
-
-    def stage_c(w):
-        for move in state[w]:
+                move = self.copies.remote(own.at[to], got.at[k], 2 * to + self.core, self.s)
+                moves.append(self.go(move))
+            self.state[w] = moves
+            return
+        far = flip(flip(self.chip, 1), 2)
+        add_rows(own.at[far], [own.at[far], other.at[far]])
+        cut = halves_of(own.shape[1:])
+        near_x, near_y = flip(self.b, 2), flip(self.b, 4)
+        top, low = own.at[far, pl.ds(0, cut)], own.at[far, pl.ds(cut, rows - cut)]
+        self.state[w] = [
+            self.go(self.copies.remote(top, half_x, near_x, self.s)),
+            self.go(self.copies.remote(low, half_y, near_y, self.s)),
+        ]
+
+    def stage_b(self, w):
+        if self.chips != 4:
+            return
+        own, other, half_x, half_y, got_x, got_y = self.scratch[w][:6]
+        rows = own.shape[1]
+        cut = halves_of(own.shape[1:])
+        top, low = pl.ds(0, cut), pl.ds(cut, rows - cut)
+        mx, my = flip(self.chip, 1), flip(self.chip, 2)
+        move_x, move_y = self.state[w]
+        move_x.wait_recv()
+        add_rows(own.at[my, top], [own.at[my, top], other.at[my, top], half_x])
+        add_rows(own.at[my, low], [own.at[my, low], other.at[my, low]])
+        next_y = self.go(self.copies.remote(own.at[my], got_y, flip(self.b, 4), self.s))
+        move_y.wait_recv()
+        add_rows(own.at[mx, low], [own.at[mx, low], other.at[mx, low], half_y])
+        add_rows(own.at[mx, top], [own.at[mx, top], other.at[mx, top]])
+        next_x = self.go(self.copies.remote(own.at[mx], got_x, flip(self.b, 2), self.s))
+        self.state[w] = [next_x, next_y]
+
+    def stage_c(self, w):
+        own, other, _, _, got_x, got_y, done, landed = self.scratch[w]
+        for move in self.state[w]:
             move.wait_recv()
-        add_rows(outs[w], terms_of(w))
-
-    row_base = {w: copies.take(2 * seq) for w in range(count) if kinds[w] == "row"}
-
-    def stage_c_row(w):
-        for move in state[w]:
-            move.wait_recv()
-        out, terms = outs[w], terms_of(w)
-        done, landed = scratch[6 * count + 2 * w], scratch[6 * count + 2 * w + 1]
-        wide = out.shape[-1]
-        me = lax.rem(place, seq)
-        base = row_base[w]
+        terms = [own.at[self.chip], other.at[self.chip]]
+        if self.chips == 4:
+            terms += [got_x, got_y]
+        else:
+            terms += [got_x.at[k] for k in range(1, self.chips)]
+        if self.kinds[w] == "col":
+            add_rows(self.outs[w], terms)
+            return
+        seq, send, recv = self.seq, self.copies.send, self.copies.recv
+        wide = self.outs[w].shape[-1]
+        me = lax.rem(self.place, seq)
+        base = self.copies.take(2 * seq)
         rows = terms[0].shape[0]
         step = 16 if rows % 16 == 0 else rows
 
@@ -767,11 +704,11 @@
                 dst_ref=landed.at[me],
                 send_sem=send.at[base + t],
                 recv_sem=recv.at[base + me],
-                device_id={"bucket": to_b, "seq": t},
+                device_id={"bucket": self.to_b, "seq": t},
                 device_id_type=MESH,
             )
             keep = pltpu.make_async_copy(done.at[t], landed.at[me], send.at[base + seq + t])
-            here = jnp.logical_and(to_b == b, s == t)
+            here = jnp.logical_and(self.to_b == self.b, self.s == t)
 
             @pl.when(jnp.logical_not(here))
             def _():
@@ -782,30 +719,30 @@
                 keep.start()
 
             moves.append((move, keep, here))
-        last[w] = moves
-
-    def stage_d(w):
-        if kinds[w] != "row":
+        self.last[w] = (base, moves)
+
+    def stage_d(self, w):
+        if self.kinds[w] != "row":
             return
-        out = outs[w]
-        done, landed = scratch[6 * count + 2 * w], scratch[6 * count + 2 * w + 1]
-        base = row_base[w]
+        done, landed = self.scratch[w][6:]
+        base, moves = self.last[w]
+        out, seq, buckets = self.outs[w], self.seq, self.buckets
         for j in range(seq):
-            d = b * seq + j
-            here = jnp.logical_and(lax.rem(d, buckets) == b, lax.div(d, buckets) == s)
+            d = self.b * seq + j
+            here = jnp.logical_and(lax.rem(d, buckets) == self.b, lax.div(d, buckets) == self.s)
 
             @pl.when(jnp.logical_not(here))
             def _():
                 pltpu.make_async_remote_copy(
                     src_ref=done.at[j],
                     dst_ref=landed.at[j],
-                    send_sem=send.at[base + j],
-                    recv_sem=recv.at[base + j],
-                    device_id={"bucket": twin, "seq": s},
+                    send_sem=self.copies.send.at[base + j],
+                    recv_sem=self.copies.recv.at[base + j],
+                    device_id={"bucket": self.twin, "seq": self.s},
                     device_id_type=MESH,
                 ).wait_recv()
 
-        for move, keep, here in last[w]:
+        for move, keep, here in moves:
 
             @pl.when(jnp.logical_not(here))
             def _():
@@ -818,50 +755,97 @@
         for j in range(seq):
             add_rows(out.at[j], [landed.at[j]])
 
-    for w in range(count + 2):
-        if w < count:
-            stage_a(w)
-        if 1 <= w <= count:
-            stage_b(w - 1)
-        if w >= 2:
-            if kinds[w - 2] == "row":
-                stage_c_row(w - 2)
-            else:
-                stage_c(w - 2)
-    for w in range(count):
-        stage_d(w)
-    for move in vec_next:
-        move.wait_recv()
-    vec_own.wait()
-    for move in sent:
-        move.wait_send()
-
-
-def scatter_all(buckets, seq, vec, grads, kinds):
+    def steps(self):
+        count = len(self.kinds)
+        for w in range(count + 2):
+            if w < count:
+                yield lambda w=w: self.stage_a(w)
+            if 1 <= w <= count:
+                yield lambda w=w: self.stage_b(w - 1)
+            if w >= 2:
+                yield lambda w=w: self.stage_c(w - 2)
+        yield lambda: [self.stage_d(w) for w in range(count)]
+
+    def end(self):
+        for move in self.sent:
+            move.wait_send()
+
+
+def greet_all(b, s, buckets, seq):
+    for k in range(1, buckets):
+        greet(lax.rem(b + k, buckets), s)
+    for k in range(1, seq):
+        greet(b, lax.rem(s + k, seq))
+    for j in range(seq):
+        d = b * seq + j
+        src_b, src_s = lax.rem(d, buckets), lax.div(d, buckets)
+
+        @pl.when(jnp.logical_not(jnp.logical_and(src_b == b, src_s == s)))
+        def _():
+            greet(src_b, src_s)
+
+    to_b = lax.div(s * buckets + b, seq)
+    return buckets - 1 + seq - 1 + seq - jnp.where(to_b == b, 1, 0)
+
+
+def sums_shapes(buckets, seq, grads, kinds):
     chips = buckets // 2
-    any_spec = pl.BlockSpec(memory_space=pl.ANY)
-    vmem = pl.BlockSpec(memory_space=pltpu.VMEM)
-    inputs, outs, scratch, tail = [], [], [], []
+    inputs, outs, scratch = [], [], []
     for grad, kind in zip(grads, kinds, strict=True):
         rows, wide = grad.shape[0] // buckets, grad.shape[1]
         inputs.append(grad.astype(BF16).reshape(chips, 2, rows, wide))
         cut = halves_of((rows, wide))
-        scratch += [
-            pltpu.VMEM((chips, rows, wide), BF16),
-            pltpu.VMEM((chips, rows, wide), BF16),
-            pltpu.VMEM((cut, wide), BF16),
-            pltpu.VMEM((rows - cut, wide), BF16),
-            pltpu.VMEM((rows, wide) if chips == 4 else (chips, rows, wide), BF16),
-            pltpu.VMEM((rows, wide) if chips == 4 else (16, 128), BF16),
-        ]
-        if kind == "row":
-            shape = (seq, rows, wide // seq)
-            outs.append(jax.ShapeDtypeStruct(shape, F32))
-            tail += [pltpu.VMEM(shape, BF16)] * 2
+        tiny = pltpu.VMEM((16, 128), BF16)
+        scratch += [pltpu.VMEM((chips, rows, wide), BF16)] * 2
+        if chips == 4:
+            scratch += [pltpu.VMEM((cut, wide), BF16), pltpu.VMEM((rows - cut, wide), BF16)]
+            scratch += [pltpu.VMEM((rows, wide), BF16)] * 2
         else:
-            outs.append(jax.ShapeDtypeStruct((rows, wide), F32))
-            tail += [pltpu.VMEM((16, 128), BF16)] * 2
+            scratch += [tiny, tiny, pltpu.VMEM((chips, rows, wide), BF16), tiny]
+        shape = (seq, rows, wide // seq) if kind == "row" else (rows, wide)
+        outs.append(jax.ShapeDtypeStruct(shape, F32))
+        scratch += [pltpu.VMEM(shape, BF16) if kind == "row" else tiny] * 2
     n_sems = 32 + 2 * buckets + len(grads) * (8 + 3 * seq + buckets)
+    return inputs, outs, scratch, n_sems
+
+
+def scatter_kernel(buckets, seq, kinds, *refs):
+    count = len(kinds)
+    vec, grads = refs[0], refs[1 : 1 + count]
+    vec_all, outs = refs[1 + count], refs[2 + count : 2 + 2 * count]
+    at = 2 + 2 * count
+    vec_seq, vec_sum, send, recv = refs[at : at + 4]
+    b, s = lax.axis_index("bucket"), lax.axis_index("seq")
+    copies = Copies(send, recv)
+    sums = GradSums(copies, b, s, buckets, seq, kinds, grads, outs, refs[at + 4 :])
+    peers = greet_all(b, s, buckets, seq)
+    pl.semaphore_wait(pltpu.get_barrier_semaphore(), peers)
+    vec_moves = []
+    for k in range(1, seq):
+        vec_moves.append(sums.go(copies.remote(vec, vec_seq.at[k], b, lax.rem(s + k, seq))))
+    for w in range(min(2, count)):
+        sums.begin(w)
+    for move in vec_moves:
+        move.wait_recv()
+    add_rows(vec_sum, [vec] + [vec_seq.at[k] for k in range(1, seq)])
+    vec_next = []
+    for k in range(1, buckets):
+        peer = lax.rem(b + k, buckets)
+        vec_next.append(sums.go(copies.remote(vec_sum, vec_all.at[b], peer, s)))
+    vec_own = copies.local(vec_sum, vec_all.at[b])
+    vec_own.start()
+    for step in sums.steps():
+        step()
+    for move in vec_next:
+        move.wait_recv()
+    vec_own.wait()
+    sums.end()
+
+
+def scatter_all(buckets, seq, vec, grads, kinds, collective_id=1):
+    any_spec = pl.BlockSpec(memory_space=pl.ANY)
+    vmem = pl.BlockSpec(memory_space=pltpu.VMEM)
+    inputs, outs, scratch, n_sems = sums_shapes(buckets, seq, grads, kinds)
     results = pl.pallas_call(
         functools.partial(scatter_kernel, buckets, seq, tuple(kinds)),
         out_shape=[jax.ShapeDtypeStruct((buckets,) + vec.shape, F32), *outs],
@@ -873,10 +857,9 @@
             pltpu.SemaphoreType.DMA((n_sems,)),
             pltpu.SemaphoreType.DMA((n_sems,)),
             *scratch,
-            *tail,
         ],
         compiler_params=pltpu.CompilerParams(
-            collective_id=1, has_side_effects=True, vmem_limit_bytes=60 * 2**20
+            collective_id=collective_id, has_side_effects=True, vmem_limit_bytes=60 * 2**20
         ),
     )(vec, *inputs)
     return results[0], [out.reshape(-1, out.shape[-1]) for out in results[1:]]
@@ -898,6 +881,806 @@
     d_key = jnp.einsum("hqk,qhd->khd", d_low, queries, preferred_element_type=F32) * scale
     d_value = jnp.einsum("hqk,qhd->khd", probs.astype(BF16), d_out, preferred_element_type=F32)
     return d_query, d_key, d_value
+
+
+def on_device_general(
+    tokens,
+    captions,
+    cotangent,
+    counts,
+    cap_lens,
+    steps_t,
+    w_query,
+    w_key,
+    w_value,
+    w_out,
+    w_cap_key,
+    w_cap_value,
+    w_gate,
+    w_up,
+    w_down,
+    w_mod,
+    gains,
+    cross_gate,
+):
+    buckets, seq = lax.axis_size("bucket"), lax.axis_size("seq")
+    b, s = lax.axis_index("bucket"), lax.axis_index("seq")
+    place = b * seq + s
+    rows, width = tokens.shape
+    span = rows * seq
+    share = width // seq
+    heads = share // HEAD_DIM
+    scale = HEAD_DIM ** (-0.5)
+    live_rows, cap_len = pick_entry(counts, b), pick_entry(cap_lens, b)
+    token_total = jnp.sum(counts).astype(F32)
+
+    cond_size = w_mod.shape[0] * buckets * seq
+    cond = jax.nn.silu(time_embed(steps_t, cond_size)).astype(BF16)
+    cond_part = lax.dynamic_slice_in_dim(cond, place * w_mod.shape[0], w_mod.shape[0], 1)
+    slim = gains.shape[1]
+    small = jnp.concatenate([gains, cross_gate[None]], axis=0).astype(F32)
+    small = jnp.pad(small, ((0, 0), (0, 128 - slim)))
+    tok_all, cap_all, small_all, mod, weights = gather_all(
+        buckets,
+        seq,
+        tokens,
+        captions,
+        small,
+        cond_part,
+        w_mod,
+        [w_query, w_key, w_value, w_cap_key, w_cap_value, w_out, w_gate, w_up, w_down],
+        ["col", "col", "col", "col", "col", "row", "col", "col", "row"],
+    )
+    wq, wk, wv, wck, wcv, wo, wg, wu, wd = weights
+    caps = cap_all.reshape(-1, captions.shape[1])
+    small_rows = small_all[..., :slim].transpose(2, 0, 1, 3).reshape(8, width)
+    gain_f = small_rows[:7]
+    own_cols = lax.dynamic_slice_in_dim(small_rows, s * share, share, 1)
+    gate_cross = jnp.tanh(own_cols[7])
+    scale_attn, gate_attn, scale_ffn, gate_ffn = mod.reshape(4, width)
+
+    hidden = pre_attn(tok_all.astype(F32), gain_f[0], scale_attn).astype(BF16).reshape(span, width)
+    query_proj, key_proj = bf_dot(hidden, wq), bf_dot(hidden, wk)
+    value_low = bf_dot(hidden, wv).astype(BF16)
+    (query_f, key_f), norm_back = jax.vjp(qk_norm, query_proj, key_proj, own_cols[4], own_cols[5])
+    cap_key_f, cap_back = jax.vjp(cap_norm, bf_dot(caps, wck), own_cols[6])
+
+    def by_head(values):
+        return values.astype(BF16).reshape(values.shape[0], heads, HEAD_DIM)
+
+    query, key, value = by_head(query_f), by_head(key_f), by_head(value_low)
+    cap_key, cap_value = by_head(cap_key_f), by_head(bf_dot(caps, wcv))
+    probs, self_out = attention(query, key, value, jnp.arange(span) < live_rows, scale)
+    cap_live = jnp.arange(caps.shape[0]) < cap_len
+    cap_probs, cross_out = attention(query, cap_key, cap_value, cap_live, scale)
+    self_out, cross_out = self_out.reshape(span, share), cross_out.reshape(span, share)
+    mixed_low = (self_out + gate_cross * cross_out).astype(BF16)
+    attn_out = line_scatter(seq, bf_dot(mixed_low, wo), 2)
+
+    tokens_f = tokens.astype(F32)
+    (resid_one, ffn_pre), middle_back = jax.vjp(
+        middle, tokens_f, attn_out, gain_f[1], gate_attn, gain_f[2], scale_ffn
+    )
+    ffn_all = line_gather(seq, ffn_pre.astype(BF16), 3)
+    act_pre, act_back = jax.vjp(activate, bf_dot(ffn_all, wg), bf_dot(ffn_all, wu))
+    act_low = act_pre.astype(BF16)
+    ffn_out = line_scatter(seq, bf_dot(act_low, wd), 4)
+    out_f, finish_back = jax.vjp(finish, resid_one, ffn_out, gain_f[3], gate_ffn)
+    block_out = out_f.astype(BF16)
+
+    row_live = (s * rows + jnp.arange(rows) < live_rows).astype(F32)
+    weighted = cotangent.astype(F32) * row_live[:, None] * (buckets * span / token_total)
+    d_resid, d_ffn_out, d_gain_last, d_gate_ffn = finish_back(weighted)
+    d_ffn_all = line_gather(seq, d_ffn_out.astype(BF16), 5)
+    d_gate, d_up = act_back(right_dot(d_ffn_all, wd))
+    d_gate, d_up = d_gate.astype(BF16), d_up.astype(BF16)
+    d_hidden_ffn = line_scatter(seq, right_dot(d_gate, wg) + right_dot(d_up, wu), 6)
+    d_tokens_one, d_attn_out, d_gain_post, d_gate_attn, d_gain_ffn, d_scale_ffn = middle_back(
+        (d_resid, d_hidden_ffn)
+    )
+    d_attn_all = line_gather(seq, d_attn_out.astype(BF16), 7)
+    d_mixed_low = right_dot(d_attn_all, wo).astype(BF16)
+    d_mixed = d_mixed_low.astype(F32)
+    d_cross_low = (gate_cross * d_mixed).astype(BF16)
+    grad_cross = jnp.sum(d_mixed * cross_out, axis=0) * (1.0 - gate_cross * gate_cross)
+
+    d_query_cross, d_cap_key, d_cap_value = attention_back(
+        cap_probs, query, cap_key, cap_value, by_head(d_cross_low), scale
+    )
+    d_query, d_key, d_value = attention_back(probs, query, key, value, by_head(d_mixed_low), scale)
+    d_cap_key, d_gain_cap = cap_back(d_cap_key.reshape(-1, share))
+    d_query, d_key, d_gain_query, d_gain_key = norm_back(
+        ((d_query + d_query_cross).reshape(span, share), d_key.reshape(span, share))
+    )
+    d_query, d_key, d_cap_key = d_query.astype(BF16), d_key.astype(BF16), d_cap_key.astype(BF16)
+    d_value = d_value.reshape(span, share).astype(BF16)
+    d_cap_value = d_cap_value.reshape(-1, share).astype(BF16)
+    d_hidden = line_scatter(
+        seq, right_dot(d_query, wq) + right_dot(d_key, wk) + right_dot(d_value, wv), 8
+    )
+    _, pre_back = jax.vjp(pre_attn, tokens_f, gain_f[0], scale_attn)
+    d_tokens_two, d_gain_pre, d_scale_attn = pre_back(d_hidden)
+    tokens_grad = d_tokens_one + d_tokens_two
+
+    own_sums = jnp.stack([d_gain_query, d_gain_key, d_gain_cap, grad_cross])
+    own_wide = lax.dynamic_update_slice(jnp.zeros((4, width), F32), own_sums, (0, s * share))
+    vec = jnp.concatenate(
+        [
+            jnp.stack([d_scale_attn, d_gate_attn, d_scale_ffn, d_gate_ffn]),
+            jnp.stack([d_gain_pre, d_gain_post, d_gain_ffn, d_gain_last]),
+            own_wide,
+            jnp.zeros((4, width), F32),
+        ]
+    )
+    grads = [
+        left_dot(ffn_all, d_gate),
+        left_dot(ffn_all, d_up),
+        left_dot(act_low, d_ffn_all),
+        left_dot(mixed_low, d_attn_all),
+        left_dot(caps, d_cap_key),
+        left_dot(caps, d_cap_value),
+        left_dot(hidden, d_query),
+        left_dot(hidden, d_key),
+        left_dot(hidden, d_value),
+    ]
+    kinds = ["col", "col", "row", "row", "col", "col", "col", "col", "col"]
+    vec_all, sums = scatter_all(buckets, seq, vec, grads, kinds)
+    s_gate, s_up, s_down, s_out, s_cap_key, s_cap_value, s_query, s_key, s_value = sums
+
+    quarter = 4 * width // seq
+    mod_rows = vec_all[:, :4].reshape(buckets, -1, quarter)
+    mod_rows = lax.dynamic_slice_in_dim(mod_rows, s, 1, 1)[:, 0]
+    cond_size = cond.shape[1] // buckets
+    cond_cols = lax.dynamic_slice_in_dim(cond, b * cond_size, cond_size, 1).astype(F32)
+    s_mod = jnp.sum(cond_cols[:, :, None] * mod_rows[:, None, :], axis=0)
+    tail = lax.dynamic_slice(vec_all, (0, 4, place * slim), (buckets, 8, slim))
+    tail = jnp.sum(tail, axis=0)
+    return (
+        block_out,
+        tokens_grad,
+        s_query,
+        s_key,
+        s_value,
+        s_out,
+        s_cap_key,
+        s_cap_value,
+        s_gate,
+        s_up,
+        s_down,
+        s_mod,
+        tail[:7],
+        tail[7],
+    )
+
+
+def low_half(shape):
+    return lax.broadcasted_iota(jnp.int32, shape, len(shape) - 1) < HEAD_DIM
+
+
+def pair_scale(values, eps):
+    low = low_half(values.shape)
+    squares = values * values
+    first = jnp.sum(jnp.where(low, squares, 0.0), axis=-1, keepdims=True)
+    second = jnp.sum(jnp.where(low, 0.0, squares), axis=-1, keepdims=True)
+    return lax.rsqrt(jnp.where(low, first, second) * (1.0 / HEAD_DIM) + eps)
+
+
+FORWARD_ORDER = ("tok", 0, "tok", 1, "tok", 2, "tok", 5, 3, "cap", 4, "cap", 6, "cap", 7, "cap", 8)
+
+
+def forward_kernel(buckets, seq, kinds, slim, *refs):
+    count = len(kinds)
+    tokens, captions, small, cond, w_mod, key_mask, cap_mask = refs[:7]
+    shards = refs[7 : 7 + count]
+    refs = refs[7 + count :]
+    cap_all = refs[0]
+    fulls = refs[1 : 1 + count]
+    refs = refs[1 + count :]
+    (
+        gain_rows,
+        mod_rows,
+        hidden,
+        query_raw,
+        key_raw,
+        cap_raw,
+        query,
+        key,
+        value,
+        cap_key,
+        cap_value,
+        cross_out,
+        mixed,
+    ) = refs[:13]
+    refs = refs[13:]
+    part, got_bucket, got_seq, mod_sum, small_all, tok_all, cap_near = refs[:7]
+    near = refs[7:12]
+    send, recv = refs[12:]
+    b, s = lax.axis_index("bucket"), lax.axis_index("seq")
+    copies = Copies(send, recv)
+    place = b * seq + s
+    to_b, to_s = lax.rem(place, buckets), lax.div(place, buckets)
+    back = s * buckets + b
+    from_b, from_s = lax.div(back, seq), lax.rem(back, seq)
+    stays = jnp.logical_and(to_b == b, to_s == s)
+
+    for k in range(1, buckets):
+        greet(lax.rem(b + k, buckets), s)
+    for k in range(1, seq):
+        greet(b, lax.rem(s + k, seq))
+
+    @pl.when(jnp.logical_not(stays))
+    def _():
+        greet(from_b, from_s)
+
+    lanes = part.shape[2]
+    for j in range(part.shape[1]):
+        part[:, j, :] = bf_dot(cond[...], w_mod[:, j * lanes : (j + 1) * lanes])
+
+    peers = buckets - 1 + seq - 1 + jnp.where(stays, 0, 1)
+    pl.semaphore_wait(pltpu.get_barrier_semaphore(), peers)
+
+    sent = []
+
+    def go(copy):
+        copy.start()
+        sent.append(copy)
+        return copy
+
+    mod_moves = []
+    for k in range(1, buckets):
+        peer = lax.rem(b + k, buckets)
+        mod_moves.append(go(copies.remote(part.at[peer], got_bucket.at[k], peer, s)))
+    small_moves = []
+    for k in range(1, seq):
+        peer = lax.rem(s + k, seq)
+        small_moves.append(go(copies.remote(small, small_all.at[b, s], b, peer)))
+    small_own = copies.local(small, small_all.at[b, s])
+    small_own.start()
+
+    tok = Relay(copies, tokens, tok_all, b, s, seq)
+    cap = Relay(copies, captions, cap_near, b, s, seq)
+    items, step = [], {"tok": 0, "cap": 0}
+    for what in FORWARD_ORDER:
+        if isinstance(what, str):
+            items.append((tok if what == "tok" else cap, step[what]))
+            step[what] += 1
+        else:
+            items.append((None, what))
+
+    first = [None] * count
+
+    def depart(at):
+        kind, shard, full = kinds[at], shards[at], fulls[at]
+        if kind == "row":
+            move = copies.remote(shard, full.at[to_b], to_b, to_s)
+            keep = copies.local(shard, full.at[b])
+
+            @pl.when(jnp.logical_not(stays))
+            def _():
+                move.start()
+
+            @pl.when(stays)
+            def _():
+                keep.start()
+
+            first[at] = (move, keep)
+            return
+        wide = full.shape[-1]
+
+        def columns(peer):
+            return shard.at[:, pl.ds(pl.multiple_of(peer * wide, 128), wide)]
+
+        moves = []
+        for k in range(1, seq):
+            peer = lax.rem(s + k, seq)
+            move = copies.remote(columns(peer), full.at[b, s], b, peer)
+            move.start()
+            moves.append(move)
+        keep = copies.local(columns(s), full.at[b, s])
+        keep.start()
+        first[at] = (moves, keep)
+
+    def arrived(at):
+        moves, keep = first[at]
+        if kinds[at] == "row":
+
+            @pl.when(jnp.logical_not(stays))
+            def _():
+                moves.wait()
+
+            @pl.when(stays)
+            def _():
+                keep.wait()
+
+            return
+        for move in moves:
+            move.wait()
+        keep.wait()
+
+    twin = flip(b, 1)
+    near_x, near_y = flip(b, 2), flip(b, 4)
+    far = flip(near_x, 4)
+    second = [None] * count
+
+    def stage_a(at):
+        full = fulls[at]
+        second[at] = {
+            "x": go(copies.remote(full.at[b], full.at[b], near_x, s)),
+            "y": go(copies.remote(full.at[b], full.at[b], near_y, s)),
+            "twin": [go(copies.remote(full.at[b], full.at[b], twin, s))],
+        }
+
+    def stage_b(at):
+        full, now = fulls[at], second[at]
+        cut = halves_of(full.shape[1:])
+        now["x"].wait_recv()
+        block = full.at[near_x, pl.ds(0, cut)]
+        now["dy"] = go(copies.remote(block, block, near_y, s))
+        block = full.at[near_x]
+        now["twin"].append(go(copies.remote(block, block, twin, s)))
+        now["y"].wait_recv()
+        block = full.at[near_y, pl.ds(cut, full.shape[1] - cut)]
+        now["dx"] = go(copies.remote(block, block, near_x, s))
+        block = full.at[near_y]
+        now["twin"].append(go(copies.remote(block, block, twin, s)))
+
+    fetched = {}
+
+    def stage_c(at):
+        full, now = fulls[at], second[at]
+        now["dy"].wait_recv()
+        now["dx"].wait_recv()
+        block = full.at[far]
+        now["twin"].append(go(copies.remote(block, block, twin, s)))
+        for move in now["twin"]:
+            move.wait_recv()
+        if at < len(near):
+            fetched[at] = copies.local(full, near[at])
+            fetched[at].start()
+
+    def fetch(at):
+        fetched[at].wait()
+        whole = near[at][...]
+        return whole.reshape(-1, whole.shape[-1])
+
+
+    rows = seq * tok_all.shape[1]
+    width = tok_all.shape[2]
+    cap_rows = seq * cap_near.shape[1]
+    share = query.shape[1]
+    pairs = share // 128
+    block_rows = tok_all.shape[1]
+
+    def small_sums():
+        for move in small_next:
+            move.wait_recv()
+        strips = [None] * (width // 128)
+        lane = lax.broadcasted_iota(jnp.int32, (8, 128), 1)
+        for d in range(buckets * seq):
+            at, shift = divmod(d * slim, 128)
+            piece = small_all[d // seq, d % seq]
+            turned = pltpu.roll(piece, shift, 1) if shift else piece
+            for index, keep in ((at, lane >= shift), (at + 1, lane < shift)):
+                if index == at + 1 and shift + slim <= 128:
+                    continue
+                add = jnp.where(keep, turned, 0.0)
+                strips[index] = add if strips[index] is None else strips[index] + add
+        for at, strip in enumerate(strips):
+            gain_rows[:, at * 128 : (at + 1) * 128] = strip
+        total = mod_sum[...]
+        for k, move in enumerate(mod_next, 1):
+            move.wait_recv()
+            total = total + got_seq[k]
+        for j in range(8):
+            at, lane_at = divmod(j * lanes, width)
+            mod_rows[at : at + 1, lane_at : lane_at + lanes] = total[j : j + 1, :]
+        mod_rows[4:8, :] = jnp.zeros((4, width), F32)
+
+    def make_hidden():
+        factor = gain_rows[0:1, :] * (1.0 + mod_rows[0:1, :])
+        for t in range(seq):
+
+            def body(i, carry):
+                at = pl.ds(pl.multiple_of(i * 32, 32), 32)
+                x = tok_all[t, at, :].astype(F32)
+                x = x * lax.rsqrt(jnp.mean(x * x, axis=-1, keepdims=True) + 1e-05) * factor
+                to = pl.ds(pl.multiple_of(t * block_rows + i * 32, 32), 32)
+                hidden[to, :] = x.astype(BF16)
+                return carry
+
+            lax.fori_loop(0, block_rows // 32, body, 0)
+
+    def gain_of(row, pair):
+        at = pl.multiple_of(s * share + pair * 128, 128)
+        return gain_rows[row : row + 1, pl.ds(at, 128)]
+
+    def make_normed(raw, out, row, scale):
+        def body(i, carry):
+            at = pl.ds(pl.multiple_of(i * 64, 64), 64)
+            for pair in range(pairs):
+                lane = slice(pair * 128, (pair + 1) * 128)
+                x = raw[at, lane]
+                x = x * pair_scale(x, 1e-06) * gain_of(row, pair)
+                out[at, lane] = x.astype(BF16)
+            return carry
+
+        del scale
+        lax.fori_loop(0, raw.shape[0] // 64, body, 0)
+
+    def make_query():
+        query_raw[...] = bf_dot(hidden[...], fetch(0))
+        make_normed(query_raw, query, 4, None)
+
+    def make_key():
+        key_raw[...] = bf_dot(hidden[...], fetch(1))
+        make_normed(key_raw, key, 5, None)
+
+    def make_value():
+        value[...] = bf_dot(hidden[...], fetch(2)).astype(BF16)
+
+    def cap_near_rows():
+        whole = cap_near[...]
+        return whole.reshape(cap_rows, whole.shape[-1])
+
+    def make_cap_key():
+        cap_raw[...] = bf_dot(cap_near_rows(), fetch(3))
+        make_normed(cap_raw, cap_key, 6, None)
+
+    def make_cap_value():
+        cap_value[...] = bf_dot(cap_near_rows(), fetch(4)).astype(BF16)
+
+    def make_mixed(pair):
+        lane = slice(pair * 128, (pair + 1) * 128)
+        gate = jnp.tanh(gain_of(7, pair))
+        low = low_half((128, 128))
+        keys, cap_keys = key[:, lane], cap_key[:, lane]
+        values = jnp.concatenate([value[:, lane] * key_mask[...], key_mask[...]], axis=1)
+        cap_values = jnp.concatenate([cap_value[:, lane] * cap_mask[...], cap_mask[...]], axis=1)
+
+        def body(i, carry):
+            at = pl.ds(pl.multiple_of(i * 128, 128), 128)
+            q = query[at, lane] * jnp.asarray(HEAD_DIM**-0.5, BF16)
+            halves = (jnp.where(low, q, jnp.zeros_like(q)), jnp.where(low, jnp.zeros_like(q), q))
+            found = []
+            for k, v in ((keys, values), (cap_keys, cap_values)):
+                outs = []
+                for half in halves:
+                    weights = jnp.exp(right_dot(half, k))
+                    outs.append(bf_dot(weights.astype(BF16), v))
+                out = jnp.where(low, outs[0][:, :128], outs[1][:, :128])
+                norm = 1.0 / jnp.where(low, outs[0][:, 128:], outs[1][:, 128:])
+                found.append(out * norm)
+            own, cross = found
+            cross_out[at, lane] = cross
+            mixed[at, lane] = (own + gate * cross).astype(BF16)
+            return carry
+
+        lax.fori_loop(0, rows // 128, body, 0)
+
+
+    def begin(i):
+        relay, j = items[i]
+        if relay is None:
+            depart(j)
+        else:
+            relay.start(j)
+
+    window = 2
+    for i in range(window):
+        begin(i)
+    for move in small_moves:
+        move.wait_recv()
+    small_own.wait()
+    small_next = []
+    for k in range(1, buckets):
+        peer = lax.rem(b + k, buckets)
+        small_next.append(go(copies.remote(small_all.at[b], small_all.at[b], peer, s)))
+    total = part[b]
+    for k, move in enumerate(mod_moves, 1):
+        move.wait_recv()
+        total = total + got_bucket[k]
+    mod_sum[...] = total
+    mod_next = []
+    for k in range(1, seq):
+        peer = lax.rem(s + k, seq)
+        mod_next.append(go(copies.remote(mod_sum, got_seq.at[k], b, peer)))
+
+    cap_out = copies.local(cap_near, cap_all)
+    pieces = {
+        7: [small_sums, make_hidden],
+        9: [make_query],
+        10: [make_key],
+        11: [make_value],
+        15: [cap_out.start, make_cap_key],
+    }
+    order = []
+    for i, (relay, j) in enumerate(items):
+        if relay is None:
+            arrived(j)
+        elif j <= seq - 2:
+            relay.sent(j)
+        if i + window < len(items):
+            begin(i + window)
+        if relay is None:
+            order.append(j)
+            stage_a(j)
+            if len(order) >= 2:
+                stage_b(order[-2])
+            if len(order) >= 3:
+                stage_c(order[-3])
+        for piece in pieces.get(i, ()):
+            piece()
+    stage_b(order[-1])
+    stage_c(order[-2])
+    make_cap_value()
+    make_mixed(0)
+    stage_c(order[-1])
+    for pair in range(1, pairs):
+        make_mixed(pair)
+    cap_out.wait()
+    for move in sent:
+        move.wait_send()
+
+
+def forward_all(buckets, seq, tokens, captions, small, slim, cond, w_mod, masks, shards, kinds):
+    any_spec = pl.BlockSpec(memory_space=pl.ANY)
+    vmem = pl.BlockSpec(memory_space=pltpu.VMEM)
+    fulls = []
+    for shard, kind in zip(shards, kinds, strict=True):
+        rows, wide = shard.shape
+        shape = (buckets, rows, wide) if kind == "row" else (buckets, seq, rows, wide // seq)
+        fulls.append(jax.ShapeDtypeStruct(shape, BF16))
+    near = [pltpu.VMEM(full.shape, BF16) for full in fulls[:5]]
+    width = tokens.shape[1]
+    mod_lanes = w_mod.shape[1] // 8
+    span, cap_span, share = seq * tokens.shape[0], seq * captions.shape[0], width // seq
+    f32_rows = jax.ShapeDtypeStruct((span, share), F32)
+    low_rows = jax.ShapeDtypeStruct((span, share), BF16)
+    cap_low = jax.ShapeDtypeStruct((cap_span, share), BF16)
+    inner = [
+        jax.ShapeDtypeStruct((8, width), F32),
+        jax.ShapeDtypeStruct((8, width), F32),
+        jax.ShapeDtypeStruct((span, width), BF16),
+        f32_rows,
+        f32_rows,
+        jax.ShapeDtypeStruct((cap_span, share), F32),
+        low_rows,
+        low_rows,
+        low_rows,
+        cap_low,
+        cap_low,
+        f32_rows,
+        low_rows,
+    ]
+    n_sems = 64 + 16 * buckets + len(shards) * (seq + 2 * buckets)
+    outs = pl.pallas_call(
+        functools.partial(forward_kernel, buckets, seq, tuple(kinds), slim),
+        out_shape=[jax.ShapeDtypeStruct((seq,) + captions.shape, BF16), *fulls, *inner],
+        in_specs=[any_spec, any_spec, any_spec, vmem, vmem, vmem, vmem] + [any_spec] * len(shards),
+        out_specs=[any_spec] * (1 + len(shards)) + [vmem] * len(inner),
+        scratch_shapes=[
+            pltpu.VMEM((buckets, 8, mod_lanes), F32),
+            pltpu.VMEM((buckets, 8, mod_lanes), F32),
+            pltpu.VMEM((seq, 8, mod_lanes), F32),
+            pltpu.VMEM((8, mod_lanes), F32),
+            pltpu.VMEM((buckets, seq) + small.shape, F32),
+            pltpu.VMEM((seq,) + tokens.shape, BF16),
+            pltpu.VMEM((seq,) + captions.shape, BF16),
+            *near,
+            pltpu.SemaphoreType.DMA((n_sems,)),
+            pltpu.SemaphoreType.DMA((n_sems,)),
+        ],
+        compiler_params=pltpu.CompilerParams(
+            collective_id=9, has_side_effects=True, vmem_limit_bytes=56 * 2**20
+        ),
+    )(tokens, captions, small, cond, w_mod, *masks, *shards)
+    at = 1 + len(shards)
+    weights = [full.reshape(-1, full.shape[-1]) for full in outs[1:at]]
+    return outs[0], weights, outs[at:]
+
+
+def backward_kernel(buckets, seq, kinds, *refs):
+    count = len(kinds)
+    (
+        d_attn,
+        w_out,
+        w_query,
+        w_key,
+        w_value,
+        query,
+        key,
+        value,
+        cap_key,
+        cap_value,
+        cross_out,
+        query_raw,
+        key_raw,
+        cap_raw,
+        gain_rows,
+        key_bias,
+        cap_bias,
+    ) = refs[:17]
+    grads = refs[17 : 17 + count]
+    refs = refs[17 + count :]
+    d_hidden, d_query, d_key, d_value, d_cap_key, d_cap_value, own_sums = refs[:7]
+    outs = refs[7 : 7 + count]
+    refs = refs[7 + count :]
+    mixed_low, cross_low, query_acc, key_acc, value_acc, cap_key_acc, cap_value_acc = refs[:7]
+    parts, from_left, from_right, send, recv = refs[7:12]
+    b, s = lax.axis_index("bucket"), lax.axis_index("seq")
+    copies = Copies(send, recv)
+    sums = GradSums(copies, b, s, buckets, seq, kinds, grads, outs, refs[12:])
+    peers = greet_all(b, s, buckets, seq)
+    pl.semaphore_wait(pltpu.get_barrier_semaphore(), peers)
+    for w in range(min(2, count)):
+        sums.begin(w)
+    steps = sums.steps()
+
+    def advance(times=1):
+        for _ in range(times):
+            step = next(steps, None)
+            if step is not None:
+                step()
+
+    rows, share = query.shape
+    pairs = share // 128
+    span_block = 256
+    scale = HEAD_DIM**-0.5
+
+    def gain_of(row, pair):
+        at = pl.multiple_of(s * share + pair * 128, 128)
+        return gain_rows[row : row + 1, pl.ds(at, 128)]
+
+    weights = w_out[...]
+    mixed_low[...] = right_dot(d_attn[...], weights.reshape(share, weights.shape[-1])).astype(BF16)
+    own_sums[...] = jnp.zeros_like(own_sums)
+    advance()
+
+    def cross_part(pair):
+        lane = slice(pair * 128, (pair + 1) * 128)
+        gate = jnp.tanh(gain_of(7, pair))
+
+        def body(i, total):
+            at = pl.ds(pl.multiple_of(i * 128, 128), 128)
+            d = mixed_low[at, lane].astype(F32)
+            cross_low[at, lane] = (gate * d).astype(BF16)
+            return total + jnp.sum(d * cross_out[at, lane], axis=0, keepdims=True)
+
+        total = lax.fori_loop(0, rows // 128, body, jnp.zeros((1, 128), F32))
+        own_sums[3:4, lane] = total * (1.0 - gate * gate)
+
+    def attend_back(pair):
+        lane = slice(pair * 128, (pair + 1) * 128)
+        low = low_half((span_block, 128))
+        sides = (
+            (key, value, key_bias, mixed_low, key_acc, value_acc),
+            (cap_key, cap_value, cap_bias, cross_low, cap_key_acc, cap_value_acc),
+        )
+        turned = [side[0][:, lane].T for side in sides]
+        for side in sides:
+            side[4][:, lane] = jnp.zeros((side[4].shape[0], 128), F32)
+            side[5][:, lane] = jnp.zeros((side[5].shape[0], 128), F32)
+
+        def body(i, carry):
+            at = pl.ds(pl.multiple_of(i * span_block, span_block), span_block)
+            q = query[at, lane] * jnp.asarray(scale, BF16)
+            d_turned = None
+            for side, k_turned in zip(sides, turned, strict=True):
+                k_ref, v_ref, bias, d_ref, k_acc, v_acc = side
+                d = d_ref[at, lane]
+                found = []
+                for keep in (low, jnp.logical_not(low)):
+                    q_half = jnp.where(keep, q, jnp.zeros_like(q))
+                    d_half = jnp.where(keep, d, jnp.zeros_like(d))
+                    scores = right_dot(k_ref[:, lane], q_half)
+                    scores = scores + jnp.concatenate([bias[...], bias[...]], axis=1)
+                    weights = jnp.exp(scores)
+                    probs = weights * (1.0 / jnp.sum(weights, axis=0, keepdims=True))
+                    d_probs = right_dot(v_ref[:, lane], d_half)
+                    delta = jnp.sum(probs * d_probs, axis=0, keepdims=True)
+                    d_scores = (probs * (d_probs - delta)).astype(BF16)
+                    k_acc[:, lane] += bf_dot(d_scores, q_half)
+                    v_acc[:, lane] += bf_dot(probs.astype(BF16), d_half)
+                    found.append(bf_dot(k_turned, d_scores))
+                both = jnp.concatenate([found[0][:HEAD_DIM], found[1][HEAD_DIM:]], axis=0)
+                d_turned = both if d_turned is None else d_turned + both
+            query_acc[at, lane] = d_turned.T * scale
+            return carry
+
+        lax.fori_loop(0, rows // span_block, body, 0)
+
+    def norm_back(raw, d_norm, out, row, sum_row):
+        for pair in range(pairs):
+            lane = slice(pair * 128, (pair + 1) * 128)
+            gain = gain_of(row, pair)
+
+            def body(i, total):
+                at = pl.ds(pl.multiple_of(i * 64, 64), 64)
+                x, d = raw[at, lane], d_norm[at, lane]
+                size = pair_scale(x, 1e-06)
+                normed, inner = x * size, d * gain
+                low = low_half(x.shape)
+                product = inner * normed
+                first = jnp.sum(jnp.where(low, product, 0.0), axis=-1, keepdims=True)
+                second = jnp.sum(jnp.where(low, 0.0, product), axis=-1, keepdims=True)
+                mean = jnp.where(low, first, second) * (1.0 / HEAD_DIM)
+                out[at, lane] = (size * (inner - normed * mean)).astype(BF16)
+                return total + jnp.sum(d * normed, axis=0, keepdims=True)
+
+            total = lax.fori_loop(0, raw.shape[0] // 64, body, jnp.zeros((1, 128), F32))
+            own_sums[sum_row : sum_row + 1, lane] = total
+
+    for pair in range(pairs):
+        cross_part(pair)
+        attend_back(pair)
+        advance(2)
+    norm_back(query_raw, query_acc, d_query, 4, 0)
+    norm_back(key_raw, key_acc, d_key, 5, 1)
+    d_value[...] = value_acc[...].astype(BF16)
+    pour = Pour(copies, parts, from_left, from_right, b, s, seq)
+    width = parts.shape[-1]
+    wide = 512
+    for at in range(0, width, wide):
+        cols = slice(at, at + wide)
+        total = right_dot(d_query[...], w_query[cols, :]) + right_dot(d_key[...], w_key[cols, :])
+        total = total + right_dot(d_value[...], w_value[cols, :])
+        parts[:, :, cols] = total.astype(BF16).reshape(seq, rows // seq, wide)
+    for q in range(2):
+        pour.step(q)
+    norm_back(cap_raw, cap_key_acc, d_cap_key, 6, 2)
+    d_cap_value[...] = cap_value_acc[...].astype(BF16)
+    for q in range(2, pour.count):
+        pour.step(q)
+        advance()
+    pour.end(d_hidden)
+    for step in steps:
+        step()
+    sums.end()
+
+
+def backward_all(buckets, seq, rows, attention_refs, grads, kinds):
+    any_spec = pl.BlockSpec(memory_space=pl.ANY)
+    vmem = pl.BlockSpec(memory_space=pltpu.VMEM)
+    inputs, outs, scratch, n_sems = sums_shapes(buckets, seq, grads, kinds)
+    d_attn, query, cap_key = attention_refs[0], attention_refs[5], attention_refs[8]
+    width = d_attn.shape[1]
+    low = jax.ShapeDtypeStruct(query.shape, BF16)
+    cap_low = jax.ShapeDtypeStruct(cap_key.shape, BF16)
+    inner = [
+        jax.ShapeDtypeStruct((rows, width), F32),
+        low,
+        low,
+        low,
+        cap_low,
+        cap_low,
+        jax.ShapeDtypeStruct((8, query.shape[1]), F32),
+    ]
+    n_sems += 8 * seq
+    results = pl.pallas_call(
+        functools.partial(backward_kernel, buckets, seq, tuple(kinds)),
+        out_shape=[*inner, *outs],
+        in_specs=[vmem] * len(attention_refs) + [any_spec] * len(grads),
+        out_specs=[vmem] * (len(inner) + len(outs)),
+        scratch_shapes=[
+            pltpu.VMEM(query.shape, BF16),
+            pltpu.VMEM(query.shape, BF16),
+            pltpu.VMEM(query.shape, F32),
+            pltpu.VMEM(query.shape, F32),
+            pltpu.VMEM(query.shape, F32),
+            pltpu.VMEM(cap_key.shape, F32),
+            pltpu.VMEM(cap_key.shape, F32),
+            pltpu.VMEM((seq, rows, width), BF16),
+            pltpu.VMEM((seq - 1, rows, width), BF16),
+            pltpu.VMEM((seq - 1, rows, width), BF16),
+            pltpu.SemaphoreType.DMA((n_sems,)),
+            pltpu.SemaphoreType.DMA((n_sems,)),
+            *scratch,
+        ],
+        compiler_params=pltpu.CompilerParams(
+            collective_id=10, has_side_effects=True, vmem_limit_bytes=60 * 2**20
+        ),
+    )(*attention_refs, *inputs)
+    return results[:7], [out.reshape(-1, out.shape[-1]) for out in results[7:]]
 
 
 def on_device(
@@ -937,41 +1720,32 @@
     slim = gains.shape[1]
     small = jnp.concatenate([gains, cross_gate[None]], axis=0).astype(F32)
     small = jnp.pad(small, ((0, 0), (0, 128 - slim)))
-    tok_all, cap_all, small_all, mod, weights = gather_all(
+    key_mask = jnp.broadcast_to((jnp.arange(span) < live_rows)[:, None], (span, 128)).astype(BF16)
+    cap_span = captions.shape[0] * seq
+    cap_mask = jnp.broadcast_to((jnp.arange(cap_span) < cap_len)[:, None], (cap_span, 128))
+    cap_all, weights, inner = forward_all(
         buckets,
         seq,
         tokens,
         captions,
         small,
+        slim,
         cond_part,
         w_mod,
+        [key_mask, cap_mask.astype(BF16)],
         [w_query, w_key, w_value, w_cap_key, w_cap_value, w_out, w_gate, w_up, w_down],
         ["col", "col", "col", "col", "col", "row", "col", "col", "row"],
     )
     wq, wk, wv, wck, wcv, wo, wg, wu, wd = weights
     caps = cap_all.reshape(-1, captions.shape[1])
-    small_rows = small_all[..., :slim].transpose(2, 0, 1, 3).reshape(8, width)
+    small_rows, mod, hidden, query_proj, key_proj, cap_proj = inner[:6]
+    query, key, value, cap_key, cap_value = inner[6:11]
+    cross_out, mixed_low = inner[11:]
     gain_f = small_rows[:7]
     own_cols = lax.dynamic_slice_in_dim(small_rows, s * share, share, 1)
     gate_cross = jnp.tanh(own_cols[7])
-    scale_attn, gate_attn, scale_ffn, gate_ffn = mod.reshape(4, width)
-
-    hidden = pre_attn(tok_all.astype(F32), gain_f[0], scale_attn).astype(BF16).reshape(span, width)
-    query_proj, key_proj = bf_dot(hidden, wq), bf_dot(hidden, wk)
-    value_low = bf_dot(hidden, wv).astype(BF16)
-    (query_f, key_f), norm_back = jax.vjp(qk_norm, query_proj, key_proj, own_cols[4], own_cols[5])
-    cap_key_f, cap_back = jax.vjp(cap_norm, bf_dot(caps, wck), own_cols[6])
-
-    def by_head(values):
-        return values.astype(BF16).reshape(values.shape[0], heads, HEAD_DIM)
-
-    query, key, value = by_head(query_f), by_head(key_f), by_head(value_low)
-    cap_key, cap_value = by_head(cap_key_f), by_head(bf_dot(caps, wcv))
-    probs, self_out = attention(query, key, value, jnp.arange(span) < live_rows, scale)
-    cap_live = jnp.arange(caps.shape[0]) < cap_len
-    cap_probs, cross_out = attention(query, cap_key, cap_value, cap_live, scale)
-    self_out, cross_out = self_out.reshape(span, share), cross_out.reshape(span, share)
-    mixed_low = (self_out + gate_cross * cross_out).astype(BF16)
+    scale_attn, gate_attn, scale_ffn, gate_ffn = mod[0], mod[1], mod[2], mod[3]
+
     attn_out = line_scatter(seq, bf_dot(mixed_low, wo), 2)
 
     tokens_f = tokens.astype(F32)
@@ -996,31 +1770,45 @@
         (d_resid, d_hidden_ffn)
     )
     d_attn_all = line_gather(seq, d_attn_out.astype(BF16), 7)
-    d_mixed_low = right_dot(d_attn_all, wo).astype(BF16)
-    d_mixed = d_mixed_low.astype(F32)
-    d_cross_low = (gate_cross * d_mixed).astype(BF16)
-    grad_cross = jnp.sum(d_mixed * cross_out, axis=0) * (1.0 - gate_cross * gate_cross)
-
-    d_query_cross, d_cap_key, d_cap_value = attention_back(
-        cap_probs, query, cap_key, cap_value, by_head(d_cross_low), scale
+    key_bias = jnp.where(jnp.arange(span) < live_rows, 0.0, -1e30).astype(F32)
+    cap_bias = jnp.where(jnp.arange(cap_span) < cap_len, 0.0, -1e30).astype(F32)
+    (d_hidden, d_query, d_key, d_value, d_cap_key, d_cap_value, own_sums), early = backward_all(
+        buckets,
+        seq,
+        rows,
+        [
+            d_attn_all,
+            wo.reshape(buckets, -1, width),
+            wq,
+            wk,
+            wv,
+            query,
+            key,
+            value,
+            cap_key,
+            cap_value,
+            cross_out,
+            query_proj,
+            key_proj,
+            cap_proj,
+            small_rows,
+            jnp.broadcast_to(key_bias[:, None], (span, 128)),
+            jnp.broadcast_to(cap_bias[:, None], (cap_span, 128)),
+        ],
+        [
+            left_dot(ffn_all, d_gate),
+            left_dot(ffn_all, d_up),
+            left_dot(act_low, d_ffn_all),
+            left_dot(mixed_low, d_attn_all),
+        ],
+        ["col", "col", "row", "row"],
     )
-    d_query, d_key, d_value = attention_back(probs, query, key, value, by_head(d_mixed_low), scale)
-    d_cap_key, d_gain_cap = cap_back(d_cap_key.reshape(-1, share))
-    d_query, d_key, d_gain_query, d_gain_key = norm_back(
-        ((d_query + d_query_cross).reshape(span, share), d_key.reshape(span, share))
-    )
-    d_query, d_key, d_cap_key = d_query.astype(BF16), d_key.astype(BF16), d_cap_key.astype(BF16)
-    d_value = d_value.reshape(span, share).astype(BF16)
-    d_cap_value = d_cap_value.reshape(-1, share).astype(BF16)
-    d_hidden = line_scatter(
-        seq, right_dot(d_query, wq) + right_dot(d_key, wk) + right_dot(d_value, wv), 8
-    )
+    s_gate, s_up, s_down, s_out = early
     _, pre_back = jax.vjp(pre_attn, tokens_f, gain_f[0], scale_attn)
     d_tokens_two, d_gain_pre, d_scale_attn = pre_back(d_hidden)
     tokens_grad = d_tokens_one + d_tokens_two
 
-    own_sums = jnp.stack([d_gain_query, d_gain_key, d_gain_cap, grad_cross])
-    own_wide = lax.dynamic_update_slice(jnp.zeros((4, width), F32), own_sums, (0, s * share))
+    own_wide = lax.dynamic_update_slice(jnp.zeros((4, width), F32), own_sums[:4], (0, s * share))
     vec = jnp.concatenate(
         [
             jnp.stack([d_scale_attn, d_gate_attn, d_scale_ffn, d_gate_ffn]),
@@ -1030,19 +1818,14 @@
         ]
     )
     grads = [
-        left_dot(ffn_all, d_gate),
-        left_dot(ffn_all, d_up),
-        left_dot(act_low, d_ffn_all),
-        left_dot(mixed_low, d_attn_all),
         left_dot(caps, d_cap_key),
         left_dot(caps, d_cap_value),
         left_dot(hidden, d_query),
         left_dot(hidden, d_key),
         left_dot(hidden, d_value),
     ]
-    kinds = ["col", "col", "row", "row", "col", "col", "col", "col", "col"]
-    vec_all, sums = scatter_all(buckets, seq, vec, grads, kinds)
-    s_gate, s_up, s_down, s_out, s_cap_key, s_cap_value, s_query, s_key, s_value = sums
+    vec_all, sums = scatter_all(buckets, seq, vec, grads, ["col"] * 5)
+    s_cap_key, s_cap_value, s_query, s_key, s_value = sums
 
     quarter = 4 * width // seq
     mod_rows = vec_all[:, :4].reshape(buckets, -1, quarter)
@@ -1086,6 +1869,14 @@
         P(None, ("bucket", "seq")),
         P(("bucket", "seq")),
     )
+    buckets, seq = mesh.shape["bucket"], mesh.shape["seq"]
+
+    def step(*args):
+        tokens, weight = args[0], args[6]
+        tiled = weight.shape[0] % 16 == 0 and weight.shape[1] // seq % 128 == 0
+        fits = buckets == 8 and seq == 4 and tokens.shape[0] % 64 == 0
+        return (on_device if tiled and fits else on_device_general)(*args)
+
     return jax.shard_map(
-        on_device, mesh=mesh, in_specs=in_specs, out_specs=out_specs, check_vma=False
+        step, mesh=mesh, in_specs=in_specs, out_specs=out_specs, check_vma=False
     )

time: 689 us -> 605 us (0.88)
  local copies, waits for them, and re-layouts: 65.1 us -> 18.3 us
  matrix products: 91.9 us -> 47.4 us
  Pallas kernels: 488 us -> 504 us
  other arithmetic: 34.3 us -> 24 us
    pallas_call x1 -> x2, Pallas kernels: 167 us -> 263 us  [the longest x1 177 us: forward_all(): pl.pallas_call(functools.partial(forward_kernel, buckets, seq, tuple(kind...]
    pallas_call x1, Pallas kernels: 118 us -> 69.7 us  [scatter_all(): pl.pallas_call(functools.partial(scatter_kernel, buckets, seq, tuple(kind...]
    pallas_call x4 -> x3, Pallas kernels: 125 us -> 85.9 us  [line_scatter(): pl.pallas_call(functools.partial(line_scatter_kernel, seq), out_shape=jax...]
    unnamed x272 -> x120, local copies, waits for them, and re-layouts: 44.9 us -> 9.77 us
    dot_general x10 -> x0, matrix products: 16.4 us -> none  [the longest x2 7.03 us: attention(): jnp.einsum('hqk,khd->qhd', probs.astype(BF16), values, preferred_element_...]
    dot_general x9 -> x4, matrix products: 22.9 us -> 11.7 us  [bf_dot(): return jnp.dot(left, right, preferred_element_type=F32)]
    sub x2 -> x0, matrix products: 9.6 us -> none  [attention(): probs = jax.nn.softmax(scores, axis=-1)]
    dot_general x3 -> x0, local copies, waits for them, and re-layouts: 8.33 us -> none  [bf_dot(): return jnp.dot(left, right, preferred_element_type=F32)]
where the time goes in v2:
time: 605 us; the launch traced here: 596 us
  Pallas kernels  504 us (83%)
  matrix products  47.4 us (8%)
  other arithmetic  24 us (4%)
  local copies, waits for them, and re-layouts  18.3 us (3%)
    pallas_call x1, Pallas kernels, forward_all(): pl.pallas_call(functools.partial(forward_kernel, buckets, seq, tuple(kind...  177 us
    pallas_call x1, Pallas kernels, backward_all(): pl.pallas_call(functools.partial(backward_kernel, buckets, seq, tuple(kin...  86.1 us
    pallas_call x3, Pallas kernels, line_scatter(): pl.pallas_call(functools.partial(line_scatter_kernel, seq), out_shape=jax...  85.9 us
    pallas_call x3, Pallas kernels, line_gather(): pl.pallas_call(functools.partial(line_gather_kernel, seq), out_shape=jax....  85.2 us
    pallas_call x1, Pallas kernels, scatter_all(): pl.pallas_call(functools.partial(scatter_kernel, buckets, seq, tuple(kind...  69.7 us
    dot_general x9, matrix products, left_dot(): lax.dot_general(rows_left, rows_right, (((0,), (0,)), ((), ())), preferre...  25.9 us

profile of v2, /device:TPU:8, one launch (start us, length us, event | category | flops | bytes accessed | tf_op | source)
XLA Modules:
  0.0 595.8 jit_solution(17009417608521004760)
XLA Ops:
  0.6 1.3 fusion.20.refs_2_
  2.0 0.7 convert_element_type.92
  2.8 0.7 constant_dynamic-slice_fusion.1.refs_3_
  3.5 1.4 fusion.33
  4.9 0.6 fusion.22
  5.5 0.8 broadcast_in_dim.41.refs_5_
  6.3 0.6 fusion.24
  6.9 0.7 broadcast_in_dim.42.refs_6_
  7.7 176.7 %shard_map.281 = (bf16[4,64,4096]{2,1,0:T(8,128)(2,1)}, bf16[8,4,48,384]{3,2,1,0:T(8,128)(2,1)}, bf16[8,4,48,384]{3,2,1,0:T(8,128)(2,1)}, bf16[8,4,48,384]{3,2,1...) custom-call(bf16[128,1536]{1,0:T(8,128)(2,1)} %refs_0_.1, ...), custom_call_target="tpu_custom_call" | custom-call | tf_op jit(solution)/shard_map/pallas_call | solution.py:1456
  184.4 1.6 slice_reduce_fusion
  186.0 2.4 convolution_convert_fusion.6
  188.4 29.9 %shard_map.282 = f32[128,1536]{1,0:T(8,128)S(1)} custom-call(bf16[4,128,1536]{2,1,0:T(8,128)(2,1)S(1)} %bitcast.64), custom_call_target="tpu_custom_call" | custom-call | tf_op jit(solution)/shard_map/pallas_call | solution.py:581
  219.0 0.6 add_reduce_fusion
  219.6 0.8 multiply_reduce_fusion.11
  220.4 0.9 multiply_convert_fusion.2.own
  221.3 33.0 %shard_map.283 = bf16[4,128,1536]{2,1,0:T(8,128)(2,1)} custom-call(bf16[128,1536]{1,0:T(8,128)(2,1)} %multiply_convert_fusion.2.own), custom_call_target="tpu_custom_call" | custom-call | tf_op jit(solution)/shard_map/pallas_call | solution.py:466
  254.3 4.3 fusion.34
  258.7 3.2 multiply_convert_fusion.1
  261.9 1.8 convolution_convert_fusion.5
  263.7 28.3 %shard_map.284 = f32[128,1536]{1,0:T(8,128)S(1)} custom-call(bf16[4,128,1536]{2,1,0:T(8,128)(2,1)S(1)} %bitcast.66), custom_call_target="tpu_custom_call" | custom-call | tf_op jit(solution)/shard_map/pallas_call | solution.py:581
  292.7 0.7 compare_convert_fusion
  293.5 1.0 multiply_reduce_fusion.1
  294.6 1.3 fusion.10
  295.9 26.6 %shard_map.285 = bf16[4,128,1536]{2,1,0:T(8,128)(2,1)} custom-call(bf16[128,1536]{1,0:T(8,128)(2,1)} %get-tuple-element.117.own), custom_call_target="tpu_custom_call" | custom-call | tf_op jit(solution)/shard_map/pallas_call | solution.py:466
  322.6 6.2 %multiply_convert_fusion = (bf16[512,1024]{1,0:T(8,128)(2,1)S(1)}, bf16[512,1024]{1,0:T(8,128)(2,1)S(1)}) fusion(f32[512,1024]{1,0:T(8,128)} %copy-done.49, f32[512,1024]{1,0:T(8,128)} %get-tuple-element.125, bf16[512,1536]{1,0:T(8,128)(2,1)} %bitcast.81, bf16[1024,1536]{1,0:T(8,128)(2,1)} %bitcast.99), kind=kOutput, calls=%fused_computation.18 | convolution fusion | flops 1617952768 | bytes 11010048 | tf_op jit(solution)/shard_map/dot_general | solution.py:48
  328.8 1.8 fusion.35
  330.6 0.8 copy-done.42
  331.4 1.8 fusion
  333.3 27.7 %shard_map.286 = f32[128,1536]{1,0:T(8,128)S(1)} custom-call(bf16[4,128,1536]{2,1,0:T(8,128)(2,1)S(1)} %bitcast.65), custom_call_target="tpu_custom_call" | custom-call | tf_op jit(solution)/shard_map/pallas_call | solution.py:581
  361.0 1.0 multiply_reduce_fusion.2
  362.1 2.2 multiply_reduce_fusion.3
  364.3 1.0 fusion.11.own
  365.2 25.6 %shard_map.287 = bf16[4,128,1536]{2,1,0:T(8,128)(2,1)} custom-call(bf16[128,1536]{1,0:T(8,128)(2,1)} %fusion.11.own), custom_call_target="tpu_custom_call" | custom-call | tf_op jit(solution)/shard_map/pallas_call | solution.py:466
  390.8 0.7 fusion.21
  391.5 0.8 broadcast_in_dim.81.refs_15_
  393.0 0.8 broadcast_in_dim.84.refs_16_
  393.7 4.8 convolution_convert_fusion.4
  398.6 3.5 convolution_convert_fusion.3
  402.1 3.5 convolution_convert_fusion.2
  405.7 1.8 convolution_convert_fusion.10
  407.5 86.1 %shard_map.288 = (f32[128,1536]{1,0:T(8,128)}, bf16[512,384]{1,0:T(8,128)(2,1)}, bf16[512,384]{1,0:T(8,128)(2,1)}, bf16[512,384]{1,0:T(8,128)(2,1)}, bf16[256,38...) custom-call(bf16[512,1536]{1,0:T(8,128)(2,1)} %bitcast.71, ...), custom_call_target="tpu_custom_call" | custom-call | tf_op jit(solution)/shard_map/pallas_call | solution.py:1659
  493.8 1.8 fusion.9
  495.6 2.3 fusion.12
  497.9 0.9 multiply_multiply_fusion.1
  498.9 1.3 concatenate.11.refs_0_
  500.3 3.0 convolution_convert_fusion.1
  503.2 3.0 convolution_convert_fusion
  506.3 2.0 convolution_convert_fusion.9
  508.3 2.1 convolution_convert_fusion.8
  510.4 2.1 convolution_convert_fusion.7
  512.5 69.7 %shard_map.289 = (f32[8,16,1536]{2,1,0:T(8,128)}, f32[512,384]{1,0:T(8,128)}, f32[512,384]{1,0:T(8,128)}, f32[192,384]{1,0:T(8,128)}, f32[192,384]{1,0:T(8,128)}, /*index=5*/f32[192,384]{1,0:T(8,128)}) custom-call(f32[16,1536]{1,0:T(8,128)} %concatenate.11.refs_0_, bf16[4,2,512,384]{3,2,1,0:T(8,128)(2,1)} %bitcast.67, bf16[4,2,512,384]{3,2,1,0:T(8,128)(2,1)} %bitcast.68, ...), custom_call_target="tpu_custom_call" | custom-call | tf_op jit(solution)/shard_map/pallas_call | solution.py:849
  582.2 1.1 slice.50
  583.5 0.7 dynamic-slice_convert_fusion
  584.1 1.4 multiply_reduce_fusion
  585.5 1.1 dynamic-slice_reduce_fusion
  587.1 1.7 copy.45
  588.8 0.7 copy.46
  589.5 0.7 copy.47
  590.3 0.7 copy.48
  591.0 0.9 copy.49
  591.9 0.9 copy.50
  592.7 0.9 copy.51
  593.6 0.9 copy.52
  594.5 0.9 copy.53
  (135 shorter events, 2.5 us)
Async XLA Ops:
  2.8 181.6 %copy-start.30 = (bf16[8,1024]{1,0:T(8,128)(2,1)}, bf16[8,1024]{1,0:T(8,128)(2,1)S(1)}, u32[]{:S(2)}) copy-start(bf16[8,1024]{1,0:T(8,128)(2,1)S(1)} %multiply_convert_fusion.3) | copy-start | bytes 49156
  186.0 175.0 %copy-start.19 = (f32[1536]{0:T(1024)}, f32[1536]{0:T(1024)S(1)}, u32[]{:S(2)}) copy-start(f32[1536]{0:T(1024)S(1)} %get-tuple-element.108) | copy-start | bytes 18436
  188.4 30.6 %copy-start.29 = (f32[8,1536]{1,0:T(8,128)S(1)}, f32[8,1536]{1,0:T(8,128)}, u32[]{:S(2)}) copy-start(f32[8,1536]{1,0:T(8,128)} %get-tuple-element.52) | copy-start | bytes 147460
  188.4 31.2 %copy-start.2 = (bf16[128,1536]{1,0:T(8,128)(2,1)S(1)}, bf16[128,1536]{1,0:T(8,128)(2,1)}, u32[]{:S(2)}) copy-start(bf16[128,1536]{1,0:T(8,128)(2,1)} %refs_0_.1) | copy-start | bytes 1179652
  218.4 0.5 copy-start.38
  219.0 35.3 %copy-start.34 = (f32[128]{0:T(128)}, f32[128]{0:T(128)S(1)}, u32[]{:S(2)}) copy-start(f32[128]{0:T(128)S(1)} %fusion.29) | copy-start | bytes 1540
  219.6 141.4 %copy-start.20 = (f32[1536]{0:T(1024)}, f32[1536]{0:T(1024)S(1)}, u32[]{:S(2)}) copy-start(f32[1536]{0:T(1024)S(1)} %get-tuple-element.103) | copy-start | bytes 18436
  220.4 140.6 %copy-start.31 = (f32[128]{0:T(128)}, f32[128]{0:T(128)S(1)}, u32[]{:S(2)}) copy-start(f32[128]{0:T(128)S(1)} %fusion.30) | copy-start | bytes 1540
  254.3 4.3 copy-start.5
  254.3 4.3 copy-start.41
  258.6 3.2 copy-start.49
  258.7 3.2 copy-start.44
  261.9 1.8 copy-start.51
  263.7 29.9 %copy-start.3 = (bf16[128,1536]{1,0:T(8,128)(2,1)S(1)}, bf16[128,1536]{1,0:T(8,128)(2,1)}, u32[]{:S(2)}) copy-start(bf16[128,1536]{1,0:T(8,128)(2,1)} %param.20) | copy-start | bytes 1179652
  293.4 2.6 copy-start.32
  322.6 6.2 %copy-start.43 = (bf16[8,4,48,1024]{3,2,1,0:T(8,128)(2,1)S(1)}, bf16[8,4,48,1024]{3,2,1,0:T(8,128)(2,1)}, u32[]{:S(2)}) copy-start(bf16[8,4,48,1024]{3,2,1,0:T(8,128)(2,1)} %get-tuple-element.56) | copy-start | bytes 9437188
  328.7 1.9 copy-start.50
  328.7 1.9 copy-start.53
  328.8 2.6 copy-start.42
  333.2 28.8 %copy-start.4 = (bf16[128,1536]{1,0:T(8,128)(2,1)S(1)}, bf16[128,1536]{1,0:T(8,128)(2,1)}, u32[]{:S(2)}) copy-start(bf16[128,1536]{1,0:T(8,128)(2,1)} %param.20) | copy-start | bytes 1179652
  333.2 28.8 %copy-start.33 = (f32[128]{0:T(128)S(1)}, f32[128]{0:T(128)}, u32[]{:S(2)}) copy-start(f32[128]{0:T(128)} %copy-done.32) | copy-start | bytes 1540
  333.3 28.8 %copy-start.35 = (f32[128]{0:T(128)S(1)}, f32[128]{0:T(128)}, u32[]{:S(2)}) copy-start(f32[128]{0:T(128)} %copy-done.34) | copy-start | bytes 1540
  362.1 2.2 copy-start.39
  364.3 29.5 %copy-start.6 = (bf16[4,128,1536]{2,1,0:T(8,128)(2,1)S(1)}, bf16[4,128,1536]{2,1,0:T(8,128)(2,1)}, u32[]{:S(2)}) copy-start(bf16[4,128,1536]{2,1,0:T(8,128)(2,1)} %shard_map.283) | copy-start | bytes 4718596
  393.7 4.8 copy-start.54
  398.6 3.6 copy-start.7
  398.6 3.6 copy-start.52
  402.1 3.6 copy-start.1
  402.1 3.6 copy-start.13
  407.5 86.2 %copy-start.40 = (f32[128]{0:T(128)S(1)}, f32[128]{0:T(128)}, u32[]{:S(2)}) copy-start(f32[128]{0:T(128)} %get-tuple-element.119) | copy-start | bytes 1540
  407.5 86.3 %copy-start.21 = (f32[1536]{0:T(1024)S(1)}, f32[1536]{0:T(1024)}, u32[]{:S(2)}) copy-start(f32[1536]{0:T(1024)} %get-tuple-element.106) | copy-start | bytes 18436
  407.5 86.3 %copy-start.22 = (f32[1536]{0:T(1024)S(1)}, f32[1536]{0:T(1024)}, u32[]{:S(2)}) copy-start(f32[1536]{0:T(1024)} %get-tuple-element.102) | copy-start | bytes 18436
  493.7 4.2 copy-start.23
  493.7 4.2 copy-start.24
  493.7 5.1 copy-start.27
  493.7 5.1 copy-start.28
  493.7 5.1 copy-start.26
  493.7 5.1 copy-start.25
  493.7 5.2 copy-start.37
  493.8 6.5 %copy-start = (bf16[4,64,4096]{2,1,0:T(8,128)(2,1)S(1)}, bf16[4,64,4096]{2,1,0:T(8,128)(2,1)}, u32[]{:S(2)}) copy-start(bf16[4,64,4096]{2,1,0:T(8,128)(2,1)} %get-tuple-element.73) | copy-start | bytes 6291460
  493.8 6.5 %copy-start.18 = (bf16[256,384]{1,0:T(8,128)(2,1)S(1)}, bf16[256,384]{1,0:T(8,128)(2,1)}, u32[]{:S(2)}) copy-start(bf16[256,384]{1,0:T(8,128)(2,1)} %get-tuple-element.74) | copy-start | bytes 589828
  500.3 3.0 copy-start.17
  503.2 3.0 copy-start.45
  503.2 3.0 copy-start.48
  506.3 2.1 copy-start.47
  508.3 2.1 copy-start.46
  582.2 6.6 %copy-start.16 = (f32[192,384]{1,0:T(8,128)S(1)}, f32[192,384]{1,0:T(8,128)}, u32[]{:S(2)}) copy-start(f32[192,384]{1,0:T(8,128)} %get-tuple-element.144) | copy-start | bytes 884740
  582.2 7.3 %copy-start.15 = (f32[192,384]{1,0:T(8,128)S(1)}, f32[192,384]{1,0:T(8,128)}, u32[]{:S(2)}) copy-start(f32[192,384]{1,0:T(8,128)} %get-tuple-element.145) | copy-start | bytes 884740
  582.2 8.0 %copy-start.14 = (f32[4,48,384]{2,1,0:T(8,128)S(1)}, f32[4,48,384]{2,1,0:T(8,128)}, u32[]{:S(2)}) copy-start(f32[4,48,384]{2,1,0:T(8,128)} %get-tuple-element.83) | copy-start | bytes 884740
  582.2 8.7 %copy-start.12 = (f32[512,384]{1,0:T(8,128)S(1)}, f32[512,384]{1,0:T(8,128)}, u32[]{:S(2)}) copy-start(f32[512,384]{1,0:T(8,128)} %get-tuple-element.147) | copy-start | bytes 2359300
  585.5 6.3 %copy-start.11 = (f32[512,384]{1,0:T(8,128)S(1)}, f32[512,384]{1,0:T(8,128)}, u32[]{:S(2)}) copy-start(f32[512,384]{1,0:T(8,128)} %get-tuple-element.148) | copy-start | bytes 2359300
  586.6 6.1 %copy-start.36 = (f32[8,48]{1,0:T(8,128)}, f32[8,48]{1,0:T(8,128)S(1)}, u32[]{:S(2)}) copy-start(f32[8,48]{1,0:T(8,128)S(1)} %dynamic-slice_reduce_fusion) | copy-start | bytes 4612
  589.5 3.2 copy-start.10
  591.0 2.7 copy-start.9
  591.9 2.7 copy-start.8

commit v3 on v2

--- a/solution.py
+++ b/solution.py
@@ -11,6 +11,7 @@
 HEAD_DIM = 64
 MESH = pl.DeviceIdType.MESH
 F32, BF16 = jnp.float32, jnp.bfloat16
+CHUNKS, CUTS, FLIGHT = 2, 2, 2
 
 
 def rms_rows(values):
@@ -75,6 +76,13 @@
 
 def flip(index, bit):
     return index + bit - 2 * bit * lax.rem(lax.div(index, bit), 2)
+
+
+def slot(index, buckets):
+    if buckets != 8:
+        return index
+    high, low = lax.div(index, 4), lax.rem(index, 4)
+    return 4 * high + 2 * lax.rem(low, 2) + lax.div(low, 2)
 
 
 class Copies:
@@ -112,17 +120,19 @@
 
 
 class Relay:
-    def __init__(self, copies, own, out, b, s, seq):
+    def __init__(self, copies, own, out, b, s, seq, part=None):
         self.copies, self.own, self.out, self.b, self.s, self.seq = copies, own, out, b, s, seq
+        self.part = part
         self.base = {1: copies.take(seq - 1), -1: copies.take(seq - 1)}
         self.up = jnp.where(s < seq - 1, s + 1, s - 1)
         self.down = jnp.where(s > 0, s - 1, s + 1)
-        self.kept = copies.local(own, out.at[s])
+        self.kept = None if own is None else copies.local(own, out.at[s])
 
     def packet(self, way, j):
-        block = self.out.at[self.s - way * j]
+        at = self.s - way * j
+        block = self.out.at[at] if self.part is None else self.out.at[at, self.part]
         return self.copies.remote(
-            self.own if j == 0 else block,
+            self.own if j == 0 and self.own is not None else block,
             block,
             self.b,
             self.up if way > 0 else self.down,
@@ -136,20 +146,23 @@
         return self.s >= j if way > 0 else self.s + j <= self.seq - 1
 
     def start(self, j):
-        if j == 0:
+        if j == 0 and self.kept is not None:
             self.kept.start()
         for way in (1, -1):
-            if j > 0:
-
-                @pl.when(self.has(way, j))
+            if j == self.seq - 1:
+
+                @pl.when(jnp.logical_not(self.sends(way)))
                 def _():
+                    for k in range(self.seq - 1):
+                        self.packet(way, k).wait_recv()
+
+                continue
+
+            @pl.when(jnp.logical_and(self.sends(way), self.has(way, j)))
+            def _():
+                if j > 0:
                     self.packet(way, j - 1).wait_recv()
-
-            if j <= self.seq - 2:
-
-                @pl.when(jnp.logical_and(self.sends(way), self.has(way, j)))
-                def _():
-                    self.packet(way, j).start()
+                self.packet(way, j).start()
 
     def sent(self, j):
         for way in (1, -1):
@@ -158,7 +171,7 @@
             def _():
                 self.packet(way, j).wait_send()
 
-        if j == 0:
+        if j == 0 and self.kept is not None:
             self.kept.wait()
 
 
@@ -493,7 +506,7 @@
         self.copies, self.parts, self.b, self.s, self.seq = copies, parts, b, s, seq
         self.got = {1: from_left, -1: from_right}
         rows = parts.shape[1]
-        self.cuts = 2 if rows % 32 == 0 else 1
+        self.cuts = CUTS if rows % (16 * CUTS) == 0 else 1
         self.thin = rows // self.cuts
         self.count = (seq - 1) * self.cuts
         self.base = {1: copies.take(self.count), -1: copies.take(self.count)}
@@ -527,8 +540,8 @@
 
         @pl.when(self.on(way, q))
         def _():
-            if q >= 2:
-                self.packet(way, q - 2).wait_send()
+            if q >= FLIGHT:
+                self.packet(way, q - FLIGHT).wait_send()
             self.packet(way, q).start()
 
     def step(self, q):
@@ -557,9 +570,9 @@
                 add_rows(out, terms)
 
         for q in range(self.count):
-            more = q + 2 < self.count
+            more = q + FLIGHT < self.count
             for way in (1, -1):
-                last = jnp.logical_not(self.on(way, q + 2)) if more else True
+                last = jnp.logical_not(self.on(way, q + FLIGHT)) if more else True
 
                 @pl.when(jnp.logical_and(self.on(way, q), last))
                 def _():
@@ -597,13 +610,14 @@
 
 
 class GradSums:
-    def __init__(self, copies, b, s, buckets, seq, kinds, grads, outs, scratch):
+    def __init__(self, copies, b, s, buckets, seq, kinds, grads, outs, scratch, near=False):
+        self.near = near
         self.copies, self.b, self.s, self.buckets, self.seq = copies, b, s, buckets, seq
         self.kinds, self.grads, self.outs = kinds, grads, outs
         self.scratch = [scratch[8 * w : 8 * w + 8] for w in range(len(kinds))]
         self.chips = buckets // 2
         self.chip, self.core = lax.div(b, 2), lax.rem(b, 2)
-        self.place = s * buckets + b
+        self.place = s * buckets + slot(b, buckets)
         self.to_b = lax.div(self.place, seq)
         self.twin = flip(b, 1)
         self.begun, self.state, self.last = {}, {}, {}
@@ -614,36 +628,45 @@
         self.sent.append(copy)
         return copy
 
+    def own(self, w, chip, rows=None):
+        where = (chip,) if rows is None else (chip, rows)
+        if self.near:
+            return self.grads[w].at[(chip, self.core, *where[1:])]
+        return self.scratch[w][0].at[where]
+
     def begin(self, w):
         own, other = self.scratch[w][:2]
         grad = self.grads[w]
         swap = self.copies.remote(grad.at[:, 1 - self.core], other, self.twin, self.s)
-        keep = self.copies.local(grad.at[:, self.core], own)
         swap.start()
-        keep.start()
-        self.begun[w] = (swap, keep)
+        self.begun[w] = [swap]
+        if not self.near:
+            keep = self.copies.local(grad.at[:, self.core], own)
+            keep.start()
+            self.begun[w].append(keep)
 
     def stage_a(self, w):
-        own, other, half_x, half_y, got, _ = self.scratch[w][:6]
+        _, other, half_x, half_y, got, _ = self.scratch[w][:6]
         for copy in self.begun[w]:
             copy.wait()
-        if w + 2 in range(len(self.kinds)) and w + 2 not in self.begun:
+        if not self.near and w + 2 in range(len(self.kinds)) and w + 2 not in self.begun:
             self.begin(w + 2)
-        rows = own.shape[1]
+        rows = other.shape[1]
         if self.chips != 4:
             moves = []
             for k in range(1, self.chips):
                 to = lax.rem(self.chip + k, self.chips)
-                add_rows(own.at[to], [own.at[to], other.at[to]])
-                move = self.copies.remote(own.at[to], got.at[k], 2 * to + self.core, self.s)
+                own = self.own(w, to)
+                add_rows(own, [own, other.at[to]])
+                move = self.copies.remote(own, got.at[k], 2 * to + self.core, self.s)
                 moves.append(self.go(move))
             self.state[w] = moves
             return
         far = flip(flip(self.chip, 1), 2)
-        add_rows(own.at[far], [own.at[far], other.at[far]])
-        cut = halves_of(own.shape[1:])
+        add_rows(self.own(w, far), [self.own(w, far), other.at[far]])
+        cut = halves_of(other.shape[1:])
         near_x, near_y = flip(self.b, 2), flip(self.b, 4)
-        top, low = own.at[far, pl.ds(0, cut)], own.at[far, pl.ds(cut, rows - cut)]
+        top, low = self.own(w, far, pl.ds(0, cut)), self.own(w, far, pl.ds(cut, rows - cut))
         self.state[w] = [
             self.go(self.copies.remote(top, half_x, near_x, self.s)),
             self.go(self.copies.remote(low, half_y, near_y, self.s)),
@@ -652,27 +675,33 @@
     def stage_b(self, w):
         if self.chips != 4:
             return
-        own, other, half_x, half_y, got_x, got_y = self.scratch[w][:6]
-        rows = own.shape[1]
-        cut = halves_of(own.shape[1:])
+        _, other, half_x, half_y, got_x, got_y = self.scratch[w][:6]
+        rows = other.shape[1]
+        cut = halves_of(other.shape[1:])
         top, low = pl.ds(0, cut), pl.ds(cut, rows - cut)
         mx, my = flip(self.chip, 1), flip(self.chip, 2)
         move_x, move_y = self.state[w]
         move_x.wait_recv()
-        add_rows(own.at[my, top], [own.at[my, top], other.at[my, top], half_x])
-        add_rows(own.at[my, low], [own.at[my, low], other.at[my, low]])
-        next_y = self.go(self.copies.remote(own.at[my], got_y, flip(self.b, 4), self.s))
+        block = self.own(w, my, top)
+        add_rows(block, [block, other.at[my, top], half_x])
+        block = self.own(w, my, low)
+        add_rows(block, [block, other.at[my, low]])
+        block = self.own(w, my)
+        next_y = self.go(self.copies.remote(block, got_y, flip(self.b, 4), self.s))
         move_y.wait_recv()
-        add_rows(own.at[mx, low], [own.at[mx, low], other.at[mx, low], half_y])
-        add_rows(own.at[mx, top], [own.at[mx, top], other.at[mx, top]])
-        next_x = self.go(self.copies.remote(own.at[mx], got_x, flip(self.b, 2), self.s))
+        block = self.own(w, mx, low)
+        add_rows(block, [block, other.at[mx, low], half_y])
+        block = self.own(w, mx, top)
+        add_rows(block, [block, other.at[mx, top]])
+        block = self.own(w, mx)
+        next_x = self.go(self.copies.remote(block, got_x, flip(self.b, 2), self.s))
         self.state[w] = [next_x, next_y]
 
     def stage_c(self, w):
-        own, other, _, _, got_x, got_y, done, landed = self.scratch[w]
+        _, other, _, _, got_x, got_y, done, landed = self.scratch[w]
         for move in self.state[w]:
             move.wait_recv()
-        terms = [own.at[self.chip], other.at[self.chip]]
+        terms = [self.own(w, self.chip), other.at[self.chip]]
         if self.chips == 4:
             terms += [got_x, got_y]
         else:
@@ -729,7 +758,8 @@
         out, seq, buckets = self.outs[w], self.seq, self.buckets
         for j in range(seq):
             d = self.b * seq + j
-            here = jnp.logical_and(lax.rem(d, buckets) == self.b, lax.div(d, buckets) == self.s)
+            from_b = slot(lax.rem(d, buckets), buckets)
+            here = jnp.logical_and(from_b == self.b, lax.div(d, buckets) == self.s)
 
             @pl.when(jnp.logical_not(here))
             def _():
@@ -778,25 +808,26 @@
         greet(b, lax.rem(s + k, seq))
     for j in range(seq):
         d = b * seq + j
-        src_b, src_s = lax.rem(d, buckets), lax.div(d, buckets)
+        src_b, src_s = slot(lax.rem(d, buckets), buckets), lax.div(d, buckets)
 
         @pl.when(jnp.logical_not(jnp.logical_and(src_b == b, src_s == s)))
         def _():
             greet(src_b, src_s)
 
-    to_b = lax.div(s * buckets + b, seq)
+    to_b = lax.div(s * buckets + slot(b, buckets), seq)
     return buckets - 1 + seq - 1 + seq - jnp.where(to_b == b, 1, 0)
 
 
-def sums_shapes(buckets, seq, grads, kinds):
+def sums_shapes(buckets, seq, shapes, kinds, near=False):
     chips = buckets // 2
     inputs, outs, scratch = [], [], []
-    for grad, kind in zip(grads, kinds, strict=True):
-        rows, wide = grad.shape[0] // buckets, grad.shape[1]
-        inputs.append(grad.astype(BF16).reshape(chips, 2, rows, wide))
+    tiny = pltpu.VMEM((16, 128), BF16)
+    for (rows, wide), kind in zip(shapes, kinds, strict=True):
+        rows = rows // buckets
+        inputs.append((chips, 2, rows, wide))
         cut = halves_of((rows, wide))
-        tiny = pltpu.VMEM((16, 128), BF16)
-        scratch += [pltpu.VMEM((chips, rows, wide), BF16)] * 2
+        scratch += [tiny if near else pltpu.VMEM((chips, rows, wide), BF16)]
+        scratch += [pltpu.VMEM((chips, rows, wide), BF16)]
         if chips == 4:
             scratch += [pltpu.VMEM((cut, wide), BF16), pltpu.VMEM((rows - cut, wide), BF16)]
             scratch += [pltpu.VMEM((rows, wide), BF16)] * 2
@@ -805,8 +836,24 @@
         shape = (seq, rows, wide // seq) if kind == "row" else (rows, wide)
         outs.append(jax.ShapeDtypeStruct(shape, F32))
         scratch += [pltpu.VMEM(shape, BF16) if kind == "row" else tiny] * 2
-    n_sems = 32 + 2 * buckets + len(grads) * (8 + 3 * seq + buckets)
+    n_sems = 32 + 2 * buckets + len(shapes) * (8 + 3 * seq + buckets)
     return inputs, outs, scratch, n_sems
+
+
+def place_grads(buckets, grads, kinds, shapes):
+    inputs = []
+    for grad, kind, shape in zip(grads, kinds, shapes, strict=True):
+        grad = grad.astype(BF16)
+        if kind == "row" and buckets == 8:
+            grad = grad.reshape((2, 2, 2) + shape[2:]).transpose(0, 2, 1, 3, 4)
+        inputs.append(grad.reshape(shape))
+    return inputs
+
+
+def spread(buckets):
+    if buckets != 8:
+        return tuple(range(buckets))
+    return tuple(4 * (p // 4) + 2 * (p % 2) + p // 2 % 2 for p in range(buckets))
 
 
 def scatter_kernel(buckets, seq, kinds, *refs):
@@ -845,7 +892,8 @@
 def scatter_all(buckets, seq, vec, grads, kinds, collective_id=1):
     any_spec = pl.BlockSpec(memory_space=pl.ANY)
     vmem = pl.BlockSpec(memory_space=pltpu.VMEM)
-    inputs, outs, scratch, n_sems = sums_shapes(buckets, seq, grads, kinds)
+    shapes, outs, scratch, n_sems = sums_shapes(buckets, seq, [g.shape for g in grads], kinds)
+    inputs = place_grads(buckets, grads, kinds, shapes)
     results = pl.pallas_call(
         functools.partial(scatter_kernel, buckets, seq, tuple(kinds)),
         out_shape=[jax.ShapeDtypeStruct((buckets,) + vec.shape, F32), *outs],
@@ -1065,7 +1113,9 @@
     return lax.rsqrt(jnp.where(low, first, second) * (1.0 / HEAD_DIM) + eps)
 
 
-FORWARD_ORDER = ("tok", 0, "tok", 1, "tok", 2, "tok", 5, 3, "cap", 4, "cap", 6, "cap", 7, "cap", 8)
+FORWARD_ORDER = ("tok", 0, "tok", 1, "tok", 2, "tok", 6, 7, "cap", 8, 3, "cap", 4, "cap", 5, "cap")
+LAG = 1
+WINDOW = 2
 
 
 def forward_kernel(buckets, seq, kinds, slim, *refs):
@@ -1092,14 +1142,15 @@
         mixed,
     ) = refs[:13]
     refs = refs[13:]
-    part, got_bucket, got_seq, mod_sum, small_all, tok_all, cap_near = refs[:7]
-    near = refs[7:12]
-    send, recv = refs[12:]
+    part, got_bucket, got_seq, mod_sum, small_all, tok_all, cap_near, own_out = refs[:8]
+    near = refs[8:13]
+    send, recv = refs[13:]
     b, s = lax.axis_index("bucket"), lax.axis_index("seq")
     copies = Copies(send, recv)
     place = b * seq + s
-    to_b, to_s = lax.rem(place, buckets), lax.div(place, buckets)
-    back = s * buckets + b
+    to_slot, to_s = lax.rem(place, buckets), lax.div(place, buckets)
+    to_b = slot(to_slot, buckets)
+    back = s * buckets + slot(b, buckets)
     from_b, from_s = lax.div(back, seq), lax.rem(back, seq)
     stays = jnp.logical_and(to_b == b, to_s == s)
 
@@ -1152,8 +1203,8 @@
     def depart(at):
         kind, shard, full = kinds[at], shards[at], fulls[at]
         if kind == "row":
-            move = copies.remote(shard, full.at[to_b], to_b, to_s)
-            keep = copies.local(shard, full.at[b])
+            move = copies.remote(shard, full.at[to_slot], to_b, to_s)
+            keep = copies.local(shard, full.at[slot(b, buckets)])
 
             @pl.when(jnp.logical_not(stays))
             def _():
@@ -1202,26 +1253,29 @@
     far = flip(near_x, 4)
     second = [None] * count
 
+    def index(at, device):
+        return slot(device, buckets) if kinds[at] == "row" else device
+
     def stage_a(at):
-        full = fulls[at]
+        block = fulls[at].at[index(at, b)]
         second[at] = {
-            "x": go(copies.remote(full.at[b], full.at[b], near_x, s)),
-            "y": go(copies.remote(full.at[b], full.at[b], near_y, s)),
-            "twin": [go(copies.remote(full.at[b], full.at[b], twin, s))],
+            "x": go(copies.remote(block, block, near_x, s)),
+            "y": go(copies.remote(block, block, near_y, s)),
+            "twin": [go(copies.remote(block, block, twin, s))],
         }
 
     def stage_b(at):
         full, now = fulls[at], second[at]
         cut = halves_of(full.shape[1:])
         now["x"].wait_recv()
-        block = full.at[near_x, pl.ds(0, cut)]
+        block = full.at[index(at, near_x), pl.ds(0, cut)]
         now["dy"] = go(copies.remote(block, block, near_y, s))
-        block = full.at[near_x]
+        block = full.at[index(at, near_x)]
         now["twin"].append(go(copies.remote(block, block, twin, s)))
         now["y"].wait_recv()
-        block = full.at[near_y, pl.ds(cut, full.shape[1] - cut)]
+        block = full.at[index(at, near_y), pl.ds(cut, full.shape[1] - cut)]
         now["dx"] = go(copies.remote(block, block, near_x, s))
-        block = full.at[near_y]
+        block = full.at[index(at, near_y)]
         now["twin"].append(go(copies.remote(block, block, twin, s)))
 
     fetched = {}
@@ -1230,13 +1284,14 @@
         full, now = fulls[at], second[at]
         now["dy"].wait_recv()
         now["dx"].wait_recv()
-        block = full.at[far]
+        block = full.at[index(at, far)]
         now["twin"].append(go(copies.remote(block, block, twin, s)))
         for move in now["twin"]:
             move.wait_recv()
         if at < len(near):
             fetched[at] = copies.local(full, near[at])
             fetched[at].start()
+            done.add(at)
 
     def fetch(at):
         fetched[at].wait()
@@ -1329,34 +1384,65 @@
     def make_cap_value():
         cap_value[...] = bf_dot(cap_near_rows(), fetch(4)).astype(BF16)
 
-    def make_mixed(pair):
+    def attend(pair, k_ref, v_ref, mask, store):
         lane = slice(pair * 128, (pair + 1) * 128)
-        gate = jnp.tanh(gain_of(7, pair))
         low = low_half((128, 128))
-        keys, cap_keys = key[:, lane], cap_key[:, lane]
-        values = jnp.concatenate([value[:, lane] * key_mask[...], key_mask[...]], axis=1)
-        cap_values = jnp.concatenate([cap_value[:, lane] * cap_mask[...], cap_mask[...]], axis=1)
+        keys = k_ref[:, lane]
+        values = jnp.concatenate([v_ref[:, lane] * mask[...], mask[...]], axis=1)
 
         def body(i, carry):
             at = pl.ds(pl.multiple_of(i * 128, 128), 128)
             q = query[at, lane] * jnp.asarray(HEAD_DIM**-0.5, BF16)
-            halves = (jnp.where(low, q, jnp.zeros_like(q)), jnp.where(low, jnp.zeros_like(q), q))
-            found = []
-            for k, v in ((keys, values), (cap_keys, cap_values)):
-                outs = []
-                for half in halves:
-                    weights = jnp.exp(right_dot(half, k))
-                    outs.append(bf_dot(weights.astype(BF16), v))
-                out = jnp.where(low, outs[0][:, :128], outs[1][:, :128])
-                norm = 1.0 / jnp.where(low, outs[0][:, 128:], outs[1][:, 128:])
-                found.append(out * norm)
-            own, cross = found
-            cross_out[at, lane] = cross
-            mixed[at, lane] = (own + gate * cross).astype(BF16)
+            outs = []
+            for half in (jnp.where(low, q, jnp.zeros_like(q)), jnp.where(low, jnp.zeros_like(q), q)):
+                weights = jnp.exp(right_dot(half, keys))
+                outs.append(bf_dot(weights.astype(BF16), values))
+            out = jnp.where(low, outs[0][:, :128], outs[1][:, :128])
+            store(at, lane, out / jnp.where(low, outs[0][:, 128:], outs[1][:, 128:]))
             return carry
 
         lax.fori_loop(0, rows // 128, body, 0)
 
+    def make_own(pair):
+        def store(at, lane, out):
+            own_out[at, lane] = out
+
+        attend(pair, key, value, key_mask, store)
+
+    def make_mixed(pair):
+        gate = jnp.tanh(gain_of(7, pair))
+
+        def store(at, lane, out):
+            cross_out[at, lane] = out
+            mixed[at, lane] = (own_out[at, lane] + gate * out).astype(BF16)
+
+        attend(pair, cap_key, cap_value, cap_mask, store)
+
+    work = [
+        (lambda: (small_sums(), make_hidden()), "h", {"tok"}),
+        (make_query, "q", {"h", 0}),
+        (make_key, "k", {"h", 1}),
+        (make_value, "v", {"h", 2}),
+        (make_cap_key, "ck", {"cap", 3}),
+        (make_cap_value, "cv", {"cap", 4}),
+        *((functools.partial(make_own, p), ("own", p), {"q", "k", "v"}) for p in range(pairs)),
+        *(
+            (functools.partial(make_mixed, p), ("all", p), {"q", "ck", "cv", ("own", p)})
+            for p in range(pairs)
+        ),
+    ]
+
+    def do_work():
+        for at, (piece, name, needs) in enumerate(work):
+            if needs <= done:
+                piece()
+                done.add(name)
+                del work[at]
+                return True
+        return False
+
+
+    done = set()
 
     def begin(i):
         relay, j = items[i]
@@ -1364,8 +1450,10 @@
             depart(j)
         else:
             relay.start(j)
-
-    window = 2
+            if j == seq - 1:
+                done.add("tok" if relay is tok else "cap")
+
+    window = WINDOW
     for i in range(window):
         begin(i)
     for move in small_moves:
@@ -1386,13 +1474,6 @@
         mod_next.append(go(copies.remote(mod_sum, got_seq.at[k], b, peer)))
 
     cap_out = copies.local(cap_near, cap_all)
-    pieces = {
-        7: [small_sums, make_hidden],
-        9: [make_query],
-        10: [make_key],
-        11: [make_value],
-        15: [cap_out.start, make_cap_key],
-    }
     order = []
     for i, (relay, j) in enumerate(items):
         if relay is None:
@@ -1404,19 +1485,19 @@
         if relay is None:
             order.append(j)
             stage_a(j)
-            if len(order) >= 2:
-                stage_b(order[-2])
-            if len(order) >= 3:
-                stage_c(order[-3])
-        for piece in pieces.get(i, ()):
-            piece()
-    stage_b(order[-1])
-    stage_c(order[-2])
-    make_cap_value()
-    make_mixed(0)
+            if len(order) > LAG:
+                stage_b(order[-1 - LAG])
+            if len(order) > LAG + 1:
+                stage_c(order[-2 - LAG])
+        do_work()
+    cap_out.start()
+    for at in range(LAG):
+        stage_b(order[len(order) - LAG + at])
+        stage_c(order[len(order) - LAG - 1 + at])
+        do_work()
     stage_c(order[-1])
-    for pair in range(1, pairs):
-        make_mixed(pair)
+    while do_work():
+        pass
     cap_out.wait()
     for move in sent:
         move.wait_send()
@@ -1466,6 +1547,7 @@
             pltpu.VMEM((buckets, seq) + small.shape, F32),
             pltpu.VMEM((seq,) + tokens.shape, BF16),
             pltpu.VMEM((seq,) + captions.shape, BF16),
+            pltpu.VMEM((span, share), F32),
             *near,
             pltpu.SemaphoreType.DMA((n_sems,)),
             pltpu.SemaphoreType.DMA((n_sems,)),
@@ -1479,14 +1561,329 @@
     return outs[0], weights, outs[at:]
 
 
+def middle_kernel(buckets, seq, chunks, kinds, *refs):
+    mixed, w_out, tokens, cotangent, row_scale, gain_rows, mod_rows = refs[:7]
+    far_weights, refs = refs[7:10], refs[10:]
+    block_out, d_tokens, d_attn, row_sums = refs[:4]
+    outs, refs = refs[4:7], refs[7:]
+    w_gate, w_up, w_down, ffn_all, d_ffn, act, d_gate, d_up = refs[:8]
+    gate_keep, up_keep, attn_keep, resid_keep, got, parts, from_left, from_right = refs[8:16]
+    send, recv = refs[16:18]
+    grads, refs = refs[18:21], refs[21:]
+    b, s = lax.axis_index("bucket"), lax.axis_index("seq")
+    copies = Copies(send, recv)
+    loads = [copies.local(a, b_) for a, b_ in zip(far_weights, (w_gate, w_up, w_down), strict=True)]
+    for load in loads:
+        load.start()
+    sums = GradSums(copies, b, s, buckets, seq, kinds, grads, outs, refs, near=True)
+    pl.semaphore_wait(pltpu.get_barrier_semaphore(), greet_all(b, s, buckets, seq))
+
+    rows, width = tokens.shape
+    thin = rows // chunks
+    tall = seq * thin
+    hidden = act.shape[-1]
+    wide = 512
+    gate_post = jnp.tanh(mod_rows[1:2, :]) * gain_rows[1:2, :]
+    gain_ffn = gain_rows[2:3, :] * (1.0 + mod_rows[2:3, :])
+    gate_last = jnp.tanh(mod_rows[3:4, :]) * gain_rows[3:4, :]
+    row_sums[...] = jnp.zeros_like(row_sums)
+
+    def of(c):
+        return pl.ds(c * thin, thin)
+
+    def chunk_of(ref, c, cols=slice(None)):
+        whole = ref[:, of(c), cols]
+        return whole.reshape(tall, whole.shape[-1])
+
+    def mean(values):
+        return jnp.mean(values, axis=-1, keepdims=True)
+
+    def over_rows(c, body):
+        step = 16
+
+        def one(i, carry):
+            return body(pl.ds(pl.multiple_of(c * thin + i * step, step), step), carry)
+
+        return lax.fori_loop(0, thin // step, one, jnp.zeros((1, width), F32), unroll=2)
+
+    def weighted(at):
+        return cotangent[at, :].astype(F32) * row_scale[at, 0:1]
+
+    def after_attn(c):
+        def body(at, carry):
+            out = got[at, :]
+            attn_keep[at, :] = out
+            resid = out * lax.rsqrt(mean(out * out) + 1e-05) * gate_post
+            resid = tokens[at, :].astype(F32) + resid
+            resid_keep[at, :] = resid
+            normed = resid * lax.rsqrt(mean(resid * resid) + 1e-05)
+            ffn_all[s, at, :] = (normed * gain_ffn).astype(BF16)
+            return carry
+
+        over_rows(c, body)
+
+    def after_ffn(c):
+        def body(at, total):
+            out, resid, grad = got[at, :], resid_keep[at, :], weighted(at)
+            size = lax.rsqrt(mean(out * out) + 1e-05)
+            normed = out * size
+            block_out[at, :] = (resid + gate_last * normed).astype(BF16)
+            inner = grad * gate_last
+            d_ffn[s, at, :] = (size * (inner - normed * mean(inner * normed))).astype(BF16)
+            return total + jnp.sum(grad * normed, axis=0, keepdims=True)
+
+        row_sums[2:3, :] += over_rows(c, body)
+
+    def after_ffn_back(c):
+        def body(at, totals):
+            first, second = totals
+            d_pre, resid, out = got[at, :], resid_keep[at, :], attn_keep[at, :]
+            size = lax.rsqrt(mean(resid * resid) + 1e-05)
+            normed, inner = resid * size, d_pre * gain_ffn
+            second = second + jnp.sum(d_pre * normed, axis=0, keepdims=True)
+            grad = weighted(at) + size * (inner - normed * mean(inner * normed))
+            d_tokens[at, :] = grad
+            size = lax.rsqrt(mean(out * out) + 1e-05)
+            normed, inner = out * size, grad * gate_post
+            first = first + jnp.sum(grad * normed, axis=0, keepdims=True)
+            d_attn[s, at, :] = (size * (inner - normed * mean(inner * normed))).astype(BF16)
+            return first, second
+
+        step, zero = 16, jnp.zeros((1, width), F32)
+
+        def one(i, carry):
+            return body(pl.ds(pl.multiple_of(c * thin + i * step, step), step), carry)
+
+        first, second = lax.fori_loop(0, thin // step, one, (zero, zero), unroll=2)
+        row_sums[0:1, :] += first
+        row_sums[1:2, :] += second
+
+    def put_parts(c, cols, total):
+        parts[c, :, :, cols] = total.astype(BF16).reshape(seq, thin, total.shape[-1])
+
+    def attn_product(c):
+        left = chunk_of(mixed, c)
+        for at in range(0, width, wide):
+            cols = slice(at, at + wide)
+            put_parts(c, cols, bf_dot(left, w_out[:, cols]))
+
+    def ffn_product(c):
+        for at in range(0, hidden, wide):
+            cols = slice(at, at + wide)
+            left = chunk_of(ffn_all, c)
+            gate, up = bf_dot(left, w_gate[:, cols]), bf_dot(left, w_up[:, cols])
+            gate_keep[c, :, cols], up_keep[c, :, cols] = gate, up
+            value = (gate * jax.nn.sigmoid(gate) * up).astype(BF16)
+            act[:, of(c), cols] = value.reshape(seq, thin, wide)
+        left = chunk_of(act, c)
+        for at in range(0, width, wide):
+            cols = slice(at, at + wide)
+            put_parts(c, cols, bf_dot(left, w_down[:, cols]))
+
+    def ffn_back_product(c):
+        for at in range(0, hidden, wide):
+            cols = slice(at, at + wide)
+            d_act = right_dot(chunk_of(d_ffn, c), w_down[cols, :])
+            gate, up = gate_keep[c, :, cols], up_keep[c, :, cols]
+            sig = jax.nn.sigmoid(gate)
+            silu = gate * sig
+            d_g = (d_act * up * (sig + silu * (1.0 - sig))).astype(BF16)
+            d_u = (d_act * silu).astype(BF16)
+            d_gate[:, of(c), cols] = d_g.reshape(seq, thin, wide)
+            d_up[:, of(c), cols] = d_u.reshape(seq, thin, wide)
+        left_g, left_u = chunk_of(d_gate, c), chunk_of(d_up, c)
+        for at in range(0, width, wide):
+            cols = slice(at, at + wide)
+            total = right_dot(left_g, w_gate[cols, :]) + right_dot(left_u, w_up[cols, :])
+            put_parts(c, cols, total)
+
+    def pour_of(c, turn):
+        left, right = from_left.at[turn * chunks + c], from_right.at[turn * chunks + c]
+        return Pour(copies, parts.at[c], left, right, b, s, seq)
+
+    gathered = (ffn_all, d_ffn, d_attn)
+    after = (after_attn, after_ffn, after_ffn_back)
+    products = (attn_product, ffn_product, ffn_back_product)
+
+    def all_rows(ref, cols=slice(None)):
+        whole = ref[:, :, cols]
+        return whole.reshape(seq * rows, whole.shape[-1])
+
+    def down_grad():
+        chips, part = buckets // 2, hidden // buckets
+        at = spread(buckets)
+        for i in range(chips):
+            turned = all_rows(act, slice(2 * i * part, 2 * (i + 1) * part)).T
+            total = bf_dot(turned, all_rows(d_ffn)).astype(BF16)
+            for half in range(2):
+                p = at[2 * i + half]
+                grads[2][p // 2, p % 2] = total[half * part : (half + 1) * part]
+        sums.begin(2)
+
+    def weight_grads():
+        chips, part = buckets // 2, width // (buckets // 2)
+        for i in range(chips):
+            turned = all_rows(ffn_all, slice(i * part, (i + 1) * part)).T
+            for grad, d in zip(grads[:2], (d_gate, d_up), strict=True):
+                total = bf_dot(turned, all_rows(d))
+                grad[i] = total.astype(BF16).reshape(2, part // 2, hidden)
+            if i == 1:
+                sums.stage_a(2)
+            yield
+        sums.begin(0)
+        sums.begin(1)
+        sums.stage_b(2)
+        yield
+        sums.stage_a(0)
+        yield
+        sums.stage_c(2)
+        sums.stage_a(1)
+        yield
+        sums.stage_b(0)
+        yield
+        sums.stage_b(1)
+        yield
+        sums.stage_c(0)
+        sums.stage_c(1)
+        sums.stage_d(2)
+
+    extra = weight_grads()
+    plan = [(turn, c) for turn in range(3) for c in range(chunks)]
+    gathers, open_gather = {}, []
+
+    def finish_gather():
+        turn, c = open_gather.pop(0)
+        gathers[turn, c].start(seq - 1)
+        for j in range(seq - 1):
+            gathers[turn, c].sent(j)
+        return turn, c
+
+    attn_product(0)
+    pours = {(0, 0): pour_of(0, 0)}
+    ready = pours[0, 0].cuts
+    for q in range(ready):
+        pours[0, 0].step(q)
+    for c in range(1, chunks):
+        attn_product(c)
+    for load in loads:
+        load.wait()
+    for at, (turn, c) in enumerate(plan):
+        pour = pours[turn, c]
+        mate = gathers[open_gather[0]] if open_gather else None
+        per = pour.count // (seq - 1)
+        final = at == len(plan) - 1
+        for j in range(2, seq):
+            if mate is not None and j < seq - 1:
+                mate.start(j)
+            if final:
+                next(extra, None)
+            for q in range((j - 1) * per, j * per):
+                pour.step(q)
+            if final:
+                next(extra, None)
+        pour.end(got.at[of(c)])
+        after[turn](c)
+        gathers[turn, c] = Relay(copies, None, gathered[turn], b, s, seq, of(c))
+        gathers[turn, c].start(0)
+        if mate is not None:
+            done_turn, done_c = finish_gather()
+            if (done_turn, done_c) == (1, chunks - 1):
+                down_grad()
+            if done_turn < 2:
+                products[done_turn + 1](done_c)
+        open_gather.append((turn, c))
+        gathers[turn, c].start(1)
+        if at + 1 < len(plan):
+            nxt = plan[at + 1]
+            pours[nxt] = pour_of(nxt[1], nxt[0])
+            for q in range(ready):
+                pours[nxt].step(q)
+            if at + 2 == len(plan):
+                next(extra)
+                next(extra)
+    turn, c = open_gather[0]
+    for j in range(2, seq - 1):
+        next(extra, None)
+        gathers[turn, c].start(j)
+    next(extra, None)
+    finish_gather()
+    for _ in extra:
+        pass
+    sums.end()
+
+
+def middle_all(buckets, seq, mixed, weights, tokens, cotangent, row_scale, gain_rows, mod_rows):
+    any_spec = pl.BlockSpec(memory_space=pl.ANY)
+    vmem = pl.BlockSpec(memory_space=pltpu.VMEM)
+    chunks = CHUNKS
+    w_out, w_gate, w_up, w_down = weights
+    rows, width = tokens.shape
+    hidden = w_gate.shape[1]
+    tall, thin = (seq, rows, width), rows // chunks
+    flat = (seq, rows, hidden)
+    blocks = pltpu.VMEM((3 * chunks, seq - 1, thin, width), BF16)
+    kinds = ("col", "col", "row")
+    shapes, sums_out, scratch, n_sems = sums_shapes(
+        buckets, seq, [w_gate.shape, w_up.shape, w_down.shape], kinds, near=True
+    )
+    n_sems += 16 + 3 * chunks * (2 * CUTS + 2) * seq
+    results = pl.pallas_call(
+        functools.partial(middle_kernel, buckets, seq, chunks, kinds),
+        out_shape=[
+            jax.ShapeDtypeStruct((rows, width), BF16),
+            jax.ShapeDtypeStruct((rows, width), F32),
+            jax.ShapeDtypeStruct(tall, BF16),
+            jax.ShapeDtypeStruct((8, width), F32),
+            *sums_out,
+        ],
+        in_specs=[vmem] * 7 + [any_spec] * 3,
+        out_specs=[vmem] * 7,
+        scratch_shapes=[
+            pltpu.VMEM(w_gate.shape, BF16),
+            pltpu.VMEM(w_up.shape, BF16),
+            pltpu.VMEM(w_down.shape, BF16),
+            pltpu.VMEM(tall, BF16),
+            pltpu.VMEM(tall, BF16),
+            *([pltpu.VMEM(flat, BF16)] * 3),
+            pltpu.VMEM((chunks, seq * thin, hidden), F32),
+            pltpu.VMEM((chunks, seq * thin, hidden), F32),
+            pltpu.VMEM((rows, width), F32),
+            pltpu.VMEM((rows, width), F32),
+            pltpu.VMEM((rows, width), F32),
+            pltpu.VMEM((chunks, seq, thin, width), BF16),
+            blocks,
+            blocks,
+            pltpu.SemaphoreType.DMA((n_sems,)),
+            pltpu.SemaphoreType.DMA((n_sems,)),
+            *[pltpu.VMEM(shape, BF16) for shape in shapes],
+            *scratch,
+        ],
+        compiler_params=pltpu.CompilerParams(
+            collective_id=11, has_side_effects=True, vmem_limit_bytes=62 * 2**20
+        ),
+    )(
+        mixed.reshape(seq, rows, mixed.shape[1]),
+        w_out,
+        tokens,
+        cotangent,
+        row_scale,
+        gain_rows,
+        mod_rows,
+        w_gate,
+        w_up,
+        w_down,
+    )
+    return results[:4], [out.reshape(-1, out.shape[-1]) for out in results[4:]]
+
+
 def backward_kernel(buckets, seq, kinds, *refs):
     count = len(kinds)
     (
         d_attn,
-        w_out,
         w_query,
         w_key,
         w_value,
+        w_out,
         query,
         key,
         value,
@@ -1497,33 +1894,31 @@
         key_raw,
         cap_raw,
         gain_rows,
+        mod_rows,
         key_bias,
         cap_bias,
-    ) = refs[:17]
-    grads = refs[17 : 17 + count]
-    refs = refs[17 + count :]
-    d_hidden, d_query, d_key, d_value, d_cap_key, d_cap_value, own_sums = refs[:7]
-    outs = refs[7 : 7 + count]
-    refs = refs[7 + count :]
+        mixed,
+        hidden,
+        captions,
+        tokens,
+        d_tokens,
+        row_sums,
+    ) = refs[:24]
+    tokens_grad, vec_all, refs = refs[24], refs[25], refs[26:]
+    outs, refs = refs[:count], refs[count:]
     mixed_low, cross_low, query_acc, key_acc, value_acc, cap_key_acc, cap_value_acc = refs[:7]
-    parts, from_left, from_right, send, recv = refs[7:12]
+    d_query, d_key, d_value, d_cap_key, d_cap_value, d_hidden, vec, vec_seq, vec_sum = refs[7:16]
+    parts, from_left, from_right, send, recv = refs[16:21]
+    grads, refs = refs[21 : 21 + count], refs[21 + count :]
     b, s = lax.axis_index("bucket"), lax.axis_index("seq")
     copies = Copies(send, recv)
-    sums = GradSums(copies, b, s, buckets, seq, kinds, grads, outs, refs[12:])
+    sums = GradSums(copies, b, s, buckets, seq, kinds, grads, outs, refs, near=True)
     peers = greet_all(b, s, buckets, seq)
-    pl.semaphore_wait(pltpu.get_barrier_semaphore(), peers)
-    for w in range(min(2, count)):
-        sums.begin(w)
-    steps = sums.steps()
-
-    def advance(times=1):
-        for _ in range(times):
-            step = next(steps, None)
-            if step is not None:
-                step()
 
     rows, share = query.shape
+    width = parts.shape[-1]
     pairs = share // 128
+    chips = buckets // 2
     span_block = 256
     scale = HEAD_DIM**-0.5
 
@@ -1531,10 +1926,11 @@
         at = pl.multiple_of(s * share + pair * 128, 128)
         return gain_rows[row : row + 1, pl.ds(at, 128)]
 
-    weights = w_out[...]
-    mixed_low[...] = right_dot(d_attn[...], weights.reshape(share, weights.shape[-1])).astype(BF16)
-    own_sums[...] = jnp.zeros_like(own_sums)
-    advance()
+    vec[...] = jnp.zeros_like(vec)
+    mixed_low[...] = right_dot(d_attn[...], w_out[...]).astype(BF16)
+
+    def own_sum(row, pair, total):
+        vec[row : row + 1, pl.ds(pl.multiple_of(s * share + pair * 128, 128), 128)] = total
 
     def cross_part(pair):
         lane = slice(pair * 128, (pair + 1) * 128)
@@ -1547,44 +1943,36 @@
             return total + jnp.sum(d * cross_out[at, lane], axis=0, keepdims=True)
 
         total = lax.fori_loop(0, rows // 128, body, jnp.zeros((1, 128), F32))
-        own_sums[3:4, lane] = total * (1.0 - gate * gate)
-
-    def attend_back(pair):
+        own_sum(11, pair, total * (1.0 - gate * gate))
+
+    def attend_back(pair, k_ref, v_ref, bias, d_ref, k_acc, v_acc, add):
         lane = slice(pair * 128, (pair + 1) * 128)
         low = low_half((span_block, 128))
-        sides = (
-            (key, value, key_bias, mixed_low, key_acc, value_acc),
-            (cap_key, cap_value, cap_bias, cross_low, cap_key_acc, cap_value_acc),
-        )
-        turned = [side[0][:, lane].T for side in sides]
-        for side in sides:
-            side[4][:, lane] = jnp.zeros((side[4].shape[0], 128), F32)
-            side[5][:, lane] = jnp.zeros((side[5].shape[0], 128), F32)
+        k_turned = k_ref[:, lane].T
+        k_acc[:, lane] = jnp.zeros((k_acc.shape[0], 128), F32)
+        v_acc[:, lane] = jnp.zeros((v_acc.shape[0], 128), F32)
 
         def body(i, carry):
             at = pl.ds(pl.multiple_of(i * span_block, span_block), span_block)
             q = query[at, lane] * jnp.asarray(scale, BF16)
-            d_turned = None
-            for side, k_turned in zip(sides, turned, strict=True):
-                k_ref, v_ref, bias, d_ref, k_acc, v_acc = side
-                d = d_ref[at, lane]
-                found = []
-                for keep in (low, jnp.logical_not(low)):
-                    q_half = jnp.where(keep, q, jnp.zeros_like(q))
-                    d_half = jnp.where(keep, d, jnp.zeros_like(d))
-                    scores = right_dot(k_ref[:, lane], q_half)
-                    scores = scores + jnp.concatenate([bias[...], bias[...]], axis=1)
-                    weights = jnp.exp(scores)
-                    probs = weights * (1.0 / jnp.sum(weights, axis=0, keepdims=True))
-                    d_probs = right_dot(v_ref[:, lane], d_half)
-                    delta = jnp.sum(probs * d_probs, axis=0, keepdims=True)
-                    d_scores = (probs * (d_probs - delta)).astype(BF16)
-                    k_acc[:, lane] += bf_dot(d_scores, q_half)
-                    v_acc[:, lane] += bf_dot(probs.astype(BF16), d_half)
-                    found.append(bf_dot(k_turned, d_scores))
-                both = jnp.concatenate([found[0][:HEAD_DIM], found[1][HEAD_DIM:]], axis=0)
-                d_turned = both if d_turned is None else d_turned + both
-            query_acc[at, lane] = d_turned.T * scale
+            d = d_ref[at, lane]
+            found = []
+            for keep in (low, jnp.logical_not(low)):
+                q_half = jnp.where(keep, q, jnp.zeros_like(q))
+                d_half = jnp.where(keep, d, jnp.zeros_like(d))
+                scores = right_dot(k_ref[:, lane], q_half)
+                scores = scores + jnp.concatenate([bias[...], bias[...]], axis=1)
+                weights = jnp.exp(scores)
+                probs = weights * (1.0 / jnp.sum(weights, axis=0, keepdims=True))
+                d_probs = right_dot(v_ref[:, lane], d_half)
+                delta = jnp.sum(probs * d_probs, axis=0, keepdims=True)
+                d_scores = (probs * (d_probs - delta)).astype(BF16)
+                k_acc[:, lane] += bf_dot(d_scores, q_half)
+                v_acc[:, lane] += bf_dot(probs.astype(BF16), d_half)
+                found.append(bf_dot(k_turned, d_scores))
+            turned = jnp.concatenate([found[0][:HEAD_DIM], found[1][HEAD_DIM:]], axis=0)
+            d_q = turned.T * scale
+            query_acc[at, lane] = query_acc[at, lane] + d_q if add else d_q
             return carry
 
         lax.fori_loop(0, rows // span_block, body, 0)
@@ -1608,59 +1996,128 @@
                 return total + jnp.sum(d * normed, axis=0, keepdims=True)
 
             total = lax.fori_loop(0, raw.shape[0] // 64, body, jnp.zeros((1, 128), F32))
-            own_sums[sum_row : sum_row + 1, lane] = total
-
+            own_sum(sum_row, pair, total)
+
+    def weight_grads(left, chosen):
+        part = left.shape[1] // chips
+        for i in range(chips):
+            turned = left[:, i * part : (i + 1) * part].T
+            for w, right in chosen:
+                total = bf_dot(turned, right[...])
+                grads[w][i] = total.astype(BF16).reshape(2, part // 2, total.shape[-1])
+            yield
+        for w, _ in chosen:
+            sums.begin(w)
+
+    def out_grad():
+        total = bf_dot(mixed[...].T, d_attn[...]).astype(BF16)
+        part = share // buckets
+        for block, p in enumerate(spread(buckets)):
+            grads[0][p // 2, p % 2] = total[block * part : (block + 1) * part]
+        sums.begin(0)
+
+    pl.semaphore_wait(pltpu.get_barrier_semaphore(), peers)
+    out_grad()
     for pair in range(pairs):
         cross_part(pair)
-        attend_back(pair)
-        advance(2)
-    norm_back(query_raw, query_acc, d_query, 4, 0)
-    norm_back(key_raw, key_acc, d_key, 5, 1)
+        attend_back(pair, cap_key, cap_value, cap_bias, cross_low, cap_key_acc, cap_value_acc, False)
+    norm_back(cap_raw, cap_key_acc, d_cap_key, 6, 10)
+    d_cap_value[...] = cap_value_acc[...].astype(BF16)
+    for _ in weight_grads(captions, ((1, d_cap_key), (2, d_cap_value))):
+        pass
+    steps = {
+        0: (lambda: sums.stage_a(0), lambda: sums.stage_a(1)),
+        1: (lambda: sums.stage_b(0), lambda: sums.stage_b(1), lambda: sums.stage_a(2)),
+        2: (lambda: sums.stage_c(0), lambda: sums.stage_b(2), lambda: sums.stage_c(1)),
+    }
+    for pair in range(pairs):
+        attend_back(pair, key, value, key_bias, mixed_low, key_acc, value_acc, True)
+        for step in steps.get(pair, ()):
+            step()
+    norm_back(query_raw, query_acc, d_query, 4, 8)
+    norm_back(key_raw, key_acc, d_key, 5, 9)
     d_value[...] = value_acc[...].astype(BF16)
     pour = Pour(copies, parts, from_left, from_right, b, s, seq)
-    width = parts.shape[-1]
     wide = 512
     for at in range(0, width, wide):
         cols = slice(at, at + wide)
         total = right_dot(d_query[...], w_query[cols, :]) + right_dot(d_key[...], w_key[cols, :])
         total = total + right_dot(d_value[...], w_value[cols, :])
         parts[:, :, cols] = total.astype(BF16).reshape(seq, rows // seq, wide)
-    for q in range(2):
+    pieces = weight_grads(hidden, ((3, d_query), (4, d_key), (5, d_value)))
+    for q in range(pour.count):
         pour.step(q)
-    norm_back(cap_raw, cap_key_acc, d_cap_key, 6, 2)
-    d_cap_value[...] = cap_value_acc[...].astype(BF16)
-    for q in range(2, pour.count):
-        pour.step(q)
-        advance()
+        next(pieces, None)
+    for _ in pieces:
+        pass
+    sums.stage_c(2)
+    sums.stage_a(3)
+    sums.stage_a(4)
+    sums.stage_b(3)
+    sums.stage_a(5)
     pour.end(d_hidden)
-    for step in steps:
-        step()
+
+    factor = gain_rows[0:1, :] * (1.0 + mod_rows[0:1, :])
+
+    def body(i, total):
+        at = pl.ds(pl.multiple_of(i * 16, 16), 16)
+        x, d = tokens[at, :].astype(F32), d_hidden[at, :]
+        size = lax.rsqrt(jnp.mean(x * x, axis=-1, keepdims=True) + 1e-05)
+        normed, inner = x * size, d * factor
+        mean = jnp.mean(inner * normed, axis=-1, keepdims=True)
+        tokens_grad[at, :] = d_tokens[at, :] + size * (inner - normed * mean)
+        return total + jnp.sum(d * normed, axis=0, keepdims=True)
+
+    total = lax.fori_loop(0, tokens.shape[0] // 16, body, jnp.zeros((1, width), F32))
+    post, last = jnp.tanh(mod_rows[1:2, :]), jnp.tanh(mod_rows[3:4, :])
+    vec[0:1, :] = total * gain_rows[0:1, :]
+    vec[1:2, :] = row_sums[0:1, :] * gain_rows[1:2, :] * (1.0 - post * post)
+    vec[2:3, :] = row_sums[1:2, :] * gain_rows[2:3, :]
+    vec[3:4, :] = row_sums[2:3, :] * gain_rows[3:4, :] * (1.0 - last * last)
+    vec[4:5, :] = total * (1.0 + mod_rows[0:1, :])
+    vec[5:6, :] = row_sums[0:1, :] * post
+    vec[6:7, :] = row_sums[1:2, :] * (1.0 + mod_rows[2:3, :])
+    vec[7:8, :] = row_sums[2:3, :] * last
+    vec_moves = []
+    for k in range(1, seq):
+        vec_moves.append(sums.go(copies.remote(vec, vec_seq.at[k], b, lax.rem(s + k, seq))))
+    sums.stage_b(4)
+    sums.stage_b(5)
+    for move in vec_moves:
+        move.wait_recv()
+    add_rows(vec_sum, [vec] + [vec_seq.at[k] for k in range(1, seq)])
+    vec_next = []
+    for k in range(1, buckets):
+        peer = lax.rem(b + k, buckets)
+        vec_next.append(sums.go(copies.remote(vec_sum, vec_all.at[b], peer, s)))
+    vec_own = copies.local(vec_sum, vec_all.at[b])
+    vec_own.start()
+    for w in (3, 4, 5):
+        sums.stage_c(w)
+    sums.stage_d(0)
+    for move in vec_next:
+        move.wait_recv()
+    vec_own.wait()
     sums.end()
 
 
-def backward_all(buckets, seq, rows, attention_refs, grads, kinds):
+def backward_all(buckets, seq, inputs, shapes, kinds):
     any_spec = pl.BlockSpec(memory_space=pl.ANY)
     vmem = pl.BlockSpec(memory_space=pltpu.VMEM)
-    inputs, outs, scratch, n_sems = sums_shapes(buckets, seq, grads, kinds)
-    d_attn, query, cap_key = attention_refs[0], attention_refs[5], attention_refs[8]
-    width = d_attn.shape[1]
-    low = jax.ShapeDtypeStruct(query.shape, BF16)
-    cap_low = jax.ShapeDtypeStruct(cap_key.shape, BF16)
-    inner = [
-        jax.ShapeDtypeStruct((rows, width), F32),
-        low,
-        low,
-        low,
-        cap_low,
-        cap_low,
-        jax.ShapeDtypeStruct((8, query.shape[1]), F32),
-    ]
-    n_sems += 8 * seq
+    shapes, outs, scratch, n_sems = sums_shapes(buckets, seq, shapes, kinds, near=True)
+    query, cap_key, tokens = inputs[5], inputs[8], inputs[21]
+    rows, width = tokens.shape
+    vec = (16, width)
+    n_sems += 8 * seq + 2 * buckets
     results = pl.pallas_call(
         functools.partial(backward_kernel, buckets, seq, tuple(kinds)),
-        out_shape=[*inner, *outs],
-        in_specs=[vmem] * len(attention_refs) + [any_spec] * len(grads),
-        out_specs=[vmem] * (len(inner) + len(outs)),
+        out_shape=[
+            jax.ShapeDtypeStruct((rows, width), F32),
+            jax.ShapeDtypeStruct((buckets,) + vec, F32),
+            *outs,
+        ],
+        in_specs=[vmem] * len(inputs),
+        out_specs=[vmem, any_spec] + [vmem] * len(outs),
         scratch_shapes=[
             pltpu.VMEM(query.shape, BF16),
             pltpu.VMEM(query.shape, BF16),
@@ -1669,18 +2126,28 @@
             pltpu.VMEM(query.shape, F32),
             pltpu.VMEM(cap_key.shape, F32),
             pltpu.VMEM(cap_key.shape, F32),
+            pltpu.VMEM(query.shape, BF16),
+            pltpu.VMEM(query.shape, BF16),
+            pltpu.VMEM(query.shape, BF16),
+            pltpu.VMEM(cap_key.shape, BF16),
+            pltpu.VMEM(cap_key.shape, BF16),
+            pltpu.VMEM((rows, width), F32),
+            pltpu.VMEM(vec, F32),
+            pltpu.VMEM((seq,) + vec, F32),
+            pltpu.VMEM(vec, F32),
             pltpu.VMEM((seq, rows, width), BF16),
             pltpu.VMEM((seq - 1, rows, width), BF16),
             pltpu.VMEM((seq - 1, rows, width), BF16),
             pltpu.SemaphoreType.DMA((n_sems,)),
             pltpu.SemaphoreType.DMA((n_sems,)),
+            *[pltpu.VMEM(shape, BF16) for shape in shapes],
             *scratch,
         ],
         compiler_params=pltpu.CompilerParams(
-            collective_id=10, has_side_effects=True, vmem_limit_bytes=60 * 2**20
+            collective_id=10, has_side_effects=True, vmem_limit_bytes=62 * 2**20
         ),
-    )(*attention_refs, *inputs)
-    return results[:7], [out.reshape(-1, out.shape[-1]) for out in results[7:]]
+    )(*inputs)
+    return results[0], results[1], [out.reshape(-1, out.shape[-1]) for out in results[2:]]
 
 
 def on_device(
@@ -1709,8 +2176,6 @@
     rows, width = tokens.shape
     span = rows * seq
     share = width // seq
-    heads = share // HEAD_DIM
-    scale = HEAD_DIM ** (-0.5)
     live_rows, cap_len = pick_entry(counts, b), pick_entry(cap_lens, b)
     token_total = jnp.sum(counts).astype(F32)
 
@@ -1741,47 +2206,30 @@
     small_rows, mod, hidden, query_proj, key_proj, cap_proj = inner[:6]
     query, key, value, cap_key, cap_value = inner[6:11]
     cross_out, mixed_low = inner[11:]
-    gain_f = small_rows[:7]
-    own_cols = lax.dynamic_slice_in_dim(small_rows, s * share, share, 1)
-    gate_cross = jnp.tanh(own_cols[7])
-    scale_attn, gate_attn, scale_ffn, gate_ffn = mod[0], mod[1], mod[2], mod[3]
-
-    attn_out = line_scatter(seq, bf_dot(mixed_low, wo), 2)
-
-    tokens_f = tokens.astype(F32)
-    (resid_one, ffn_pre), middle_back = jax.vjp(
-        middle, tokens_f, attn_out, gain_f[1], gate_attn, gain_f[2], scale_ffn
+    row_live = (s * rows + jnp.arange(rows) < live_rows).astype(F32)
+    row_scale = row_live * (buckets * span / token_total)
+    (block_out, d_tokens, d_attn_all, row_sums), (s_gate, s_up, s_down) = middle_all(
+        buckets,
+        seq,
+        mixed_low,
+        (wo, wg, wu, wd),
+        tokens,
+        cotangent,
+        jnp.broadcast_to(row_scale[:, None], (rows, 128)),
+        small_rows,
+        mod,
     )
-    ffn_all = line_gather(seq, ffn_pre.astype(BF16), 3)
-    act_pre, act_back = jax.vjp(activate, bf_dot(ffn_all, wg), bf_dot(ffn_all, wu))
-    act_low = act_pre.astype(BF16)
-    ffn_out = line_scatter(seq, bf_dot(act_low, wd), 4)
-    out_f, finish_back = jax.vjp(finish, resid_one, ffn_out, gain_f[3], gate_ffn)
-    block_out = out_f.astype(BF16)
-
-    row_live = (s * rows + jnp.arange(rows) < live_rows).astype(F32)
-    weighted = cotangent.astype(F32) * row_live[:, None] * (buckets * span / token_total)
-    d_resid, d_ffn_out, d_gain_last, d_gate_ffn = finish_back(weighted)
-    d_ffn_all = line_gather(seq, d_ffn_out.astype(BF16), 5)
-    d_gate, d_up = act_back(right_dot(d_ffn_all, wd))
-    d_gate, d_up = d_gate.astype(BF16), d_up.astype(BF16)
-    d_hidden_ffn = line_scatter(seq, right_dot(d_gate, wg) + right_dot(d_up, wu), 6)
-    d_tokens_one, d_attn_out, d_gain_post, d_gate_attn, d_gain_ffn, d_scale_ffn = middle_back(
-        (d_resid, d_hidden_ffn)
-    )
-    d_attn_all = line_gather(seq, d_attn_out.astype(BF16), 7)
     key_bias = jnp.where(jnp.arange(span) < live_rows, 0.0, -1e30).astype(F32)
     cap_bias = jnp.where(jnp.arange(cap_span) < cap_len, 0.0, -1e30).astype(F32)
-    (d_hidden, d_query, d_key, d_value, d_cap_key, d_cap_value, own_sums), early = backward_all(
+    tokens_grad, vec_all, sums = backward_all(
         buckets,
         seq,
-        rows,
         [
-            d_attn_all,
-            wo.reshape(buckets, -1, width),
+            d_attn_all.reshape(span, width),
             wq,
             wk,
             wv,
+            wo,
             query,
             key,
             value,
@@ -1792,40 +2240,20 @@
             key_proj,
             cap_proj,
             small_rows,
+            mod,
             jnp.broadcast_to(key_bias[:, None], (span, 128)),
             jnp.broadcast_to(cap_bias[:, None], (cap_span, 128)),
+            mixed_low,
+            hidden,
+            caps,
+            tokens,
+            d_tokens,
+            row_sums,
         ],
-        [
-            left_dot(ffn_all, d_gate),
-            left_dot(ffn_all, d_up),
-            left_dot(act_low, d_ffn_all),
-            left_dot(mixed_low, d_attn_all),
-        ],
-        ["col", "col", "row", "row"],
+        [x.shape for x in (wo, wck, wcv, wq, wk, wv)],
+        ["row", "col", "col", "col", "col", "col"],
     )
-    s_gate, s_up, s_down, s_out = early
-    _, pre_back = jax.vjp(pre_attn, tokens_f, gain_f[0], scale_attn)
-    d_tokens_two, d_gain_pre, d_scale_attn = pre_back(d_hidden)
-    tokens_grad = d_tokens_one + d_tokens_two
-
-    own_wide = lax.dynamic_update_slice(jnp.zeros((4, width), F32), own_sums[:4], (0, s * share))
-    vec = jnp.concatenate(
-        [
-            jnp.stack([d_scale_attn, d_gate_attn, d_scale_ffn, d_gate_ffn]),
-            jnp.stack([d_gain_pre, d_gain_post, d_gain_ffn, d_gain_last]),
-            own_wide,
-            jnp.zeros((4, width), F32),
-        ]
-    )
-    grads = [
-        left_dot(caps, d_cap_key),
-        left_dot(caps, d_cap_value),
-        left_dot(hidden, d_query),
-        left_dot(hidden, d_key),
-        left_dot(hidden, d_value),
-    ]
-    vec_all, sums = scatter_all(buckets, seq, vec, grads, ["col"] * 5)
-    s_cap_key, s_cap_value, s_query, s_key, s_value = sums
+    s_out, s_cap_key, s_cap_value, s_query, s_key, s_value = sums
 
     quarter = 4 * width // seq
     mod_rows = vec_all[:, :4].reshape(buckets, -1, quarter)

time: 605 us -> 505 us (0.83)
  matrix products: 47.4 us -> 0 us
  Pallas kernels: 504 us -> 469 us
  other arithmetic: 24 us -> 9.11 us
    pallas_call x7 -> x1, Pallas kernels: 241 us -> 187 us  [middle_all(): pl.pallas_call(functools.partial(middle_kernel, buckets, seq, chunks, kin...]
    dot_general x16 -> x0, matrix products: 47.4 us -> none  [the longest x9 25.9 us: left_dot(): lax.dot_general(rows_left, rows_right, (((0,), (0,)), ((), ())), preferre...]
    pallas_call x1, Pallas kernels: 86.1 us -> 118 us  [backward_all(): pl.pallas_call(functools.partial(backward_kernel, buckets, seq, tuple(kin...]
    pallas_call x1, Pallas kernels: 177 us -> 164 us  [forward_all(): pl.pallas_call(functools.partial(forward_kernel, buckets, seq, tuple(kind...]
    reduce_sum x7 -> x0, other arithmetic: 7.01 us -> none  [the longest x1 2.15 us: middle(): resid_one = tokens_in + jnp.tanh(gate_attn) * rms_rows(attn_out) * gain_post]
where the time goes in v3:
time: 505 us; the launch traced here: 496 us
  Pallas kernels  469 us (93%)
  local copies, waits for them, and re-layouts  16.3 us (3%)
  other arithmetic  9.11 us (2%)
    pallas_call x1, Pallas kernels, middle_all(): pl.pallas_call(functools.partial(middle_kernel, buckets, seq, chunks, kin...  187 us
    pallas_call x1, Pallas kernels, forward_all(): pl.pallas_call(functools.partial(forward_kernel, buckets, seq, tuple(kind...  164 us
    pallas_call x1, Pallas kernels, backward_all(): pl.pallas_call(functools.partial(backward_kernel, buckets, seq, tuple(kin...  118 us
    unnamed x34, local copies, waits for them, and re-layouts  10.1 us

profile of v3, /device:TPU:8, one launch (start us, length us, event | category | flops | bytes accessed | tf_op | source)
XLA Modules:
  0.0 496.0 jit_solution(10585273505544407446)
XLA Ops:
  0.7 0.7 convert_element_type.22
  1.3 0.1 multiply_cosine_fusion
  1.5 0.7 constant_dynamic-slice_fusion.1.refs_3_
  2.2 1.3 fusion.10
  3.5 0.6 fusion.5
  4.2 0.8 broadcast_in_dim.59.refs_5_
  4.9 0.6 fusion.7
  5.6 0.7 broadcast_in_dim.60.refs_6_
  6.3 1.3 fusion.3.refs_2_
  7.6 163.5 %shard_map.281 = (bf16[4,64,4096]{2,1,0:T(8,128)(2,1)}, bf16[8,4,48,384]{3,2,1,0:T(8,128)(2,1)}, bf16[8,4,48,384]{3,2,1,0:T(8,128)(2,1)}, bf16[8,4,48,384]{3,2,1...) custom-call(bf16[128,1536]{1,0:T(8,128)(2,1)} %refs_21_.1, ...), custom_call_target="tpu_custom_call" | custom-call | tf_op jit(solution)/shard_map/pallas_call | solution.py:1537
  171.9 0.7 compare_select_fusion
  172.5 0.7 broadcast_in_dim.61.refs_4_
  173.2 187.0 %shard_map.282 = (bf16[128,1536]{1,0:T(8,128)(2,1)}, f32[128,1536]{1,0:T(8,128)}, bf16[4,128,1536]{2,1,0:T(8,128)(2,1)}, f32[8,1536]{1,0:T(8,128)}, f32[192,1024...) custom-call(bf16[4,128,384]{2,1,0:T(8,128)(2,1)} %bitcast.26, bf16[384,1536]{1,0:T(8,128)(2,1)} %bitcast.19, ...), custom_call_target="tpu_custom_call" | custom-call | tf_op jit(solution)/shard_map/pallas_call | solution.py:1830
  360.3 0.7 fusion.4
  360.9 0.8 broadcast_in_dim.64.refs_16_
  361.7 0.6 fusion.6
  362.4 0.8 broadcast_in_dim.67.refs_17_
  363.2 0.0 copy-start.5
  363.2 118.1 %shard_map.283 = (f32[128,1536]{1,0:T(8,128)}, f32[8,16,1536]{2,1,0:T(8,128)}, f32[4,48,384]{2,1,0:T(8,128)}, f32[512,384]{1,0:T(8,128)}, f32[512,384]{1,0:T(8,1...) custom-call(bf16[512,1536]{1,0:T(8,128)(2,1)} %bitcast.25, bf16[1536,384]{1,0:T(8,128)(2,1)} %bitcast.27, ...), custom_call_target="tpu_custom_call" | custom-call | tf_op jit(solution)/shard_map/pallas_call | solution.py:2112
  481.2 0.0 copy-start.9
  481.2 0.0 copy-start.8
  481.3 0.0 copy-start.7
  481.3 0.0 copy-start.6
  481.3 0.0 copy-start.4
  481.3 1.2 slice.9
  482.5 1.4 multiply_reduce_fusion
  483.9 1.0 dynamic-slice_reduce_fusion
  484.9 0.0 copy-start.10
  484.9 0.5 slice_bitcast_fusion
  485.4 0.0 copy-done.5
  485.4 0.0 copy-start.3
  485.4 0.7 copy.46
  486.2 2.1 copy.47
  488.3 0.0 copy-done.9
  488.3 0.0 copy-start.2
  488.3 0.7 copy.48
  489.0 0.0 copy-done.8
  489.0 0.0 copy-start.1
  489.0 0.7 copy.49
  489.7 0.0 copy-done.7
  489.7 0.7 copy.50
  490.4 0.0 copy-done.6
  490.4 0.7 copy.51
  491.1 0.0 copy-done.4
  491.1 0.0 copy-start
  491.1 0.9 copy.52
  492.0 0.0 copy-done.10
  492.0 0.0 copy-done.3
  492.0 0.9 copy.53
  492.9 0.0 copy-done.2
  492.9 0.9 copy.54
  493.8 0.0 copy-done.1
  493.8 0.9 copy.55
  494.7 0.0 copy-done
  494.7 0.9 copy.56
  (5 shorter events, 0.1 us)
Async XLA Ops:
  363.2 122.3 %copy-start.5 = (bf16[128,1536]{1,0:T(8,128)(2,1)S(1)}, bf16[128,1536]{1,0:T(8,128)(2,1)}, u32[]{:S(2)}) copy-start(bf16[128,1536]{1,0:T(8,128)(2,1)} %get-tuple-element.105) | copy-start | bytes 1179652
  481.2 7.0 %copy-start.9 = (f32[192,384]{1,0:T(8,128)S(1)}, f32[192,384]{1,0:T(8,128)}, u32[]{:S(2)}) copy-start(f32[192,384]{1,0:T(8,128)} %get-tuple-element.107) | copy-start | bytes 884740
  481.2 7.7 %copy-start.8 = (f32[192,384]{1,0:T(8,128)S(1)}, f32[192,384]{1,0:T(8,128)}, u32[]{:S(2)}) copy-start(f32[192,384]{1,0:T(8,128)} %get-tuple-element.108) | copy-start | bytes 884740
  481.3 8.4 %copy-start.7 = (f32[192,384]{1,0:T(8,128)S(1)}, f32[192,384]{1,0:T(8,128)}, u32[]{:S(2)}) copy-start(f32[192,384]{1,0:T(8,128)} %get-tuple-element.109) | copy-start | bytes 884740
  481.3 9.1 %copy-start.6 = (f32[4,48,384]{2,1,0:T(8,128)S(1)}, f32[4,48,384]{2,1,0:T(8,128)}, u32[]{:S(2)}) copy-start(f32[4,48,384]{2,1,0:T(8,128)} %get-tuple-element.79) | copy-start | bytes 884740
  481.3 9.9 %copy-start.4 = (f32[512,384]{1,0:T(8,128)S(1)}, f32[512,384]{1,0:T(8,128)}, u32[]{:S(2)}) copy-start(f32[512,384]{1,0:T(8,128)} %get-tuple-element.111) | copy-start | bytes 2359300
  484.9 7.1 %copy-start.10 = (f32[8,48]{1,0:T(8,128)}, f32[8,48]{1,0:T(8,128)S(1)}, u32[]{:S(2)}) copy-start(f32[8,48]{1,0:T(8,128)S(1)} %dynamic-slice_reduce_fusion) | copy-start | bytes 4612
  485.4 6.6 %copy-start.3 = (f32[512,384]{1,0:T(8,128)S(1)}, f32[512,384]{1,0:T(8,128)}, u32[]{:S(2)}) copy-start(f32[512,384]{1,0:T(8,128)} %get-tuple-element.112) | copy-start | bytes 2359300
  488.3 4.6 copy-start.2
  489.0 4.8 copy-start.1
  491.1 3.5 copy-start

commit v4 on v3

--- a/solution.py
+++ b/solution.py
@@ -1105,12 +1105,21 @@
     return lax.broadcasted_iota(jnp.int32, shape, len(shape) - 1) < HEAD_DIM
 
 
+def pair_sums(values):
+    row = lax.broadcasted_iota(jnp.int32, (128, 128), 0) < HEAD_DIM
+    same = (row == low_half((128, 128))).astype(BF16)
+    high = values.astype(BF16)
+    rest = (values - high.astype(F32)).astype(BF16)
+    return bf_dot(high, same) + bf_dot(rest, same)
+
+
 def pair_scale(values, eps):
-    low = low_half(values.shape)
-    squares = values * values
-    first = jnp.sum(jnp.where(low, squares, 0.0), axis=-1, keepdims=True)
-    second = jnp.sum(jnp.where(low, 0.0, squares), axis=-1, keepdims=True)
-    return lax.rsqrt(jnp.where(low, first, second) * (1.0 / HEAD_DIM) + eps)
+    return lax.rsqrt(pair_sums(values * values) * (1.0 / HEAD_DIM) + eps)
+
+
+def fill_rows(out, live, first, yes, no):
+    row = lax.broadcasted_iota(jnp.int32, out.shape, 0) + first
+    out[...] = jnp.where(row < live, yes, no).astype(out.dtype)
 
 
 FORWARD_ORDER = ("tok", 0, "tok", 1, "tok", 2, "tok", 6, 7, "cap", 8, 3, "cap", 4, "cap", 5, "cap")
@@ -1120,11 +1129,11 @@
 
 def forward_kernel(buckets, seq, kinds, slim, *refs):
     count = len(kinds)
-    tokens, captions, small, cond, w_mod, key_mask, cap_mask = refs[:7]
+    tokens, captions, small, cond, w_mod, counts, cap_lens = refs[:7]
     shards = refs[7 : 7 + count]
     refs = refs[7 + count :]
     cap_all = refs[0]
-    fulls = refs[1 : 1 + count]
+    far_fulls = refs[1 : 1 + count]
     refs = refs[1 + count :]
     (
         gain_rows,
@@ -1143,8 +1152,8 @@
     ) = refs[:13]
     refs = refs[13:]
     part, got_bucket, got_seq, mod_sum, small_all, tok_all, cap_near, own_out = refs[:8]
-    near = refs[8:13]
-    send, recv = refs[13:]
+    fulls = refs[8 : 8 + count]
+    key_mask, cap_mask, send, recv = refs[8 + count :]
     b, s = lax.axis_index("bucket"), lax.axis_index("seq")
     copies = Copies(send, recv)
     place = b * seq + s
@@ -1163,6 +1172,8 @@
     def _():
         greet(from_b, from_s)
 
+    fill_rows(key_mask, counts[b], 0, 1.0, 0.0)
+    fill_rows(cap_mask, cap_lens[b], 0, 1.0, 0.0)
     lanes = part.shape[2]
     for j in range(part.shape[1]):
         part[:, j, :] = bf_dot(cond[...], w_mod[:, j * lanes : (j + 1) * lanes])
@@ -1288,14 +1299,13 @@
         now["twin"].append(go(copies.remote(block, block, twin, s)))
         for move in now["twin"]:
             move.wait_recv()
-        if at < len(near):
-            fetched[at] = copies.local(full, near[at])
-            fetched[at].start()
-            done.add(at)
+        go_local = copies.local(full, far_fulls[at])
+        go_local.start()
+        fetched[at] = go_local
+        done.add(at)
 
     def fetch(at):
-        fetched[at].wait()
-        whole = near[at][...]
+        whole = fulls[at][...]
         return whole.reshape(-1, whole.shape[-1])
 
 
@@ -1499,6 +1509,8 @@
     while do_work():
         pass
     cap_out.wait()
+    for copy in fetched.values():
+        copy.wait()
     for move in sent:
         move.wait_send()
 
@@ -1506,12 +1518,13 @@
 def forward_all(buckets, seq, tokens, captions, small, slim, cond, w_mod, masks, shards, kinds):
     any_spec = pl.BlockSpec(memory_space=pl.ANY)
     vmem = pl.BlockSpec(memory_space=pltpu.VMEM)
+    smem = pl.BlockSpec(memory_space=pltpu.SMEM)
     fulls = []
     for shard, kind in zip(shards, kinds, strict=True):
         rows, wide = shard.shape
         shape = (buckets, rows, wide) if kind == "row" else (buckets, seq, rows, wide // seq)
         fulls.append(jax.ShapeDtypeStruct(shape, BF16))
-    near = [pltpu.VMEM(full.shape, BF16) for full in fulls[:5]]
+    near = [pltpu.VMEM(full.shape, BF16) for full in fulls]
     width = tokens.shape[1]
     mod_lanes = w_mod.shape[1] // 8
     span, cap_span, share = seq * tokens.shape[0], seq * captions.shape[0], width // seq
@@ -1537,7 +1550,7 @@
     outs = pl.pallas_call(
         functools.partial(forward_kernel, buckets, seq, tuple(kinds), slim),
         out_shape=[jax.ShapeDtypeStruct((seq,) + captions.shape, BF16), *fulls, *inner],
-        in_specs=[any_spec, any_spec, any_spec, vmem, vmem, vmem, vmem] + [any_spec] * len(shards),
+        in_specs=[any_spec, any_spec, any_spec, vmem, vmem, smem, smem] + [any_spec] * len(shards),
         out_specs=[any_spec] * (1 + len(shards)) + [vmem] * len(inner),
         scratch_shapes=[
             pltpu.VMEM((buckets, 8, mod_lanes), F32),
@@ -1549,11 +1562,13 @@
             pltpu.VMEM((seq,) + captions.shape, BF16),
             pltpu.VMEM((span, share), F32),
             *near,
+            pltpu.VMEM((span, 128), BF16),
+            pltpu.VMEM((cap_span, 128), BF16),
             pltpu.SemaphoreType.DMA((n_sems,)),
             pltpu.SemaphoreType.DMA((n_sems,)),
         ],
         compiler_params=pltpu.CompilerParams(
-            collective_id=9, has_side_effects=True, vmem_limit_bytes=56 * 2**20
+            collective_id=9, has_side_effects=True, vmem_limit_bytes=62 * 2**20
         ),
     )(tokens, captions, small, cond, w_mod, *masks, *shards)
     at = 1 + len(shards)
@@ -1562,14 +1577,14 @@
 
 
 def middle_kernel(buckets, seq, chunks, kinds, *refs):
-    mixed, w_out, tokens, cotangent, row_scale, gain_rows, mod_rows = refs[:7]
+    mixed, w_out, tokens, cotangent, counts, gain_rows, mod_rows = refs[:7]
     far_weights, refs = refs[7:10], refs[10:]
     block_out, d_tokens, d_attn, row_sums = refs[:4]
     outs, refs = refs[4:7], refs[7:]
     w_gate, w_up, w_down, ffn_all, d_ffn, act, d_gate, d_up = refs[:8]
     gate_keep, up_keep, attn_keep, resid_keep, got, parts, from_left, from_right = refs[8:16]
-    send, recv = refs[16:18]
-    grads, refs = refs[18:21], refs[21:]
+    row_scale, send, recv = refs[16:19]
+    grads, refs = refs[19:22], refs[22:]
     b, s = lax.axis_index("bucket"), lax.axis_index("seq")
     copies = Copies(send, recv)
     loads = [copies.local(a, b_) for a, b_ in zip(far_weights, (w_gate, w_up, w_down), strict=True)]
@@ -1579,6 +1594,10 @@
     pl.semaphore_wait(pltpu.get_barrier_semaphore(), greet_all(b, s, buckets, seq))
 
     rows, width = tokens.shape
+    live = sum(counts[k] for k in range(buckets))
+    factor = buckets * seq * rows / jnp.full((rows, 128), live, jnp.int32).astype(F32)
+    row = lax.broadcasted_iota(jnp.int32, (rows, 128), 0) + s * rows
+    row_scale[...] = jnp.where(row < counts[b], factor, 0.0)
     thin = rows // chunks
     tall = seq * thin
     hidden = act.shape[-1]
@@ -1812,9 +1831,10 @@
     sums.end()
 
 
-def middle_all(buckets, seq, mixed, weights, tokens, cotangent, row_scale, gain_rows, mod_rows):
+def middle_all(buckets, seq, mixed, weights, tokens, cotangent, counts, gain_rows, mod_rows):
     any_spec = pl.BlockSpec(memory_space=pl.ANY)
     vmem = pl.BlockSpec(memory_space=pltpu.VMEM)
+    smem = pl.BlockSpec(memory_space=pltpu.SMEM)
     chunks = CHUNKS
     w_out, w_gate, w_up, w_down = weights
     rows, width = tokens.shape
@@ -1836,7 +1856,7 @@
             jax.ShapeDtypeStruct((8, width), F32),
             *sums_out,
         ],
-        in_specs=[vmem] * 7 + [any_spec] * 3,
+        in_specs=[vmem] * 4 + [smem] + [vmem] * 2 + [any_spec] * 3,
         out_specs=[vmem] * 7,
         scratch_shapes=[
             pltpu.VMEM(w_gate.shape, BF16),
@@ -1853,6 +1873,7 @@
             pltpu.VMEM((chunks, seq, thin, width), BF16),
             blocks,
             blocks,
+            pltpu.VMEM((rows, 128), F32),
             pltpu.SemaphoreType.DMA((n_sems,)),
             pltpu.SemaphoreType.DMA((n_sems,)),
             *[pltpu.VMEM(shape, BF16) for shape in shapes],
@@ -1866,7 +1887,7 @@
         w_out,
         tokens,
         cotangent,
-        row_scale,
+        counts,
         gain_rows,
         mod_rows,
         w_gate,
@@ -1895,8 +1916,8 @@
         cap_raw,
         gain_rows,
         mod_rows,
-        key_bias,
-        cap_bias,
+        counts,
+        cap_lens,
         mixed,
         hidden,
         captions,
@@ -1904,12 +1925,13 @@
         d_tokens,
         row_sums,
     ) = refs[:24]
-    tokens_grad, vec_all, refs = refs[24], refs[25], refs[26:]
+    tokens_grad, mod_all, small_out, refs = refs[24], refs[25], refs[26], refs[27:]
     outs, refs = refs[:count], refs[count:]
     mixed_low, cross_low, query_acc, key_acc, value_acc, cap_key_acc, cap_value_acc = refs[:7]
-    d_query, d_key, d_value, d_cap_key, d_cap_value, d_hidden, vec, vec_seq, vec_sum = refs[7:16]
-    parts, from_left, from_right, send, recv = refs[16:21]
-    grads, refs = refs[21 : 21 + count], refs[21 + count :]
+    d_query, d_key, d_value, d_cap_key, d_cap_value, d_hidden, vec = refs[7:14]
+    mod_give, mod_got, mod_sum, wide_give, wide_got, slim_give, slim_got = refs[14:21]
+    key_bias, cap_bias, parts, from_left, from_right, send, recv = refs[21:28]
+    grads, refs = refs[28 : 28 + count], refs[28 + count :]
     b, s = lax.axis_index("bucket"), lax.axis_index("seq")
     copies = Copies(send, recv)
     sums = GradSums(copies, b, s, buckets, seq, kinds, grads, outs, refs, near=True)
@@ -1927,6 +1949,11 @@
         return gain_rows[row : row + 1, pl.ds(at, 128)]
 
     vec[...] = jnp.zeros_like(vec)
+    mod_give[...] = jnp.zeros_like(mod_give)
+    wide_give[...] = jnp.zeros_like(wide_give)
+    slim_give[...] = jnp.zeros_like(slim_give)
+    fill_rows(key_bias, counts[b], 0, 0.0, -1e30)
+    fill_rows(cap_bias, cap_lens[b], 0, 0.0, -1e30)
     mixed_low[...] = right_dot(d_attn[...], w_out[...]).astype(BF16)
 
     def own_sum(row, pair, total):
@@ -1943,7 +1970,7 @@
             return total + jnp.sum(d * cross_out[at, lane], axis=0, keepdims=True)
 
         total = lax.fori_loop(0, rows // 128, body, jnp.zeros((1, 128), F32))
-        own_sum(11, pair, total * (1.0 - gate * gate))
+        own_sum(7, pair, total * (1.0 - gate * gate))
 
     def attend_back(pair, k_ref, v_ref, bias, d_ref, k_acc, v_acc, add):
         lane = slice(pair * 128, (pair + 1) * 128)
@@ -1983,19 +2010,15 @@
             gain = gain_of(row, pair)
 
             def body(i, total):
-                at = pl.ds(pl.multiple_of(i * 64, 64), 64)
+                at = pl.ds(pl.multiple_of(i * 128, 128), 128)
                 x, d = raw[at, lane], d_norm[at, lane]
                 size = pair_scale(x, 1e-06)
                 normed, inner = x * size, d * gain
-                low = low_half(x.shape)
-                product = inner * normed
-                first = jnp.sum(jnp.where(low, product, 0.0), axis=-1, keepdims=True)
-                second = jnp.sum(jnp.where(low, 0.0, product), axis=-1, keepdims=True)
-                mean = jnp.where(low, first, second) * (1.0 / HEAD_DIM)
+                mean = pair_sums(inner * normed) * (1.0 / HEAD_DIM)
                 out[at, lane] = (size * (inner - normed * mean)).astype(BF16)
                 return total + jnp.sum(d * normed, axis=0, keepdims=True)
 
-            total = lax.fori_loop(0, raw.shape[0] // 64, body, jnp.zeros((1, 128), F32))
+            total = lax.fori_loop(0, raw.shape[0] // 128, body, jnp.zeros((1, 128), F32))
             own_sum(sum_row, pair, total)
 
     def weight_grads(left, chosen):
@@ -2017,25 +2040,19 @@
         sums.begin(0)
 
     pl.semaphore_wait(pltpu.get_barrier_semaphore(), peers)
-    out_grad()
     for pair in range(pairs):
         cross_part(pair)
         attend_back(pair, cap_key, cap_value, cap_bias, cross_low, cap_key_acc, cap_value_acc, False)
-    norm_back(cap_raw, cap_key_acc, d_cap_key, 6, 10)
+    norm_back(cap_raw, cap_key_acc, d_cap_key, 6, 6)
     d_cap_value[...] = cap_value_acc[...].astype(BF16)
     for _ in weight_grads(captions, ((1, d_cap_key), (2, d_cap_value))):
         pass
-    steps = {
-        0: (lambda: sums.stage_a(0), lambda: sums.stage_a(1)),
-        1: (lambda: sums.stage_b(0), lambda: sums.stage_b(1), lambda: sums.stage_a(2)),
-        2: (lambda: sums.stage_c(0), lambda: sums.stage_b(2), lambda: sums.stage_c(1)),
-    }
+    steps = (lambda: sums.stage_a(1), lambda: sums.stage_a(2), lambda: sums.stage_b(1))
     for pair in range(pairs):
         attend_back(pair, key, value, key_bias, mixed_low, key_acc, value_acc, True)
-        for step in steps.get(pair, ()):
-            step()
-    norm_back(query_raw, query_acc, d_query, 4, 8)
-    norm_back(key_raw, key_acc, d_key, 5, 9)
+        steps[pair]()
+    norm_back(query_raw, query_acc, d_query, 4, 4)
+    norm_back(key_raw, key_acc, d_key, 5, 5)
     d_value[...] = value_acc[...].astype(BF16)
     pour = Pour(copies, parts, from_left, from_right, b, s, seq)
     wide = 512
@@ -2045,16 +2062,18 @@
         total = total + right_dot(d_value[...], w_value[cols, :])
         parts[:, :, cols] = total.astype(BF16).reshape(seq, rows // seq, wide)
     pieces = weight_grads(hidden, ((3, d_query), (4, d_key), (5, d_value)))
+    between = {1: out_grad, 2: lambda: sums.stage_b(2)}
     for q in range(pour.count):
         pour.step(q)
-        next(pieces, None)
+        if q in between:
+            between[q]()
+        elif q > 2:
+            next(pieces, None)
     for _ in pieces:
         pass
+    sums.stage_a(0)
+    sums.stage_c(1)
     sums.stage_c(2)
-    sums.stage_a(3)
-    sums.stage_a(4)
-    sums.stage_b(3)
-    sums.stage_a(5)
     pour.end(d_hidden)
 
     factor = gain_rows[0:1, :] * (1.0 + mod_rows[0:1, :])
@@ -2070,54 +2089,87 @@
 
     total = lax.fori_loop(0, tokens.shape[0] // 16, body, jnp.zeros((1, width), F32))
     post, last = jnp.tanh(mod_rows[1:2, :]), jnp.tanh(mod_rows[3:4, :])
-    vec[0:1, :] = total * gain_rows[0:1, :]
-    vec[1:2, :] = row_sums[0:1, :] * gain_rows[1:2, :] * (1.0 - post * post)
-    vec[2:3, :] = row_sums[1:2, :] * gain_rows[2:3, :]
-    vec[3:4, :] = row_sums[2:3, :] * gain_rows[3:4, :] * (1.0 - last * last)
-    vec[4:5, :] = total * (1.0 + mod_rows[0:1, :])
-    vec[5:6, :] = row_sums[0:1, :] * post
-    vec[6:7, :] = row_sums[1:2, :] * (1.0 + mod_rows[2:3, :])
-    vec[7:8, :] = row_sums[2:3, :] * last
-    vec_moves = []
-    for k in range(1, seq):
-        vec_moves.append(sums.go(copies.remote(vec, vec_seq.at[k], b, lax.rem(s + k, seq))))
-    sums.stage_b(4)
-    sums.stage_b(5)
-    for move in vec_moves:
+    vec[8:9, :] = total * gain_rows[0:1, :]
+    vec[9:10, :] = row_sums[0:1, :] * gain_rows[1:2, :] * (1.0 - post * post)
+    vec[10:11, :] = row_sums[1:2, :] * gain_rows[2:3, :]
+    vec[11:12, :] = row_sums[2:3, :] * gain_rows[3:4, :] * (1.0 - last * last)
+    vec[0:1, :] = total * (1.0 + mod_rows[0:1, :])
+    vec[1:2, :] = row_sums[0:1, :] * post
+    vec[2:3, :] = row_sums[1:2, :] * (1.0 + mod_rows[2:3, :])
+    vec[3:4, :] = row_sums[2:3, :] * last
+    piece, wide = width // 4, width // buckets
+    slim = wide // seq
+    for t in range(seq):
+        for j in range(4):
+            mod_give[t, j : j + 1, :] = vec[8 + t : 9 + t, j * piece : (j + 1) * piece]
+    for t in range(buckets):
+        wide_give[t, :, :wide] = vec[0:8, t * wide : (t + 1) * wide]
+    mod_moves, wide_moves = [], []
+    for j in range(1, seq):
+        peer = lax.rem(s + j, seq)
+        mod_moves.append(sums.go(copies.remote(mod_give.at[peer], mod_got.at[j], b, peer)))
+    for j in range(1, buckets):
+        peer = lax.rem(b + j, buckets)
+        wide_moves.append(sums.go(copies.remote(wide_give.at[peer], wide_got.at[j], peer, s)))
+    sums.stage_a(3)
+    sums.stage_a(4)
+    sums.stage_a(5)
+    total = mod_give[s]
+    for j, move in enumerate(mod_moves, 1):
         move.wait_recv()
-    add_rows(vec_sum, [vec] + [vec_seq.at[k] for k in range(1, seq)])
-    vec_next = []
-    for k in range(1, buckets):
-        peer = lax.rem(b + k, buckets)
-        vec_next.append(sums.go(copies.remote(vec_sum, vec_all.at[b], peer, s)))
-    vec_own = copies.local(vec_sum, vec_all.at[b])
-    vec_own.start()
+        total = total + mod_got[j]
+    mod_sum[...] = total
+    mod_next, slim_next = [], []
+    for j in range(1, buckets):
+        peer = lax.rem(b + j, buckets)
+        mod_next.append(sums.go(copies.remote(mod_sum, mod_all.at[b], peer, s)))
+    mod_own = copies.local(mod_sum, mod_all.at[b])
+    mod_own.start()
+    total = wide_give[b]
+    for j, move in enumerate(wide_moves, 1):
+        move.wait_recv()
+        total = total + wide_got[j]
+    for t in range(seq):
+        slim_give[t, :, :slim] = total[:, t * slim : (t + 1) * slim]
+    for j in range(1, seq):
+        peer = lax.rem(s + j, seq)
+        slim_next.append(sums.go(copies.remote(slim_give.at[peer], slim_got.at[j], b, peer)))
+    for w in (0, 3, 4, 5):
+        sums.stage_b(w)
+    sums.stage_c(0)
     for w in (3, 4, 5):
         sums.stage_c(w)
     sums.stage_d(0)
-    for move in vec_next:
+    total = slim_give[s]
+    for j, move in enumerate(slim_next, 1):
         move.wait_recv()
-    vec_own.wait()
+        total = total + slim_got[j]
+    small_out[...] = total
+    for move in mod_next:
+        move.wait_recv()
+    mod_own.wait()
     sums.end()
 
 
 def backward_all(buckets, seq, inputs, shapes, kinds):
     any_spec = pl.BlockSpec(memory_space=pl.ANY)
     vmem = pl.BlockSpec(memory_space=pltpu.VMEM)
+    smem = pl.BlockSpec(memory_space=pltpu.SMEM)
     shapes, outs, scratch, n_sems = sums_shapes(buckets, seq, shapes, kinds, near=True)
     query, cap_key, tokens = inputs[5], inputs[8], inputs[21]
     rows, width = tokens.shape
     vec = (16, width)
-    n_sems += 8 * seq + 2 * buckets
+    n_sems += 12 * seq + 4 * buckets
     results = pl.pallas_call(
         functools.partial(backward_kernel, buckets, seq, tuple(kinds)),
         out_shape=[
             jax.ShapeDtypeStruct((rows, width), F32),
-            jax.ShapeDtypeStruct((buckets,) + vec, F32),
+            jax.ShapeDtypeStruct((buckets, 8, width // 4), F32),
+            jax.ShapeDtypeStruct((8, 128), F32),
             *outs,
         ],
-        in_specs=[vmem] * len(inputs),
-        out_specs=[vmem, any_spec] + [vmem] * len(outs),
+        in_specs=[vmem] * 16 + [smem] * 2 + [vmem] * (len(inputs) - 18),
+        out_specs=[vmem, any_spec, vmem] + [vmem] * len(outs),
         scratch_shapes=[
             pltpu.VMEM(query.shape, BF16),
             pltpu.VMEM(query.shape, BF16),
@@ -2133,8 +2185,15 @@
             pltpu.VMEM(cap_key.shape, BF16),
             pltpu.VMEM((rows, width), F32),
             pltpu.VMEM(vec, F32),
-            pltpu.VMEM((seq,) + vec, F32),
-            pltpu.VMEM(vec, F32),
+            pltpu.VMEM((seq, 8, width // 4), F32),
+            pltpu.VMEM((seq, 8, width // 4), F32),
+            pltpu.VMEM((8, width // 4), F32),
+            pltpu.VMEM((buckets, 8, 256), F32),
+            pltpu.VMEM((buckets, 8, 256), F32),
+            pltpu.VMEM((seq, 8, 128), F32),
+            pltpu.VMEM((seq, 8, 128), F32),
+            pltpu.VMEM((query.shape[0], 128), F32),
+            pltpu.VMEM((cap_key.shape[0], 128), F32),
             pltpu.VMEM((seq, rows, width), BF16),
             pltpu.VMEM((seq - 1, rows, width), BF16),
             pltpu.VMEM((seq - 1, rows, width), BF16),
@@ -2147,7 +2206,52 @@
             collective_id=10, has_side_effects=True, vmem_limit_bytes=62 * 2**20
         ),
     )(*inputs)
-    return results[0], results[1], [out.reshape(-1, out.shape[-1]) for out in results[2:]]
+    sums = [out.reshape(-1, out.shape[-1]) for out in results[3:]]
+    return results[0], results[1], results[2], sums
+
+
+def last_kernel(buckets, seq, slim, *refs):
+    cond, mod_all, small = refs[:3]
+    count = (len(refs) - 7) // 2
+    sources, refs = refs[3 : 3 + count], refs[3 + count :]
+    mod_grad, gains, cross = refs[:3]
+    targets, sems = refs[3 : 3 + count], refs[3 + count]
+    copies = [
+        pltpu.make_async_copy(a, b, sems.at[i])
+        for i, (a, b) in enumerate(zip(sources, targets, strict=True))
+    ]
+    for copy in copies:
+        copy.start()
+    piece = mod_all.shape[2]
+    for j in range(4):
+        total = None
+        for k in range(buckets):
+            term = cond[:, k : k + 1] * mod_all[k, j : j + 1, :]
+            total = term if total is None else total + term
+        mod_grad[:, j * piece : (j + 1) * piece] = total
+    gains[...] = small[0:7, :slim]
+    cross[...] = small[7:8, :slim]
+    for copy in copies:
+        copy.wait()
+
+
+def last_all(buckets, seq, slim, cond, mod_all, small, results):
+    any_spec = pl.BlockSpec(memory_space=pl.ANY)
+    vmem = pl.BlockSpec(memory_space=pltpu.VMEM)
+    outs = pl.pallas_call(
+        functools.partial(last_kernel, buckets, seq, slim),
+        out_shape=[
+            jax.ShapeDtypeStruct((cond.shape[0], 4 * mod_all.shape[2]), F32),
+            jax.ShapeDtypeStruct((7, slim), F32),
+            jax.ShapeDtypeStruct((1, slim), F32),
+            *[jax.ShapeDtypeStruct(x.shape, x.dtype) for x in results],
+        ],
+        in_specs=[vmem] * 3 + [any_spec] * len(results),
+        out_specs=[vmem] * (3 + len(results)),
+        scratch_shapes=[pltpu.SemaphoreType.DMA((len(results),))],
+        compiler_params=pltpu.CompilerParams(vmem_limit_bytes=62 * 2**20),
+    )(cond, mod_all, small, *results)
+    return outs[0], outs[1], outs[2].reshape(slim), outs[3:]
 
 
 def on_device(
@@ -2176,8 +2280,6 @@
     rows, width = tokens.shape
     span = rows * seq
     share = width // seq
-    live_rows, cap_len = pick_entry(counts, b), pick_entry(cap_lens, b)
-    token_total = jnp.sum(counts).astype(F32)
 
     cond_size = w_mod.shape[0] * buckets * seq
     cond = jax.nn.silu(time_embed(steps_t, cond_size)).astype(BF16)
@@ -2185,9 +2287,6 @@
     slim = gains.shape[1]
     small = jnp.concatenate([gains, cross_gate[None]], axis=0).astype(F32)
     small = jnp.pad(small, ((0, 0), (0, 128 - slim)))
-    key_mask = jnp.broadcast_to((jnp.arange(span) < live_rows)[:, None], (span, 128)).astype(BF16)
-    cap_span = captions.shape[0] * seq
-    cap_mask = jnp.broadcast_to((jnp.arange(cap_span) < cap_len)[:, None], (cap_span, 128))
     cap_all, weights, inner = forward_all(
         buckets,
         seq,
@@ -2197,7 +2296,7 @@
         slim,
         cond_part,
         w_mod,
-        [key_mask, cap_mask.astype(BF16)],
+        [counts, cap_lens],
         [w_query, w_key, w_value, w_cap_key, w_cap_value, w_out, w_gate, w_up, w_down],
         ["col", "col", "col", "col", "col", "row", "col", "col", "row"],
     )
@@ -2206,8 +2305,6 @@
     small_rows, mod, hidden, query_proj, key_proj, cap_proj = inner[:6]
     query, key, value, cap_key, cap_value = inner[6:11]
     cross_out, mixed_low = inner[11:]
-    row_live = (s * rows + jnp.arange(rows) < live_rows).astype(F32)
-    row_scale = row_live * (buckets * span / token_total)
     (block_out, d_tokens, d_attn_all, row_sums), (s_gate, s_up, s_down) = middle_all(
         buckets,
         seq,
@@ -2215,13 +2312,11 @@
         (wo, wg, wu, wd),
         tokens,
         cotangent,
-        jnp.broadcast_to(row_scale[:, None], (rows, 128)),
+        counts,
         small_rows,
         mod,
     )
-    key_bias = jnp.where(jnp.arange(span) < live_rows, 0.0, -1e30).astype(F32)
-    cap_bias = jnp.where(jnp.arange(cap_span) < cap_len, 0.0, -1e30).astype(F32)
-    tokens_grad, vec_all, sums = backward_all(
+    tokens_grad, mod_all, small_sums, sums = backward_all(
         buckets,
         seq,
         [
@@ -2241,8 +2336,8 @@
             cap_proj,
             small_rows,
             mod,
-            jnp.broadcast_to(key_bias[:, None], (span, 128)),
-            jnp.broadcast_to(cap_bias[:, None], (cap_span, 128)),
+            counts,
+            cap_lens,
             mixed_low,
             hidden,
             caps,
@@ -2255,30 +2350,14 @@
     )
     s_out, s_cap_key, s_cap_value, s_query, s_key, s_value = sums
 
-    quarter = 4 * width // seq
-    mod_rows = vec_all[:, :4].reshape(buckets, -1, quarter)
-    mod_rows = lax.dynamic_slice_in_dim(mod_rows, s, 1, 1)[:, 0]
     cond_size = cond.shape[1] // buckets
-    cond_cols = lax.dynamic_slice_in_dim(cond, b * cond_size, cond_size, 1).astype(F32)
-    s_mod = jnp.sum(cond_cols[:, :, None] * mod_rows[:, None, :], axis=0)
-    tail = lax.dynamic_slice(vec_all, (0, 4, place * slim), (buckets, 8, slim))
-    tail = jnp.sum(tail, axis=0)
-    return (
-        block_out,
-        tokens_grad,
-        s_query,
-        s_key,
-        s_value,
-        s_out,
-        s_cap_key,
-        s_cap_value,
-        s_gate,
-        s_up,
-        s_down,
-        s_mod,
-        tail[:7],
-        tail[7],
+    cond_cols = lax.dynamic_slice_in_dim(cond, b * cond_size, cond_size, 1).astype(F32).T
+    results = [block_out, tokens_grad, s_query, s_key, s_value, s_out]
+    results += [s_cap_key, s_cap_value, s_gate, s_up, s_down]
+    s_mod, s_gains, s_cross, results = last_all(
+        buckets, seq, slim, cond_cols, mod_all, small_sums, results
     )
+    return (*results, s_mod, s_gains, s_cross)
 
 
 def solution(mesh):

time: 505 us -> 465 us (0.921)
  Pallas kernels: 469 us -> 451 us
  local copies, waits for them, and re-layouts: 16.3 us -> 1.2 us
  other arithmetic: 9.11 us -> 2.92 us
    pallas_call x1, Pallas kernels: 118 us -> 97.7 us  [backward_all(): pl.pallas_call(functools.partial(backward_kernel, buckets, seq, tuple(kin...]
    unnamed x34 -> x0, local copies, waits for them, and re-layouts: 10.1 us -> none
    pallas_call x0 -> x1, Pallas kernels: none -> 6.72 us  [last_all(): pl.pallas_call(functools.partial(last_kernel, buckets, seq, slim), out_sh...]
where the time goes in v4:
time: 465 us; the launch traced here: 457 us
  Pallas kernels  451 us (97%)
    pallas_call x1, Pallas kernels, middle_all(): pl.pallas_call(functools.partial(middle_kernel, buckets, seq, chunks, kin...  184 us
    pallas_call x1, Pallas kernels, forward_all(): pl.pallas_call(functools.partial(forward_kernel, buckets, seq, tuple(kind...  163 us
    pallas_call x1, Pallas kernels, backward_all(): pl.pallas_call(functools.partial(backward_kernel, buckets, seq, tuple(kin...  97.7 us

profile of v4, /device:TPU:8, one launch (start us, length us, event | category | flops | bytes accessed | tf_op | source)
XLA Modules:
  0.0 456.7 jit_solution(2018192532961104608)
XLA Ops:
  0.7 0.7 convert_element_type.10
  1.3 1.3 fusion.3.refs_2_
  2.6 0.1 multiply_cosine_fusion
  2.8 0.2 copy.37
  3.0 0.1 add_divide_fusion
  3.1 0.2 copy.40
  3.3 0.2 copy.41
  3.5 0.6 convert_bitcast_fusion.refs_0_
  4.2 0.7 copy.42.refs_3_
  4.8 162.7 %shard_map.281 = (bf16[4,64,4096]{2,1,0:T(8,128)(2,1)}, bf16[8,4,48,384]{3,2,1,0:T(8,128)(2,1)}, bf16[8,4,48,384]{3,2,1,0:T(8,128)(2,1)}, bf16[8,4,48,384]{3,2,1...) custom-call(bf16[128,1536]{1,0:T(8,128)(2,1)} %refs_21_.1, ...), custom_call_target="tpu_custom_call" | custom-call | tf_op jit(solution)/shard_map/pallas_call | solution.py:1550
  167.5 184.3 %shard_map.282 = (bf16[128,1536]{1,0:T(8,128)(2,1)}, f32[128,1536]{1,0:T(8,128)}, bf16[4,128,1536]{2,1,0:T(8,128)(2,1)}, f32[8,1536]{1,0:T(8,128)}, f32[192,1024...) custom-call(bf16[4,128,384]{2,1,0:T(8,128)(2,1)} %bitcast.23, bf16[384,1536]{1,0:T(8,128)(2,1)} %bitcast.16, ...), custom_call_target="tpu_custom_call" | custom-call | tf_op jit(solution)/shard_map/pallas_call | solution.py:1850
  351.8 97.7 %shard_map.283 = (f32[128,1536]{1,0:T(8,128)}, f32[8,8,384]{2,1,0:T(8,128)}, f32[8,128]{1,0:T(8,128)}, f32[4,48,384]{2,1,0:T(8,128)}, f32[512,384]{1,0:T(8,128)}...) custom-call(bf16[512,1536]{1,0:T(8,128)(2,1)} %bitcast.22, ...), custom_call_target="tpu_custom_call" | custom-call | tf_op jit(solution)/shard_map/pallas_call | solution.py:2163
  449.5 6.7 %shard_map.284 = (f32[128,1536]{1,0:T(8,128)}, f32[7,48]{1,0:T(8,128)}, f32[1,48]{1,0:T(1,128)}, bf16[128,1536]{1,0:T(8,128)(2,1)}, f32[128,1536]{1,0:T(8,128)},...) custom-call(f32[128,8]{1,0:T(8,128)} %convert_bitcast_fusion.refs_0_, ...), custom_call_target="tpu_custom_call" | custom-call | tf_op jit(solution)/shard_map/pallas_call | solution.py:2241
  (4 shorter events, 0.0 us)

commit v5 on v4

--- a/solution.py
+++ b/solution.py
@@ -710,8 +710,9 @@
             add_rows(self.outs[w], terms)
             return
         seq, send, recv = self.seq, self.copies.send, self.copies.recv
-        wide = self.outs[w].shape[-1]
-        me = lax.rem(self.place, seq)
+        wide = done.shape[-1]
+        far = self.kinds[w] == "row"
+        to_b, me = (self.to_b, lax.rem(self.place, seq)) if far else (self.b, self.s)
         base = self.copies.take(2 * seq)
         rows = terms[0].shape[0]
         step = 16 if rows % 16 == 0 else rows
@@ -733,11 +734,11 @@
                 dst_ref=landed.at[me],
                 send_sem=send.at[base + t],
                 recv_sem=recv.at[base + me],
-                device_id={"bucket": self.to_b, "seq": t},
+                device_id={"bucket": to_b, "seq": t},
                 device_id_type=MESH,
             )
             keep = pltpu.make_async_copy(done.at[t], landed.at[me], send.at[base + seq + t])
-            here = jnp.logical_and(self.to_b == self.b, self.s == t)
+            here = jnp.logical_and(to_b == self.b, self.s == t) if far else self.s == t
 
             @pl.when(jnp.logical_not(here))
             def _():
@@ -751,7 +752,7 @@
         self.last[w] = (base, moves)
 
     def stage_d(self, w):
-        if self.kinds[w] != "row":
+        if self.kinds[w] == "col":
             return
         done, landed = self.scratch[w][6:]
         base, moves = self.last[w]
@@ -760,6 +761,8 @@
             d = self.b * seq + j
             from_b = slot(lax.rem(d, buckets), buckets)
             here = jnp.logical_and(from_b == self.b, lax.div(d, buckets) == self.s)
+            if self.kinds[w] != "row":
+                here = self.s == j
 
             @pl.when(jnp.logical_not(here))
             def _():
@@ -783,7 +786,12 @@
                 keep.wait()
 
         for j in range(seq):
-            add_rows(out.at[j], [landed.at[j]])
+            if self.kinds[w] != "strip":
+                add_rows(out.at[j], [landed.at[j]])
+                continue
+            for part in range(landed.shape[-1] // 128):
+                cols = slice((part * seq + j) * 128, (part * seq + j + 1) * 128)
+                out[:, cols] = landed[j, :, part * 128 : (part + 1) * 128].astype(F32)
 
     def steps(self):
         count = len(self.kinds)
@@ -833,9 +841,9 @@
             scratch += [pltpu.VMEM((rows, wide), BF16)] * 2
         else:
             scratch += [tiny, tiny, pltpu.VMEM((chips, rows, wide), BF16), tiny]
-        shape = (seq, rows, wide // seq) if kind == "row" else (rows, wide)
-        outs.append(jax.ShapeDtypeStruct(shape, F32))
-        scratch += [pltpu.VMEM(shape, BF16) if kind == "row" else tiny] * 2
+        split = (seq, rows, wide // seq)
+        outs.append(jax.ShapeDtypeStruct(split if kind in ("row", "stay") else (rows, wide), F32))
+        scratch += [tiny if kind == "col" else pltpu.VMEM(split, BF16)] * 2
     n_sems = 32 + 2 * buckets + len(shapes) * (8 + 3 * seq + buckets)
     return inputs, outs, scratch, n_sems
 
@@ -1122,9 +1130,140 @@
     out[...] = jnp.where(row < live, yes, no).astype(out.dtype)
 
 
-FORWARD_ORDER = ("tok", 0, "tok", 1, "tok", 2, "tok", 6, 7, "cap", 8, 3, "cap", 4, "cap", 5, "cap")
+FORWARD_ORDER = (8, "tok", 0, "tok", 1, "tok", 2, "tok", 6, 7, "cap", 3, "cap", 4, "cap", 5, "cap")
+MOVED = ()
 LAG = 1
 WINDOW = 2
+
+
+class Gather:
+    def __init__(self, copies, b, s, buckets, seq, kinds, shards, fulls, keep_at=None):
+        self.copies, self.b, self.s, self.buckets, self.seq = copies, b, s, buckets, seq
+        self.kinds, self.shards, self.fulls, self.keep_at = kinds, shards, fulls, keep_at
+        place = b * seq + s
+        self.to_slot, self.to_s = lax.rem(place, buckets), lax.div(place, buckets)
+        self.to_b = slot(self.to_slot, buckets)
+        back = s * buckets + slot(b, buckets)
+        self.from_b, self.from_s = lax.div(back, seq), lax.rem(back, seq)
+        self.stays = jnp.logical_and(self.to_b == b, self.to_s == s)
+        self.twin, self.near_x, self.near_y = flip(b, 1), flip(b, 2), flip(b, 4)
+        self.far = flip(self.near_x, 4)
+        self.first, self.second, self.kept, self.sent = {}, {}, [], []
+
+    def greet_source(self):
+        @pl.when(jnp.logical_not(self.stays))
+        def _():
+            greet(self.from_b, self.from_s)
+
+        return jnp.where(self.stays, 0, 1)
+
+    def go(self, src, dst, b):
+        copy = self.copies.remote(src, dst, b, self.s)
+        copy.start()
+        self.sent.append(copy)
+        return copy
+
+    def depart(self, at):
+        copies, b, s, seq = self.copies, self.b, self.s, self.seq
+        shard, full = self.shards[at], self.fulls[at]
+        if self.kinds[at] == "stay":
+            keep = copies.local(shard, full.at[b])
+            keep.start()
+            self.first[at] = ((), keep)
+            return
+        if self.kinds[at] == "row":
+            move = copies.remote(shard, full.at[self.to_slot], self.to_b, self.to_s)
+            keep = copies.local(shard, full.at[slot(b, self.buckets)])
+
+            @pl.when(jnp.logical_not(self.stays))
+            def _():
+                move.start()
+
+            @pl.when(self.stays)
+            def _():
+                keep.start()
+
+            self.first[at] = (move, keep)
+            return
+        wide = full.shape[-1]
+
+        def columns(peer):
+            if self.kinds[at] == "cut":
+                return shard.at[peer]
+            return shard.at[:, pl.ds(pl.multiple_of(peer * wide, 128), wide)]
+
+        moves = []
+        for k in range(1, seq):
+            peer = lax.rem(s + k, seq)
+            move = copies.remote(columns(peer), full.at[b, s], b, peer)
+            move.start()
+            moves.append(move)
+        keep = copies.local(columns(s), full.at[b, s])
+        keep.start()
+        self.first[at] = (moves, keep)
+
+    def arrived(self, at):
+        moves, keep = self.first[at]
+        if self.kinds[at] == "row":
+
+            @pl.when(jnp.logical_not(self.stays))
+            def _():
+                moves.wait()
+
+            @pl.when(self.stays)
+            def _():
+                keep.wait()
+
+            return
+        for move in moves:
+            move.wait()
+        keep.wait()
+
+    def index(self, at, device):
+        return slot(device, self.buckets) if self.kinds[at] == "row" else device
+
+    def stage_a(self, at):
+        block = self.fulls[at].at[self.index(at, self.b)]
+        self.second[at] = {
+            "x": self.go(block, block, self.near_x),
+            "y": self.go(block, block, self.near_y),
+            "twin": [self.go(block, block, self.twin)],
+        }
+
+    def stage_b(self, at):
+        full, now = self.fulls[at], self.second[at]
+        cut = halves_of(full.shape[1:])
+        now["x"].wait_recv()
+        block = full.at[self.index(at, self.near_x), pl.ds(0, cut)]
+        now["dy"] = self.go(block, block, self.near_y)
+        block = full.at[self.index(at, self.near_x)]
+        now["twin"].append(self.go(block, block, self.twin))
+        now["y"].wait_recv()
+        block = full.at[self.index(at, self.near_y), pl.ds(cut, full.shape[1] - cut)]
+        now["dx"] = self.go(block, block, self.near_x)
+        block = full.at[self.index(at, self.near_y)]
+        now["twin"].append(self.go(block, block, self.twin))
+
+    def stage_c(self, at):
+        full, now = self.fulls[at], self.second[at]
+        now["dy"].wait_recv()
+        now["dx"].wait_recv()
+        block = full.at[self.index(at, self.far)]
+        now["twin"].append(self.go(block, block, self.twin))
+
+    def stage_d(self, at):
+        for move in self.second[at]["twin"]:
+            move.wait_recv()
+        if self.keep_at is not None:
+            copy = self.copies.local(self.fulls[at], self.keep_at[at])
+            copy.start()
+            self.kept.append(copy)
+
+    def end(self):
+        for copy in self.kept:
+            copy.wait()
+        for move in self.sent:
+            move.wait_send()
 
 
 def forward_kernel(buckets, seq, kinds, slim, *refs):
@@ -1153,24 +1292,24 @@
     refs = refs[13:]
     part, got_bucket, got_seq, mod_sum, small_all, tok_all, cap_near, own_out = refs[:8]
     fulls = refs[8 : 8 + count]
-    key_mask, cap_mask, send, recv = refs[8 + count :]
+    key_mask, cap_mask, send, recv = refs[8 + count : 12 + count]
+    strips = refs[12 + count :]
     b, s = lax.axis_index("bucket"), lax.axis_index("seq")
     copies = Copies(send, recv)
-    place = b * seq + s
-    to_slot, to_s = lax.rem(place, buckets), lax.div(place, buckets)
-    to_b = slot(to_slot, buckets)
-    back = s * buckets + slot(b, buckets)
-    from_b, from_s = lax.div(back, seq), lax.rem(back, seq)
-    stays = jnp.logical_and(to_b == b, to_s == s)
-
+    shards = list(shards)
+    cuts = [at for at in range(count) if kinds[at] == "cut"]
+    for at, strip in zip(cuts, strips, strict=True):
+        for t in range(seq):
+            for j in range(strip.shape[2] // 128):
+                cols = slice((j * seq + t) * 128, (j * seq + t + 1) * 128)
+                strip[t, :, j * 128 : (j + 1) * 128] = shards[at][:, cols]
+        shards[at] = strip
+    weights = Gather(copies, b, s, buckets, seq, kinds, shards, fulls, far_fulls)
     for k in range(1, buckets):
         greet(lax.rem(b + k, buckets), s)
     for k in range(1, seq):
         greet(b, lax.rem(s + k, seq))
-
-    @pl.when(jnp.logical_not(stays))
-    def _():
-        greet(from_b, from_s)
+    peers = buckets - 1 + seq - 1 + weights.greet_source()
 
     fill_rows(key_mask, counts[b], 0, 1.0, 0.0)
     fill_rows(cap_mask, cap_lens[b], 0, 1.0, 0.0)
@@ -1178,7 +1317,6 @@
     for j in range(part.shape[1]):
         part[:, j, :] = bf_dot(cond[...], w_mod[:, j * lanes : (j + 1) * lanes])
 
-    peers = buckets - 1 + seq - 1 + jnp.where(stays, 0, 1)
     pl.semaphore_wait(pltpu.get_barrier_semaphore(), peers)
 
     sent = []
@@ -1208,101 +1346,6 @@
             step[what] += 1
         else:
             items.append((None, what))
-
-    first = [None] * count
-
-    def depart(at):
-        kind, shard, full = kinds[at], shards[at], fulls[at]
-        if kind == "row":
-            move = copies.remote(shard, full.at[to_slot], to_b, to_s)
-            keep = copies.local(shard, full.at[slot(b, buckets)])
-
-            @pl.when(jnp.logical_not(stays))
-            def _():
-                move.start()
-
-            @pl.when(stays)
-            def _():
-                keep.start()
-
-            first[at] = (move, keep)
-            return
-        wide = full.shape[-1]
-
-        def columns(peer):
-            return shard.at[:, pl.ds(pl.multiple_of(peer * wide, 128), wide)]
-
-        moves = []
-        for k in range(1, seq):
-            peer = lax.rem(s + k, seq)
-            move = copies.remote(columns(peer), full.at[b, s], b, peer)
-            move.start()
-            moves.append(move)
-        keep = copies.local(columns(s), full.at[b, s])
-        keep.start()
-        first[at] = (moves, keep)
-
-    def arrived(at):
-        moves, keep = first[at]
-        if kinds[at] == "row":
-
-            @pl.when(jnp.logical_not(stays))
-            def _():
-                moves.wait()
-
-            @pl.when(stays)
-            def _():
-                keep.wait()
-
-            return
-        for move in moves:
-            move.wait()
-        keep.wait()
-
-    twin = flip(b, 1)
-    near_x, near_y = flip(b, 2), flip(b, 4)
-    far = flip(near_x, 4)
-    second = [None] * count
-
-    def index(at, device):
-        return slot(device, buckets) if kinds[at] == "row" else device
-
-    def stage_a(at):
-        block = fulls[at].at[index(at, b)]
-        second[at] = {
-            "x": go(copies.remote(block, block, near_x, s)),
-            "y": go(copies.remote(block, block, near_y, s)),
-            "twin": [go(copies.remote(block, block, twin, s))],
-        }
-
-    def stage_b(at):
-        full, now = fulls[at], second[at]
-        cut = halves_of(full.shape[1:])
-        now["x"].wait_recv()
-        block = full.at[index(at, near_x), pl.ds(0, cut)]
-        now["dy"] = go(copies.remote(block, block, near_y, s))
-        block = full.at[index(at, near_x)]
-        now["twin"].append(go(copies.remote(block, block, twin, s)))
-        now["y"].wait_recv()
-        block = full.at[index(at, near_y), pl.ds(cut, full.shape[1] - cut)]
-        now["dx"] = go(copies.remote(block, block, near_x, s))
-        block = full.at[index(at, near_y)]
-        now["twin"].append(go(copies.remote(block, block, twin, s)))
-
-    fetched = {}
-
-    def stage_c(at):
-        full, now = fulls[at], second[at]
-        now["dy"].wait_recv()
-        now["dx"].wait_recv()
-        block = full.at[index(at, far)]
-        now["twin"].append(go(copies.remote(block, block, twin, s)))
-        for move in now["twin"]:
-            move.wait_recv()
-        go_local = copies.local(full, far_fulls[at])
-        go_local.start()
-        fetched[at] = go_local
-        done.add(at)
 
     def fetch(at):
         whole = fulls[at][...]
@@ -1457,11 +1500,16 @@
     def begin(i):
         relay, j = items[i]
         if relay is None:
-            depart(j)
+            weights.depart(j)
         else:
             relay.start(j)
             if j == seq - 1:
                 done.add("tok" if relay is tok else "cap")
+
+    def complete(at):
+        weights.stage_c(at)
+        weights.stage_d(at)
+        done.add(at)
 
     window = WINDOW
     for i in range(window):
@@ -1487,30 +1535,29 @@
     order = []
     for i, (relay, j) in enumerate(items):
         if relay is None:
-            arrived(j)
+            weights.arrived(j)
         elif j <= seq - 2:
             relay.sent(j)
         if i + window < len(items):
             begin(i + window)
         if relay is None:
             order.append(j)
-            stage_a(j)
+            weights.stage_a(j)
             if len(order) > LAG:
-                stage_b(order[-1 - LAG])
+                weights.stage_b(order[-1 - LAG])
             if len(order) > LAG + 1:
-                stage_c(order[-2 - LAG])
+                complete(order[-2 - LAG])
         do_work()
     cap_out.start()
     for at in range(LAG):
-        stage_b(order[len(order) - LAG + at])
-        stage_c(order[len(order) - LAG - 1 + at])
+        weights.stage_b(order[len(order) - LAG + at])
+        complete(order[len(order) - LAG - 1 + at])
         do_work()
-    stage_c(order[-1])
+    complete(order[-1])
     while do_work():
         pass
     cap_out.wait()
-    for copy in fetched.values():
-        copy.wait()
+    weights.end()
     for move in sent:
         move.wait_send()
 
@@ -1522,7 +1569,7 @@
     fulls = []
     for shard, kind in zip(shards, kinds, strict=True):
         rows, wide = shard.shape
-        shape = (buckets, rows, wide) if kind == "row" else (buckets, seq, rows, wide // seq)
+        shape = (buckets, rows, wide) if kind in ("row", "stay") else (buckets, seq, rows, wide // seq)
         fulls.append(jax.ShapeDtypeStruct(shape, BF16))
     near = [pltpu.VMEM(full.shape, BF16) for full in fulls]
     width = tokens.shape[1]
@@ -1550,7 +1597,8 @@
     outs = pl.pallas_call(
         functools.partial(forward_kernel, buckets, seq, tuple(kinds), slim),
         out_shape=[jax.ShapeDtypeStruct((seq,) + captions.shape, BF16), *fulls, *inner],
-        in_specs=[any_spec, any_spec, any_spec, vmem, vmem, smem, smem] + [any_spec] * len(shards),
+        in_specs=[any_spec, any_spec, any_spec, vmem, vmem, smem, smem]
+        + [vmem if kind == "cut" else any_spec for kind in kinds],
         out_specs=[any_spec] * (1 + len(shards)) + [vmem] * len(inner),
         scratch_shapes=[
             pltpu.VMEM((buckets, 8, mod_lanes), F32),
@@ -1566,14 +1614,18 @@
             pltpu.VMEM((cap_span, 128), BF16),
             pltpu.SemaphoreType.DMA((n_sems,)),
             pltpu.SemaphoreType.DMA((n_sems,)),
+            *(
+                pltpu.VMEM((seq,) + full.shape[2:], BF16)
+                for full, kind in zip(fulls, kinds, strict=True)
+                if kind == "cut"
+            ),
         ],
         compiler_params=pltpu.CompilerParams(
             collective_id=9, has_side_effects=True, vmem_limit_bytes=62 * 2**20
         ),
     )(tokens, captions, small, cond, w_mod, *masks, *shards)
     at = 1 + len(shards)
-    weights = [full.reshape(-1, full.shape[-1]) for full in outs[1:at]]
-    return outs[0], weights, outs[at:]
+    return outs[0], outs[1:at], outs[at:]
 
 
 def middle_kernel(buckets, seq, chunks, kinds, *refs):
@@ -1587,11 +1639,16 @@
     grads, refs = refs[19:22], refs[22:]
     b, s = lax.axis_index("bucket"), lax.axis_index("seq")
     copies = Copies(send, recv)
-    loads = [copies.local(a, b_) for a, b_ in zip(far_weights, (w_gate, w_up, w_down), strict=True)]
+    sums = GradSums(copies, b, s, buckets, seq, kinds, grads, outs, refs, near=True)
+    shards = (w_gate, w_up, w_down)
+    weights = Gather(copies, b, s, buckets, seq, ("cut", "cut", "stay"), far_weights, shards)
+    peers = greet_all(b, s, buckets, seq) + weights.greet_source()
+    pl.semaphore_wait(pltpu.get_barrier_semaphore(), peers)
+    loads = [copies.local(far_weights[w], shards[w]) for w in range(3) if w not in MOVED]
     for load in loads:
         load.start()
-    sums = GradSums(copies, b, s, buckets, seq, kinds, grads, outs, refs, near=True)
-    pl.semaphore_wait(pltpu.get_barrier_semaphore(), greet_all(b, s, buckets, seq))
+    if MOVED:
+        weights.depart(MOVED[0])
 
     rows, width = tokens.shape
     live = sum(counts[k] for k in range(buckets))
@@ -1677,6 +1734,9 @@
         row_sums[0:1, :] += first
         row_sums[1:2, :] += second
 
+    def flat(values):
+        return values.reshape(-1, values.shape[-1])
+
     def put_parts(c, cols, total):
         parts[c, :, :, cols] = total.astype(BF16).reshape(seq, thin, total.shape[-1])
 
@@ -1690,19 +1750,21 @@
         for at in range(0, hidden, wide):
             cols = slice(at, at + wide)
             left = chunk_of(ffn_all, c)
-            gate, up = bf_dot(left, w_gate[:, cols]), bf_dot(left, w_up[:, cols])
+            gate = bf_dot(left, flat(w_gate[:, :, :, cols]))
+            up = bf_dot(left, flat(w_up[:, :, :, cols]))
             gate_keep[c, :, cols], up_keep[c, :, cols] = gate, up
             value = (gate * jax.nn.sigmoid(gate) * up).astype(BF16)
             act[:, of(c), cols] = value.reshape(seq, thin, wide)
         left = chunk_of(act, c)
         for at in range(0, width, wide):
             cols = slice(at, at + wide)
-            put_parts(c, cols, bf_dot(left, w_down[:, cols]))
+            put_parts(c, cols, bf_dot(left, flat(w_down[:, :, cols])))
 
     def ffn_back_product(c):
+        block = w_down.shape[1]
         for at in range(0, hidden, wide):
             cols = slice(at, at + wide)
-            d_act = right_dot(chunk_of(d_ffn, c), w_down[cols, :])
+            d_act = right_dot(chunk_of(d_ffn, c), flat(w_down[at // block : (at + wide) // block]))
             gate, up = gate_keep[c, :, cols], up_keep[c, :, cols]
             sig = jax.nn.sigmoid(gate)
             silu = gate * sig
@@ -1711,9 +1773,11 @@
             d_gate[:, of(c), cols] = d_g.reshape(seq, thin, wide)
             d_up[:, of(c), cols] = d_u.reshape(seq, thin, wide)
         left_g, left_u = chunk_of(d_gate, c), chunk_of(d_up, c)
-        for at in range(0, width, wide):
-            cols = slice(at, at + wide)
-            total = right_dot(left_g, w_gate[cols, :]) + right_dot(left_u, w_up[cols, :])
+        half = buckets // 2
+        for at in range(0, buckets, half):
+            cols = slice(at * width // buckets, (at + half) * width // buckets)
+            total = right_dot(left_g, flat(w_gate[at : at + half]))
+            total = total + right_dot(left_u, flat(w_up[at : at + half]))
             put_parts(c, cols, total)
 
     def pour_of(c, turn):
@@ -1730,13 +1794,11 @@
 
     def down_grad():
         chips, part = buckets // 2, hidden // buckets
-        at = spread(buckets)
         for i in range(chips):
             turned = all_rows(act, slice(2 * i * part, 2 * (i + 1) * part)).T
             total = bf_dot(turned, all_rows(d_ffn)).astype(BF16)
             for half in range(2):
-                p = at[2 * i + half]
-                grads[2][p // 2, p % 2] = total[half * part : (half + 1) * part]
+                grads[2][i, half] = total[half * part : (half + 1) * part]
         sums.begin(2)
 
     def weight_grads():
@@ -1763,8 +1825,10 @@
         sums.stage_b(1)
         yield
         sums.stage_c(0)
+        sums.stage_d(2)
         sums.stage_c(1)
-        sums.stage_d(2)
+        sums.stage_d(0)
+        sums.stage_d(1)
 
     extra = weight_grads()
     plan = [(turn, c) for turn in range(3) for c in range(chunks)]
@@ -1777,6 +1841,25 @@
             gathers[turn, c].sent(j)
         return turn, c
 
+    def weights_come():
+        count = len(MOVED)
+        for n in range(count + 3):
+            if n < count:
+                weights.arrived(MOVED[n])
+                if n + 1 < count:
+                    weights.depart(MOVED[n + 1])
+                weights.stage_a(MOVED[n])
+                yield
+            if 1 <= n <= count:
+                weights.stage_b(MOVED[n - 1])
+                yield
+            if 2 <= n <= count + 1:
+                weights.stage_c(MOVED[n - 2])
+            if 3 <= n:
+                weights.stage_d(MOVED[n - 3])
+            yield
+
+    coming = weights_come()
     attn_product(0)
     pours = {(0, 0): pour_of(0, 0)}
     ready = pours[0, 0].cuts
@@ -1798,6 +1881,7 @@
                 next(extra, None)
             for q in range((j - 1) * per, j * per):
                 pour.step(q)
+                next(coming, None)
             if final:
                 next(extra, None)
         pour.end(got.at[of(c)])
@@ -1808,6 +1892,8 @@
             done_turn, done_c = finish_gather()
             if (done_turn, done_c) == (1, chunks - 1):
                 down_grad()
+            for _ in coming:
+                pass
             if done_turn < 2:
                 products[done_turn + 1](done_c)
         open_gather.append((turn, c))
@@ -1829,6 +1915,7 @@
     for _ in extra:
         pass
     sums.end()
+    weights.end()
 
 
 def middle_all(buckets, seq, mixed, weights, tokens, cotangent, counts, gain_rows, mod_rows):
@@ -1838,15 +1925,16 @@
     chunks = CHUNKS
     w_out, w_gate, w_up, w_down = weights
     rows, width = tokens.shape
-    hidden = w_gate.shape[1]
+    hidden = w_down.shape[-2] * buckets if 2 in MOVED else w_down.shape[0] * w_down.shape[1]
+    part = width // (buckets * seq)
     tall, thin = (seq, rows, width), rows // chunks
     flat = (seq, rows, hidden)
     blocks = pltpu.VMEM((3 * chunks, seq - 1, thin, width), BF16)
-    kinds = ("col", "col", "row")
+    kinds = ("strip", "strip", "stay")
     shapes, sums_out, scratch, n_sems = sums_shapes(
-        buckets, seq, [w_gate.shape, w_up.shape, w_down.shape], kinds, near=True
+        buckets, seq, [(width, hidden), (width, hidden), (hidden, width)], kinds, near=True
     )
-    n_sems += 16 + 3 * chunks * (2 * CUTS + 2) * seq
+    n_sems += 64 + 3 * chunks * (2 * CUTS + 2) * seq
     results = pl.pallas_call(
         functools.partial(middle_kernel, buckets, seq, chunks, kinds),
         out_shape=[
@@ -1859,9 +1947,9 @@
         in_specs=[vmem] * 4 + [smem] + [vmem] * 2 + [any_spec] * 3,
         out_specs=[vmem] * 7,
         scratch_shapes=[
-            pltpu.VMEM(w_gate.shape, BF16),
-            pltpu.VMEM(w_up.shape, BF16),
-            pltpu.VMEM(w_down.shape, BF16),
+            pltpu.VMEM((buckets, seq, part, hidden), BF16),
+            pltpu.VMEM((buckets, seq, part, hidden), BF16),
+            pltpu.VMEM((buckets, hidden // buckets, width), BF16),
             pltpu.VMEM(tall, BF16),
             pltpu.VMEM(tall, BF16),
             *([pltpu.VMEM(flat, BF16)] * 3),
@@ -2287,6 +2375,8 @@
     slim = gains.shape[1]
     small = jnp.concatenate([gains, cross_gate[None]], axis=0).astype(F32)
     small = jnp.pad(small, ((0, 0), (0, 128 - slim)))
+    feed = [w_gate, w_up, w_down]
+    early = [w for w in range(3) if w not in MOVED]
     cap_all, weights, inner = forward_all(
         buckets,
         seq,
@@ -2297,10 +2387,12 @@
         cond_part,
         w_mod,
         [counts, cap_lens],
-        [w_query, w_key, w_value, w_cap_key, w_cap_value, w_out, w_gate, w_up, w_down],
-        ["col", "col", "col", "col", "col", "row", "col", "col", "row"],
+        [w_query, w_key, w_value, w_cap_key, w_cap_value, w_out, *(feed[w] for w in early)],
+        ["col", "col", "col", "col", "col", "row", *(("cut", "cut", "stay")[w] for w in early)],
     )
-    wq, wk, wv, wck, wcv, wo, wg, wu, wd = weights
+    wq, wk, wv, wck, wcv, wo = (x.reshape(-1, x.shape[-1]) for x in weights[:6])
+    for w, full in zip(early, weights[6:], strict=True):
+        feed[w] = full
     caps = cap_all.reshape(-1, captions.shape[1])
     small_rows, mod, hidden, query_proj, key_proj, cap_proj = inner[:6]
     query, key, value, cap_key, cap_value = inner[6:11]
@@ -2309,7 +2401,7 @@
         buckets,
         seq,
         mixed_low,
-        (wo, wg, wu, wd),
+        (wo, *feed),
         tokens,
         cotangent,
         counts,

time: 465 us -> 455 us (0.978)
  Pallas kernels: 451 us -> 441 us
    pallas_call x1, Pallas kernels: 163 us -> 143 us  [forward_all(): pl.pallas_call(functools.partial(forward_kernel, buckets, seq, tuple(kind...]
    pallas_call x1, Pallas kernels: 184 us -> 191 us  [middle_all(): pl.pallas_call(functools.partial(middle_kernel, buckets, seq, chunks, kin...]
where the time goes in v5:
time: 455 us; the launch traced here: 446 us
  Pallas kernels  441 us (97%)
    pallas_call x1, Pallas kernels, middle_all(): pl.pallas_call(functools.partial(middle_kernel, buckets, seq, chunks, kin...  191 us
    pallas_call x1, Pallas kernels, forward_all(): pl.pallas_call(functools.partial(forward_kernel, buckets, seq, tuple(kind...  143 us
    pallas_call x1, Pallas kernels, backward_all(): pl.pallas_call(functools.partial(backward_kernel, buckets, seq, tuple(kin...  101 us

profile of v5, /device:TPU:8, one launch (start us, length us, event | category | flops | bytes accessed | tf_op | source)
XLA Modules:
  0.0 446.4 jit_solution(6249900412286837520)
XLA Ops:
  0.7 0.7 convert_element_type.10
  1.3 1.3 fusion.3.refs_2_
  2.6 0.1 multiply_cosine_fusion
  2.8 0.2 copy.37
  3.0 0.1 add_divide_fusion
  3.1 0.2 copy.40
  3.3 0.2 copy.41
  3.5 0.6 convert_bitcast_fusion.refs_0_
  4.2 0.7 copy.42.refs_3_
  4.8 142.6 %shard_map.281 = (bf16[4,64,4096]{2,1,0:T(8,128)(2,1)}, bf16[8,4,48,384]{3,2,1,0:T(8,128)(2,1)}, bf16[8,4,48,384]{3,2,1,0:T(8,128)(2,1)}, bf16[8,4,48,384]{3,2,1...) custom-call(bf16[128,1536]{1,0:T(8,128)(2,1)} %refs_21_.1, ...), custom_call_target="tpu_custom_call" | custom-call | tf_op jit(solution)/shard_map/pallas_call | solution.py:1597
  147.4 191.2 %shard_map.282 = (bf16[128,1536]{1,0:T(8,128)(2,1)}, f32[128,1536]{1,0:T(8,128)}, bf16[4,128,1536]{2,1,0:T(8,128)(2,1)}, f32[8,1536]{1,0:T(8,128)}, f32[192,1024...) custom-call(bf16[4,128,384]{2,1,0:T(8,128)(2,1)} %bitcast.17, bf16[384,1536]{1,0:T(8,128)(2,1)} %bitcast.13, ...), custom_call_target="tpu_custom_call" | custom-call | tf_op jit(solution)/shard_map/pallas_call | solution.py:1938
  338.6 100.6 %shard_map.283 = (f32[128,1536]{1,0:T(8,128)}, f32[8,8,384]{2,1,0:T(8,128)}, f32[8,128]{1,0:T(8,128)}, f32[4,48,384]{2,1,0:T(8,128)}, f32[512,384]{1,0:T(8,128)}...) custom-call(bf16[512,1536]{1,0:T(8,128)(2,1)} %bitcast.16, ...), custom_call_target="tpu_custom_call" | custom-call | tf_op jit(solution)/shard_map/pallas_call | solution.py:2251
  439.2 6.7 %shard_map.284 = (f32[128,1536]{1,0:T(8,128)}, f32[7,48]{1,0:T(8,128)}, f32[1,48]{1,0:T(1,128)}, bf16[128,1536]{1,0:T(8,128)(2,1)}, f32[128,1536]{1,0:T(8,128)},...) custom-call(f32[128,8]{1,0:T(8,128)} %convert_bitcast_fusion.refs_0_, ...), custom_call_target="tpu_custom_call" | custom-call | tf_op jit(solution)/shard_map/pallas_call | solution.py:2329
  (4 shorter events, 0.0 us)
